TPU v7x, 32 devices: a whole 2x2x4 slice. The times are simulated.
32 devices in a mesh: rep: 8 (over y, x, core), shard: 4 (over z).
Axes of the slice: x: 2, y: 2, z: 4, core: 2. Of those that a mesh axis runs over, the one named last changes fastest.
Arguments:
- hidden_in: bfloat16 [32768, 768], P(('rep', 'shard')), may hold values from -6 to 6
- segment: int32 [32, 1024], P(('rep', 'shard')), may hold values from 0 to 32, as said below
- cotangent: bfloat16 [32768, 768], P(('rep', 'shard')), may hold values from -6 to 6
- ln1_gain: bfloat16 [768], P('shard'), may hold values from 0.5 to 1.5
- ln1_bias: bfloat16 [768], P('shard'), may hold values from -1.75 to 1.75
- qkv_weight: bfloat16 [768, 2304], P('shard'), may hold values from -0.21875 to 0.21875
- query_bias: bfloat16 [768], P('shard'), may hold values from -3 to 3
- value_bias: bfloat16 [768], P('shard'), may hold values from -3 to 3
- out_weight: bfloat16 [768, 768], P('shard'), may hold values from -2 to 2
- out_bias: bfloat16 [768], P('shard'), may hold values from -3 to 3
- ln2_gain: bfloat16 [768], P('shard'), may hold values from 0.5 to 1.5
- ln2_bias: bfloat16 [768], P('shard'), may hold values from -1.75 to 1.75
- fc_weight: bfloat16 [768, 3072], P('shard'), may hold values from -0.21875 to 0.21875
- fc_bias: bfloat16 [3072], P('shard'), may hold values from -3 to 3
- proj_weight: bfloat16 [3072, 768], P('shard'), may hold values from -0.109375 to 0.109375
- proj_bias: bfloat16 [768], P('shard'), may hold values from -3 to 3
Outputs:
- block_out: bfloat16 [32768, 768], P(('rep', 'shard'))
- input_grad: bfloat16 [32768, 768], P(('rep', 'shard'))
- grad_ln1_gain: float32 [768], P('shard')
- grad_ln1_bias: float32 [768], P('shard')
- grad_qkv_weight: float32 [768, 2304], P('shard')
- grad_query_bias: float32 [768], P('shard')
- grad_value_bias: float32 [768], P('shard')
- grad_out_weight: float32 [768, 768], P('shard')
- grad_out_bias: float32 [768], P('shard')
- grad_ln2_gain: float32 [768], P('shard')
- grad_ln2_bias: float32 [768], P('shard')
- grad_fc_weight: float32 [768, 3072], P('shard')
- grad_fc_bias: float32 [3072], P('shard')
- grad_proj_weight: float32 [3072, 768], P('shard')
- grad_proj_bias: float32 [768], P('shard')
Inputs may be any that keep to these rules, and one draw needn't show every extreme that they name: Each row holds one device's tokens; segment numbers start at 0 in every row and never fall along it; equal numbers in a row mark one sequence. One row in every draw holds a single sequence of 1024 tokens, and some row in every draw reaches the largest number.
All inputs are finite; a program needn't handle non-finite values.
Results may differ from a plain program's by a relative error of at most 0.019.
Values may be sent and summed in bfloat16 or wider, within the bound.
No kernel may reach another device: no remote copies, remote signals or barrier semaphores. Data moves between devices by JAX's collectives and lax.ppermute only.
A program may use at most 320 MiB of HBM per device.

v0:
```python
import jax
import jax.numpy as jnp
from jax import lax
from jax.sharding import PartitionSpec as P

HEADS = 12
HEAD_DIM = 64


def layer_norm(values, gain, shift):
    center = values - jnp.mean(values, axis=-1, keepdims=True)
    spread = jnp.mean(center * center, axis=-1, keepdims=True)
    return center * lax.rsqrt(spread + 1e-05) * gain + shift


def norm_scale(values, gain):
    center = values - jnp.mean(values, axis=-1, keepdims=True)
    spread = jnp.mean(center * center, axis=-1, keepdims=True)
    return center * lax.rsqrt(spread + 1e-05) * gain


def gelu_tanh(values):
    return jax.nn.gelu(values, approximate=True)


def masked_scores(query_block, key_heads, seg_row, position, offset):
    rows_here = query_block.shape[0]
    scores = jnp.einsum(
        "qhd,khd->hqk", query_block, key_heads, preferred_element_type=jnp.float32
    ) * HEAD_DIM ** (-0.5)
    seg_block = seg_row[offset : offset + rows_here]
    allowed = (seg_block[:, None] == seg_row[None, :]) & (
        position[offset : offset + rows_here, None] >= position[None, :]
    )
    return jnp.where(allowed[None], scores, -1e30)


def attend_forward(queries, key_rows, value_rows, seg_row):
    length = queries.shape[0]
    query_heads = queries.reshape(length, HEADS, HEAD_DIM)
    key_heads = key_rows.reshape(length, HEADS, HEAD_DIM)
    value_heads = value_rows.reshape(length, HEADS, HEAD_DIM)
    block_rows = min(512, length)
    position = jnp.arange(length)
    outputs = []
    totals = []
    for offset in range(0, length, block_rows):
        scores = masked_scores(
            query_heads[offset : offset + block_rows], key_heads, seg_row, position, offset
        )
        highest = jnp.max(scores, axis=-1, keepdims=True)
        expo = jnp.exp(scores - highest)
        summed = jnp.sum(expo, axis=-1, keepdims=True)
        attn_low = (expo / summed).astype(jnp.bfloat16)
        outputs.append(
            jnp.einsum("hqk,khd->qhd", attn_low, value_heads, preferred_element_type=jnp.float32)
        )
        totals.append(highest + jnp.log(summed))
    return (
        jnp.concatenate(outputs, axis=0).reshape(length, HEADS * HEAD_DIM),
        jnp.concatenate(totals, axis=1),
    )


def attend_backward(queries, key_rows, value_rows, seg_row, totals, grad_attended):
    length = queries.shape[0]
    scale = HEAD_DIM ** (-0.5)
    query_heads = queries.reshape(length, HEADS, HEAD_DIM)
    key_heads = key_rows.reshape(length, HEADS, HEAD_DIM)
    value_heads = value_rows.reshape(length, HEADS, HEAD_DIM)
    grad_heads = grad_attended.reshape(length, HEADS, HEAD_DIM)
    block_rows = min(512, length)
    position = jnp.arange(length)
    grad_keys = jnp.zeros((length, HEADS, HEAD_DIM), jnp.float32)
    grad_values = jnp.zeros((length, HEADS, HEAD_DIM), jnp.float32)
    grad_query_list = []
    for offset in range(0, length, block_rows):
        query_block = query_heads[offset : offset + block_rows]
        grad_block = grad_heads[offset : offset + block_rows]
        scores = masked_scores(query_block, key_heads, seg_row, position, offset)
        attn_probs = jnp.exp(scores - totals[:, offset : offset + block_rows])
        attn_low = attn_probs.astype(jnp.bfloat16)
        grad_values = grad_values + jnp.einsum(
            "hqk,qhd->khd", attn_low, grad_block, preferred_element_type=jnp.float32
        )
        grad_probs = jnp.einsum(
            "qhd,khd->hqk", grad_block, value_heads, preferred_element_type=jnp.float32
        )
        inner = jnp.sum(grad_probs * attn_probs, axis=-1, keepdims=True)
        grad_scores = (attn_probs * (grad_probs - inner)).astype(jnp.bfloat16)
        grad_query_list.append(
            jnp.einsum("hqk,khd->qhd", grad_scores, key_heads, preferred_element_type=jnp.float32)
            * scale
        )
        grad_keys = (
            grad_keys
            + jnp.einsum(
                "hqk,qhd->khd", grad_scores, query_block, preferred_element_type=jnp.float32
            )
            * scale
        )
    width = HEADS * HEAD_DIM
    grad_queries = jnp.concatenate(grad_query_list, axis=0).reshape(length, width)
    return (grad_queries, grad_keys.reshape(length, width), grad_values.reshape(length, width))


def column_sum(values):
    return jnp.sum(values.astype(jnp.float32), axis=0)


def shards(
    hidden_in,
    segment,
    cotangent,
    ln1_gain,
    ln1_bias,
    qkv_weight,
    query_bias,
    value_bias,
    out_weight,
    out_bias,
    ln2_gain,
    ln2_bias,
    fc_weight,
    fc_bias,
    proj_weight,
    proj_bias,
):
    gathered = (
        lax.all_gather(ln1_gain, "shard", axis=0, tiled=True),
        lax.all_gather(ln1_bias, "shard", axis=0, tiled=True),
        lax.all_gather(qkv_weight, "shard", axis=0, tiled=True),
        lax.all_gather(query_bias, "shard", axis=0, tiled=True),
        lax.all_gather(value_bias, "shard", axis=0, tiled=True),
        lax.all_gather(out_weight, "shard", axis=0, tiled=True),
        lax.all_gather(out_bias, "shard", axis=0, tiled=True),
        lax.all_gather(ln2_gain, "shard", axis=0, tiled=True),
        lax.all_gather(ln2_bias, "shard", axis=0, tiled=True),
        lax.all_gather(fc_weight, "shard", axis=0, tiled=True),
        lax.all_gather(fc_bias, "shard", axis=0, tiled=True),
        lax.all_gather(proj_weight, "shard", axis=0, tiled=True),
        lax.all_gather(proj_bias, "shard", axis=0, tiled=True),
    )
    (
        gain_one,
        shift_one,
        w_qkv,
        bias_query,
        bias_value,
        w_out,
        bias_out,
        gain_two,
        shift_two,
        w_fc,
        bias_fc,
        w_proj,
        bias_proj,
    ) = gathered
    width = hidden_in.shape[1]
    seg_row = segment[0]
    inputs = hidden_in.astype(jnp.float32)
    gain_one_f = gain_one.astype(jnp.float32)
    gain_two_f = gain_two.astype(jnp.float32)
    norm_one = layer_norm(inputs, gain_one_f, shift_one.astype(jnp.float32)).astype(jnp.bfloat16)
    joined = jnp.dot(norm_one, w_qkv, preferred_element_type=jnp.float32)
    queries = (joined[:, :width] + bias_query.astype(jnp.float32)).astype(jnp.bfloat16)
    key_rows = joined[:, width : 2 * width].astype(jnp.bfloat16)
    value_rows = (joined[:, 2 * width :] + bias_value.astype(jnp.float32)).astype(jnp.bfloat16)
    attended_f, totals = attend_forward(queries, key_rows, value_rows, seg_row)
    attended = attended_f.astype(jnp.bfloat16)
    resid = (
        inputs
        + jnp.dot(attended, w_out, preferred_element_type=jnp.float32)
        + bias_out.astype(jnp.float32)
    )
    norm_two = layer_norm(resid, gain_two_f, shift_two.astype(jnp.float32)).astype(jnp.bfloat16)
    pre_act = jnp.dot(norm_two, w_fc, preferred_element_type=jnp.float32) + bias_fc.astype(
        jnp.float32
    )
    gelu_low = gelu_tanh(pre_act).astype(jnp.bfloat16)
    block_out = (
        resid
        + jnp.dot(gelu_low, w_proj, preferred_element_type=jnp.float32)
        + bias_proj.astype(jnp.float32)
    ).astype(jnp.bfloat16)
    back_gain_one, back_qkv, back_out, back_gain_two, back_fc, back_proj = (
        lax.all_gather(ln1_gain, "shard", axis=0, tiled=True),
        lax.all_gather(qkv_weight, "shard", axis=0, tiled=True),
        lax.all_gather(out_weight, "shard", axis=0, tiled=True),
        lax.all_gather(ln2_gain, "shard", axis=0, tiled=True),
        lax.all_gather(fc_weight, "shard", axis=0, tiled=True),
        lax.all_gather(proj_weight, "shard", axis=0, tiled=True),
    )
    back_gain_one = back_gain_one.astype(jnp.float32)
    back_gain_two = back_gain_two.astype(jnp.float32)
    grad_out = cotangent.astype(jnp.float32)
    d_proj_bias = column_sum(cotangent)
    d_proj_weight = jnp.einsum("tf,td->fd", gelu_low, cotangent, preferred_element_type=jnp.float32)
    grad_gelu = jnp.einsum("td,fd->tf", cotangent, back_proj, preferred_element_type=jnp.float32)
    _, gelu_pull = jax.vjp(gelu_tanh, pre_act)
    grad_pre = gelu_pull(grad_gelu)[0].astype(jnp.bfloat16)
    d_fc_bias = column_sum(grad_pre)
    d_fc_weight = jnp.einsum("td,tf->df", norm_two, grad_pre, preferred_element_type=jnp.float32)
    grad_norm_two = jnp.einsum("tf,df->td", grad_pre, back_fc, preferred_element_type=jnp.float32)
    _, norm_pull_two = jax.vjp(norm_scale, resid, back_gain_two)
    grad_resid_norm, d_ln2_gain = norm_pull_two(grad_norm_two)
    d_ln2_bias = jnp.sum(grad_norm_two, axis=0)
    grad_resid = grad_out + grad_resid_norm
    grad_branch = grad_resid.astype(jnp.bfloat16)
    d_out_bias = column_sum(grad_branch)
    d_out_weight = jnp.einsum(
        "td,te->de", attended, grad_branch, preferred_element_type=jnp.float32
    )
    grad_attended = jnp.einsum(
        "te,de->td", grad_branch, back_out, preferred_element_type=jnp.float32
    ).astype(jnp.bfloat16)
    grad_queries, grad_keys, grad_values = attend_backward(
        queries, key_rows, value_rows, seg_row, totals, grad_attended
    )
    grad_queries = grad_queries.astype(jnp.bfloat16)
    grad_keys = grad_keys.astype(jnp.bfloat16)
    grad_values = grad_values.astype(jnp.bfloat16)
    d_query_bias = column_sum(grad_queries)
    d_value_bias = column_sum(grad_values)
    grad_qkv = jnp.concatenate([grad_queries, grad_keys, grad_values], axis=1)
    d_qkv_weight = jnp.einsum("td,te->de", norm_one, grad_qkv, preferred_element_type=jnp.float32)
    grad_norm_one = jnp.einsum("te,de->td", grad_qkv, back_qkv, preferred_element_type=jnp.float32)
    _, norm_pull_one = jax.vjp(norm_scale, inputs, back_gain_one)
    grad_input_norm, d_ln1_gain = norm_pull_one(grad_norm_one)
    d_ln1_bias = jnp.sum(grad_norm_one, axis=0)
    input_grad = (grad_resid + grad_input_norm).astype(jnp.bfloat16)
    grads = (
        d_ln1_gain,
        d_ln1_bias,
        d_qkv_weight,
        d_query_bias,
        d_value_bias,
        d_out_weight,
        d_out_bias,
        d_ln2_gain,
        d_ln2_bias,
        d_fc_weight,
        d_fc_bias,
        d_proj_weight,
        d_proj_bias,
    )
    shares = (
        lax.psum_scatter(
            grads[0].astype(jnp.bfloat16), "shard", scatter_dimension=0, tiled=True
        ).astype(jnp.float32),
        lax.psum_scatter(
            grads[1].astype(jnp.bfloat16), "shard", scatter_dimension=0, tiled=True
        ).astype(jnp.float32),
        lax.psum_scatter(
            grads[2].astype(jnp.bfloat16), "shard", scatter_dimension=0, tiled=True
        ).astype(jnp.float32),
        lax.psum_scatter(
            grads[3].astype(jnp.bfloat16), "shard", scatter_dimension=0, tiled=True
        ).astype(jnp.float32),
        lax.psum_scatter(
            grads[4].astype(jnp.bfloat16), "shard", scatter_dimension=0, tiled=True
        ).astype(jnp.float32),
        lax.psum_scatter(
            grads[5].astype(jnp.bfloat16), "shard", scatter_dimension=0, tiled=True
        ).astype(jnp.float32),
        lax.psum_scatter(
            grads[6].astype(jnp.bfloat16), "shard", scatter_dimension=0, tiled=True
        ).astype(jnp.float32),
        lax.psum_scatter(
            grads[7].astype(jnp.bfloat16), "shard", scatter_dimension=0, tiled=True
        ).astype(jnp.float32),
        lax.psum_scatter(
            grads[8].astype(jnp.bfloat16), "shard", scatter_dimension=0, tiled=True
        ).astype(jnp.float32),
        lax.psum_scatter(
            grads[9].astype(jnp.bfloat16), "shard", scatter_dimension=0, tiled=True
        ).astype(jnp.float32),
        lax.psum_scatter(
            grads[10].astype(jnp.bfloat16), "shard", scatter_dimension=0, tiled=True
        ).astype(jnp.float32),
        lax.psum_scatter(
            grads[11].astype(jnp.bfloat16), "shard", scatter_dimension=0, tiled=True
        ).astype(jnp.float32),
        lax.psum_scatter(
            grads[12].astype(jnp.bfloat16), "shard", scatter_dimension=0, tiled=True
        ).astype(jnp.float32),
    )
    totals_out = (
        lax.psum(shares[0].astype(jnp.bfloat16), "rep").astype(jnp.float32),
        lax.psum(shares[1].astype(jnp.bfloat16), "rep").astype(jnp.float32),
        lax.psum(shares[2].astype(jnp.bfloat16), "rep").astype(jnp.float32),
        lax.psum(shares[3].astype(jnp.bfloat16), "rep").astype(jnp.float32),
        lax.psum(shares[4].astype(jnp.bfloat16), "rep").astype(jnp.float32),
        lax.psum(shares[5].astype(jnp.bfloat16), "rep").astype(jnp.float32),
        lax.psum(shares[6].astype(jnp.bfloat16), "rep").astype(jnp.float32),
        lax.psum(shares[7].astype(jnp.bfloat16), "rep").astype(jnp.float32),
        lax.psum(shares[8].astype(jnp.bfloat16), "rep").astype(jnp.float32),
        lax.psum(shares[9].astype(jnp.bfloat16), "rep").astype(jnp.float32),
        lax.psum(shares[10].astype(jnp.bfloat16), "rep").astype(jnp.float32),
        lax.psum(shares[11].astype(jnp.bfloat16), "rep").astype(jnp.float32),
        lax.psum(shares[12].astype(jnp.bfloat16), "rep").astype(jnp.float32),
    )
    return (
        block_out,
        input_grad,
        totals_out[0],
        totals_out[1],
        totals_out[2],
        totals_out[3],
        totals_out[4],
        totals_out[5],
        totals_out[6],
        totals_out[7],
        totals_out[8],
        totals_out[9],
        totals_out[10],
        totals_out[11],
        totals_out[12],
    )


def solution(mesh):
    in_specs = (
        P(("rep", "shard"), None),
        P(("rep", "shard"), None),
        P(("rep", "shard"), None),
        P("shard"),
        P("shard"),
        P("shard", None),
        P("shard"),
        P("shard"),
        P("shard", None),
        P("shard"),
        P("shard"),
        P("shard"),
        P("shard", None),
        P("shard"),
        P("shard", None),
        P("shard"),
    )
    out_specs = (
        P(("rep", "shard"), None),
        P(("rep", "shard"), None),
        P("shard"),
        P("shard"),
        P("shard", None),
        P("shard"),
        P("shard"),
        P("shard", None),
        P("shard"),
        P("shard"),
        P("shard"),
        P("shard", None),
        P("shard"),
        P("shard", None),
        P("shard"),
    )
    return jax.shard_map(shards, mesh=mesh, in_specs=in_specs, out_specs=out_specs, check_vma=False)
```

profile of v0, /device:TPU:0, one launch (start us, length us, event | category | flops | bytes accessed | tf_op | source)
XLA Modules:
  0.0 815.9 jit_solution(18127650699581201732)
XLA Ops:
  13.1 21.0 %all-reduce.20 = (bf16[768]{0:T(1024)(128)(2,1)S(1)}, bf16[768]{0:T(1024)(128)(2,1)S(1)}, bf16[768]{0:T(1024)(128)(2,1)S(1)}, bf16[768]{0:T(1024)(128)(2,1)S(1)}...) all-reduce(bf16[768]{0:T(1024)(128)(2,1)S(1)} %dynamic-update-slice, ...), channel_id=1, replica_groups=mesh['rep'=8,'shard'=4] {'shard'}, use_global_device_ids=true, to_apply=%add.1 | all-reduce | flops 5376 | bytes 21504
  35.3 13.2 %all-gather = bf16[4,1,768]{2,1,0:T(2,128)(2,1)S(1)} all-gather(bf16[1,1,768]{2,1,0:T(2,128)(2,1)S(1)} %reshape.268), channel_id=1, replica_groups=mesh['rep'=8,'shard'=4] {'shard'}, dimensions={0}, use_global_device_ids=true | all-gather | bytes 7680 | tf_op jit(solution)/shard_map/all_gather | solution.py:140
  56.3 26.5 %all-gather.6.cloned.1.call-done = bf16[768,2304]{1,0:T(8,128)(2,1)} async-done(((bf16[192,2304]{1,0:T(8,128)(2,1)}), bf16[768,2304]{1,0:T(8,128)(2,1)}) %all-gather.6.cloned.1.call-update) | async-done | bytes 3538960 | tf_op jit(solution)/shard_map/all_gather | solution.py:132
  82.8 6.1 fusion.59
  89.0 3.6 copy-done.21
  95.6 5.1 fusion.33
  106.6 2.6 copy.66
  109.2 12.5 %fusion.20 = (f32[12,512]{1,0:T(8,128)S(1)}, f32[12,512,1024]{2,1,0:T(8,128)}) fusion(pred[512,1024]{1,0:T(8,128)(4,1)} %get-tuple-element.107, bf16[512,12,64]{0,2,1:T(8,128)(2,1)} %bitcast.72, bf16[1024,12,64]{0,2,1:T(8,128)(2,1)S(1)} %bitcast.64), kind=kOutput, calls=%fused_computation.33 | convolution fusion | flops 824174592 | bytes 28073984 | tf_op jit(solution)/shard_map/qhd,khd->hqk/dot_general | solution.py:28
  121.7 12.8 %fusion.1 = f32[12,512]{1,0:T(8,128)S(1)} fusion(f32[12,512]{1,0:T(8,128)S(1)} %get-tuple-element.112, f32[12,512,1024]{2,1,0:T(8,128)} %get-tuple-element.113, pred[512,1024]{1,0:T(8,128)(4,1)} %get-tuple-element.107), kind=kLoop, calls=%fused_computation.13 | loop fusion | flops 25159680 | bytes 25739264 | tf_op jit(solution)/shard_map/reduce_sum | solution.py:53
  134.5 3.8 copy-done.1
  138.3 9.6 %fusion.44 = bf16[512,12,64]{0,2,1:T(8,128)(2,1)} fusion(bf16[1024,12,64]{0,2,1:T(8,128)(2,1)S(1)} %bitcast.68, f32[12,512]{1,0:T(8,128)S(1)} %fusion.1, f32[12,512]{1,0:T(8,128)S(1)} %get-tuple-element.112, f32[12,512,1024]{2,1,0:T(8,128)S(1)} %copy-done.1, pred[512,1024]{1,0:T(8,128)(4,1)} %get-tuple-element.107), kind=kOutput, calls=%fused_computation.84 | convolution fusion | flops 837156864 | bytes 28098560 | tf_op jit(solution)/shard_map/hqk,khd->qhd/dot_general | solution.py:56
  147.9 12.1 %fusion.19 = (f32[12,512]{1,0:T(8,128)S(1)}, f32[12,512,1024]{2,1,0:T(8,128)}) fusion(pred[512,1024]{1,0:T(8,128)(4,1)} %get-tuple-element.106, bf16[512,12,64]{0,2,1:T(8,128)(2,1)} %bitcast.74, bf16[1024,12,64]{0,2,1:T(8,128)(2,1)S(1)} %bitcast.65), kind=kOutput, calls=%fused_computation.32 | convolution fusion | flops 824174592 | bytes 28073984 | tf_op jit(solution)/shard_map/qhd,khd->hqk/dot_general | solution.py:28
  160.0 13.6 %fusion = f32[12,512]{1,0:T(8,128)S(1)} fusion(f32[12,512]{1,0:T(8,128)S(1)} %get-tuple-element.114, f32[12,512,1024]{2,1,0:T(8,128)} %get-tuple-element.115, pred[512,1024]{1,0:T(8,128)(4,1)} %get-tuple-element.106), kind=kLoop, calls=%fused_computation.12 | loop fusion | flops 25159680 | bytes 25739264 | tf_op jit(solution)/shard_map/reduce_sum | solution.py:53
  176.1 8.5 %fusion.43 = bf16[512,12,64]{0,2,1:T(8,128)(2,1)} fusion(bf16[1024,12,64]{0,2,1:T(8,128)(2,1)S(1)} %bitcast.69, f32[12,512]{1,0:T(8,128)S(1)} %fusion, f32[12,512]{1,0:T(8,128)S(1)} %get-tuple-element.114, f32[12,512,1024]{2,1,0:T(8,128)S(1)} %copy-done, pred[512,1024]{1,0:T(8,128)(4,1)S(1)} %copy-done.16), kind=kOutput, calls=%fused_computation.83 | convolution fusion | flops 837156864 | bytes 28098560 | tf_op jit(solution)/shard_map/hqk,khd->qhd/dot_general | solution.py:56
  186.3 3.4 fusion.70
  191.9 11.7 %all-gather.10.cloned.1.call-done = bf16[768,3072]{1,0:T(8,128)(2,1)} async-done(((bf16[192,3072]{1,0:T(8,128)(2,1)}), bf16[768,3072]{1,0:T(8,128)(2,1)}) %all-gather.10.cloned.1.call-update) | async-done | bytes 4718608 | tf_op jit(solution)/shard_map/all_gather | solution.py:139
  203.6 11.2 %fusion.61 = f32[1024,3072]{1,0:T(8,128)} fusion(bf16[768,3072]{1,0:T(8,128)(2,1)} %all-gather.10.cloned.1.call-done, f32[1024,768]{0,1:T(8,128)} %copy-done.5, f32[768]{0:T(1024)S(1)} %copy-done.37, f32[768]{0:T(1024)S(1)} %copy-done.36, f32[1024]{0:T(1024)S(1)} %fusion.47, f32[1024]{0:T(1024)S(1)} %broadcast_multiply_fusion), kind=kOutput, calls=%fused_computation.109 | convolution fusion | flops 4835770368 | bytes 20461568 | tf_op jit(solution)/shard_map/dot_general | solution.py:177
  214.8 78.1 %all-gather.12.cloned.1.call-done = bf16[3072,768]{1,0:T(8,128)(2,1)} async-done(((bf16[768,768]{1,0:T(8,128)(2,1)}), bf16[3072,768]{1,0:T(8,128)(2,1)}) %all-gather.12.cloned.1.call-update) | async-done | bytes 4718608 | tf_op jit(solution)/shard_map/all_gather | solution.py:141
  292.9 15.5 %fusion.74 = (bf16[3072]{0:T(1024)(128)(2,1)}, bf16[1024,3072]{1,0:T(8,128)(2,1)S(1)}) fusion(f32[1024,3072]{1,0:T(8,128)} %fusion.61, f32[3072]{0:T(1024)S(1)} %bitcast.87, bf16[1024,768]{1,0:T(8,128)(2,1)S(1)} %copy-done.23, bf16[3072,768]{1,0:T(8,128)(2,1)} %all-gather.12.cloned.1.call-done), kind=kOutput, calls=%fused_computation.121 | convolution fusion | flops 4901041152 | bytes 25184256 | tf_op jit(solution)/shard_map/td,fd->tf/dot_general | solution.py:199
  308.4 7.3 fusion.73
  315.7 4.0 copy.72
  319.7 3.5 multiply_reduce_fusion.2
  331.7 13.2 %fusion.11 = f32[12,64,1024]{2,1,0:T(8,128)} fusion(bf16[512,12,64]{0,2,1:T(8,128)(2,1)S(1)} %bitcast.80, f32[12,512]{1,0:T(8,128)S(1)} %log_add_fusion, f32[12,512,1024]{2,1,0:T(8,128)} %get-tuple-element.113, pred[512,1024]{1,0:T(8,128)(4,1)S(1)} %copy-done.19), kind=kOutput, calls=%fused_computation.25 | convolution fusion | flops 830472192 | bytes 29646848 | tf_op jit(solution)/shard_map/hqk,qhd->khd/dot_general | solution.py:83
  344.9 17.8 %multiply_reduce_fusion = (f32[12,512]{1,0:T(8,128)S(1)}, f32[12,512,1024]{2,1,0:T(8,128)}) fusion(f32[12,512]{1,0:T(8,128)S(1)} %log_add_fusion, f32[12,512,1024]{2,1,0:T(8,128)} %get-tuple-element.113, pred[512,1024]{1,0:T(8,128)(4,1)S(1)} %copy-done.19, bf16[512,12,64]{0,2,1:T(8,128)(2,1)} %bitcast.81, bf16[1024,12,64]{0,2,1:T(8,128)(2,1)S(1)} %bitcast.70), kind=kOutput, calls=%fused_computation.1 | convolution fusion | flops 836757504 | bytes 53264384 | tf_op jit(solution)/shard_map/qhd,khd->hqk/dot_general | solution.py:86
  362.6 21.6 %multiply_reduce_fusion.1 = (f32[12,512]{1,0:T(8,128)S(1)}, f32[12,512,1024]{2,1,0:T(8,128)}) fusion(f32[12,512]{1,0:T(8,128)S(1)} %log_add_fusion.1, f32[12,512,1024]{2,1,0:T(8,128)} %get-tuple-element.115, pred[512,1024]{1,0:T(8,128)(4,1)S(1)} %copy-done.17, bf16[512,12,64]{0,2,1:T(8,128)(2,1)S(1)} %bitcast.78, bf16[1024,12,64]{0,2,1:T(8,128)(2,1)S(1)} %bitcast.71), kind=kOutput, calls=%fused_computation.4 | convolution fusion | flops 836757504 | bytes 53264384 | tf_op jit(solution)/shard_map/qhd,khd->hqk/dot_general | solution.py:86
  384.2 41.8 %multiply_convert_fusion = (bf16[12,512,1024]{2,1,0:T(8,128)(2,1)}, bf16[12,512,1024]{2,1,0:T(8,128)(2,1)}) fusion(f32[12,512,1024]{2,1,0:T(8,128)} %get-tuple-element.121, f32[12,512]{1,0:T(8,128)S(1)} %get-tuple-element.120, f32[12,512]{1,0:T(8,128)S(1)} %log_add_fusion, f32[12,512,1024]{2,1,0:T(8,128)} %get-tuple-element.113, ...), kind=kLoop, calls=%fused_computation | loop fusion | flops 75497472 | bytes 126976000 | tf_op jit(solution)/shard_map/convert_element_type | solution.py:90
  426.0 10.0 %multiply_bitcast_fusion.1 = bf16[512,12,64]{0,2,1:T(8,128)(2,1)} fusion(bf16[1024,12,64]{0,2,1:T(8,128)(2,1)} %bitcast.66, bf16[12,512,1024]{2,1,0:T(8,128)(2,1)} %get-tuple-element.131), kind=kOutput, calls=%fused_computation.79 | convolution fusion | flops 806092800 | bytes 14942208 | tf_op jit(solution)/shard_map/hqk,khd->qhd/dot_general | solution.py:92
  436.0 5.1 fusion.75
  441.6 9.3 %multiply_bitcast_fusion = bf16[512,12,64]{0,2,1:T(8,128)(2,1)S(1)} fusion(bf16[1024,12,64]{0,2,1:T(8,128)(2,1)} %bitcast.67, bf16[12,512,1024]{2,1,0:T(8,128)(2,1)} %get-tuple-element.130), kind=kOutput, calls=%fused_computation.78 | convolution fusion | flops 806092800 | bytes 14942208 | tf_op jit(solution)/shard_map/hqk,khd->qhd/dot_general | solution.py:92
  450.9 7.0 multiply_convert_fusion.3
  459.9 13.4 %fusion.72 = (bf16[12,64]{1,0:T(8,128)(2,1)S(1)}, bf16[12,64,1024]{2,1,0:T(8,128)(2,1)S(1)}) fusion(f32[12,64,1024]{2,1,0:T(8,128)} %fusion.11, bf16[512,12,64]{0,2,1:T(8,128)(2,1)S(1)} %bitcast.79, f32[12,512]{1,0:T(8,128)S(1)} %log_add_fusion.1, f32[12,512,1024]{2,1,0:T(8,128)} %get-tuple-element.115, pred[512,1024]{1,0:T(8,128)(4,1)S(1)} %copy-done.18), kind=kOutput, calls=%fused_computation.119 | convolution fusion | flops 832830720 | bytes 31221248 | tf_op jit(solution)/shard_map/hqk,qhd->khd/dot_general | solution.py:83
  474.5 5.9 convolution_convert_fusion.2
  481.8 12.1 %convolution_convert_fusion = bf16[3072,768]{1,0:T(8,128)(2,1)} fusion(bf16[1024,768]{1,0:T(8,128)(2,1)S(1)} %copy-done.24, f32[1024,3072]{1,0:T(8,128)} %fusion.61, f32[3072]{0:T(1024)S(1)} %bitcast.88), kind=kOutput, calls=%fused_computation.34 | convolution fusion | flops 4865654784 | bytes 18886656 | tf_op jit(solution)/shard_map/tf,td->fd/dot_general | solution.py:198
  494.6 9.8 %convolution_convert_fusion.1 = bf16[768,3072]{1,0:T(8,128)(2,1)} fusion(bf16[1024,3072]{1,0:T(8,128)(2,1)} %copy-done.71, f32[1024,768]{0,1:T(8,128)} %copy-done.5, f32[768]{0:T(1024)S(1)} %copy-done.38, f32[768]{0:T(1024)S(1)} %copy-done.36, f32[1024]{0:T(1024)S(1)} %fusion.47, f32[1024]{0:T(1024)S(1)} %broadcast_multiply_fusion), kind=kOutput, calls=%fused_computation.35 | convolution fusion | flops 4838129664 | bytes 14170112 | tf_op jit(solution)/shard_map/td,tf->df/dot_general | solution.py:203
  506.5 9.0 %fusion.71 = (bf16[768]{0:T(1024)(128)(2,1)S(1)}, f32[1024,768]{1,0:T(8,128)}) fusion(bf16[768,2304]{1,0:T(8,128)(2,1)} %all-gather.6.cloned.1.call-done, bf16[1024,768]{0,1:T(8,128)(2,1)} %bitcast.93, bf16[1024,768]{0,1:T(8,128)(2,1)} %bitcast.77, bf16[1024,768]{0,1:T(8,128)(2,1)} %bitcast.83), kind=kOutput, calls=%fused_computation.118 | convolution fusion | flops 3638820096 | bytes 11404800 | tf_op jit(solution)/shard_map/te,de->td/dot_general | solution.py:227
  515.4 3.6 copy.73
  519.0 2.6 fusion.31
  523.2 18.0 %all-reduce.19 = (bf16[768]{0:T(1024)(128)(2,1)S(1)}, bf16[768]{0:T(1024)(128)(2,1)S(1)}, bf16[768]{0:T(1024)(128)(2,1)S(1)}, bf16[768]{0:T(1024)(128)(2,1)S(1)}...) all-reduce(bf16[768]{0:T(1024)(128)(2,1)S(1)} %dynamic-update-slice, ...), channel_id=1, replica_groups=mesh['rep'=8,'shard'=4] {'shard'}, use_global_device_ids=true, to_apply=%add.7 | all-reduce | flops 9984 | bytes 39936
  541.2 5.0 reduce-scatter.5.cloned.1.call-done
  546.2 87.8 %reduce-scatter.11.cloned.1.call-done = bf16[768,768]{1,0:T(8,128)(2,1)} async-done(((bf16[3072,768]{1,0:T(8,128)(2,1)}), bf16[768,768]{1,0:T(8,128)(2,1)}) %reduce-scatter.11.cloned.1.call-update) | async-done | bytes 1179664 | tf_op jit(solution)/shard_map/reduce_scatter | solution.py:281
  634.1 88.1 %reduce-scatter.9.cloned.1.call-done = bf16[192,3072]{1,0:T(8,128)(2,1)} async-done(((bf16[768,3072]{1,0:T(8,128)(2,1)}), bf16[192,3072]{1,0:T(8,128)(2,1)}) %reduce-scatter.9.cloned.1.call-update) | async-done | bytes 1179664 | tf_op jit(solution)/shard_map/reduce_scatter | solution.py:275
  722.2 12.2 %add_convert_fusion.2 = bf16[1024,768]{0,1:T(8,128)(2,1)} fusion(f32[1024,768]{0,1:T(8,128)} %copy-done.5, bf16[3072,768]{1,0:T(8,128)(2,1)} %all-gather.12.cloned.1.call-done, f32[768]{0:T(1024)S(1)} %convert_element_type.231, f32[1024,3072]{1,0:T(8,128)} %fusion.61, f32[3072]{0:T(1024)S(1)} %bitcast.89), kind=kOutput, calls=%fused_computation.67 | convolution fusion | flops 4865654784 | bytes 22035456 | tf_op jit(solution)/shard_map/dot_general | solution.py:183
  735.1 15.1 %all-reduce.17 = (bf16[192]{0:T(256)(128)(2,1)S(1)}, bf16[192]{0:T(256)(128)(2,1)S(1)}, bf16[192]{0:T(256)(128)(2,1)S(1)}, bf16[192]{0:T(256)(128)(2,1)S(1)}, bf...) all-reduce(bf16[192]{0:T(256)(128)(2,1)S(1)} %dynamic-slice.9, ...), channel_id=1, replica_groups=mesh['rep'=8,'shard'=4] {'rep'}, use_global_device_ids=true, to_apply=%region_16.17 | all-reduce | flops 2304 | bytes 9216 | tf_op jit(solution)/shard_map/psum | solution.py:289
  754.8 2.7 copy.76
  758.1 5.5 add_convert_fusion
  763.6 2.6 copy.77
  766.1 35.2 %all-reduce.23.cloned.1.call-done = (bf16[192,2304]{1,0:T(8,128)(2,1)}, bf16[192,768]{1,0:T(8,128)(2,1)}, bf16[192,3072]{1,0:T(8,128)(2,1)}, bf16[768,768]{1,0:T(8,128)(2,1)}) async-done(((bf16[192,2304]{1,0:T(8,128)(2,1)}, bf16[192,768]{1,0:T(8,128)(2,1)}, bf16[192,3072]{1,0:T(8,128)(2,1)}, bf16[768,768]{1,0:T(8,128)(2,1)}), (bf16[192,2304]{1,0:T(8,128)(2,1)}, bf16[192,768]{1,0:T(8,128)(2,1)}, ...) | async-done | bytes 3538960 | tf_op jit(solution)/shard_map/psum | solution.py:291
  803.3 2.6 convert_element_type.255
  (248 shorter events, 56.4 us)
Async XLA Ops:
  7.2 4.9 copy-start.65
  7.2 5.1 copy-start.66
  7.2 5.3 copy-start.67
  7.3 5.6 copy-start.68
  7.3 26.8 %copy-start.60 = (bf16[768]{0:T(1024)(128)(2,1)S(1)}, bf16[768]{0:T(1024)(128)(2,1)}, u32[]{:S(2)}) copy-start(bf16[768]{0:T(1024)(128)(2,1)} %param.29) | copy-start | bytes 4612
  7.3 28.0 %copy-start.49 = (s32[1,1024]{1,0:T(1,128)S(1)}, s32[1,1024]{1,0:T(1,128)}, u32[]{:S(2)}) copy-start(s32[1,1024]{1,0:T(1,128)} %param.17) | copy-start | bytes 12292
  7.3 75.5 %all-gather.6.cloned.1.call-start = ((), (), s32[]{:S(2)}) async-start(), calls=%async_computation.4 | async-start | bytes 4423680 | tf_op jit(solution)/shard_map/all_gather | solution.py:132
  8.0 178.3 %all-gather.8.cloned.1.call-start = ((), (), s32[]{:S(2)}) async-start(), calls=%async_computation.5 | async-start | bytes 1474560 | tf_op jit(solution)/shard_map/all_gather | solution.py:135
  8.8 194.8 %all-gather.10.cloned.1.call-start = ((), (), s32[]{:S(2)}) async-start(), calls=%async_computation.6 | async-start | bytes 5898240 | tf_op jit(solution)/shard_map/all_gather | solution.py:139
  9.5 283.4 %all-gather.12.cloned.1.call-start = ((), (), s32[]{:S(2)}) async-start(), calls=%async_computation.7 | async-start | bytes 5898240 | tf_op jit(solution)/shard_map/all_gather | solution.py:141
  10.1 531.1 %reduce-scatter.7.cloned.1.call-start = ((), (), s32[]{:S(2)}) async-start(), calls=%async_computation.9 | async-start | bytes 1474560 | tf_op jit(solution)/shard_map/reduce_scatter | solution.py:263
  34.0 48.8 %copy-start.56 = (f32[768]{0:T(1024)}, f32[768]{0:T(1024)S(1)}, u32[]{:S(2)}) copy-start(f32[768]{0:T(1024)S(1)} %convert_element_type.216) | copy-start | bytes 9220
  34.1 48.8 %copy-start.41 = (f32[768]{0:T(1024)}, f32[768]{0:T(1024)S(1)}, u32[]{:S(2)}) copy-start(f32[768]{0:T(1024)S(1)} %convert_element_type.215) | copy-start | bytes 9220
  35.3 16.9 %copy-start.52 = (s32[1024]{0:T(1024)}, s32[1024]{0:T(1024)S(1)}, u32[]{:S(2)}) copy-start(s32[1024]{0:T(1024)S(1)} %iota.18) | copy-start | bytes 12292
  51.4 134.9 %copy-start.3 = (bf16[1024,768]{0,1:T(8,128)(2,1)}, bf16[1024,768]{0,1:T(8,128)(2,1)S(1)}, u32[]{:S(2)}) copy-start(bf16[1024,768]{0,1:T(8,128)(2,1)S(1)} %copy.65) | copy-start | bytes 4718596
  51.7 37.3 %copy-start.39 = (f32[1024]{0:T(1024)}, f32[1024]{0:T(1024)S(1)}, u32[]{:S(2)}) copy-start(f32[1024]{0:T(1024)S(1)} %broadcast_multiply_fusion.1) | copy-start | bytes 12292
  52.7 36.2 %copy-start.43 = (f32[1024]{0:T(1024)}, f32[1024]{0:T(1024)S(1)}, u32[]{:S(2)}) copy-start(f32[1024]{0:T(1024)S(1)} %fusion.46) | copy-start | bytes 12292
  95.6 52.3 %copy-start.8 = (bf16[1024,768]{0,1:T(8,128)(2,1)}, bf16[1024,768]{0,1:T(8,128)(2,1)S(1)}, u32[]{:S(2)}) copy-start(bf16[1024,768]{0,1:T(8,128)(2,1)S(1)} %copy.68) | copy-start | bytes 4718596
  109.2 25.3 %copy-start.12 = (bf16[1024,768]{0,1:T(8,128)(2,1)S(1)}, bf16[1024,768]{0,1:T(8,128)(2,1)}, u32[]{:S(2)}) copy-start(bf16[1024,768]{0,1:T(8,128)(2,1)} %copy.66) | copy-start | bytes 4718596
  121.7 16.7 %copy-start.1 = (f32[12,512,1024]{2,1,0:T(8,128)S(1)}, f32[12,512,1024]{2,1,0:T(8,128)}, u32[]{:S(2)}) copy-start(f32[12,512,1024]{2,1,0:T(8,128)} %get-tuple-element.113) | copy-start | bytes 75497472
  160.0 16.1 %copy-start = (f32[12,512,1024]{2,1,0:T(8,128)S(1)}, f32[12,512,1024]{2,1,0:T(8,128)}, u32[]{:S(2)}) copy-start(f32[12,512,1024]{2,1,0:T(8,128)} %get-tuple-element.115) | copy-start | bytes 75497472
  160.0 16.2 %copy-start.16 = (pred[512,1024]{1,0:T(8,128)(4,1)S(1)}, pred[512,1024]{1,0:T(8,128)(4,1)}, u32[]{:S(2)}) copy-start(pred[512,1024]{1,0:T(8,128)(4,1)} %get-tuple-element.106) | copy-start | bytes 1572868
  189.8 13.8 %copy-start.36 = (f32[768]{0:T(1024)S(1)}, f32[768]{0:T(1024)}, u32[]{:S(2)}) copy-start(f32[768]{0:T(1024)} %convert_element_type.226) | copy-start | bytes 9220
  189.8 13.8 %copy-start.37 = (f32[768]{0:T(1024)S(1)}, f32[768]{0:T(1024)}, u32[]{:S(2)}) copy-start(f32[768]{0:T(1024)} %convert_element_type.227) | copy-start | bytes 9220
  191.9 101.0 %copy-start.23 = (bf16[1024,768]{1,0:T(8,128)(2,1)S(1)}, bf16[1024,768]{1,0:T(8,128)(2,1)}, u32[]{:S(2)}) copy-start(bf16[1024,768]{1,0:T(8,128)(2,1)} %param.18) | copy-start | bytes 4718596
  191.9 101.0 %copy-start.50 = (f32[4,1,768]{2,1,0:T(1,128)S(1)}, f32[4,1,768]{2,1,0:T(1,128)}, u32[]{:S(2)}) copy-start(f32[4,1,768]{2,1,0:T(1,128)} %convert_element_type.271) | copy-start | bytes 36868
  292.9 15.5 %copy-start.25 = (bf16[768,3072]{1,0:T(8,128)(2,1)S(1)}, bf16[768,3072]{1,0:T(8,128)(2,1)}, u32[]{:S(2)}) copy-start(bf16[768,3072]{1,0:T(8,128)(2,1)} %all-gather.10.cloned.1.call-done) | copy-start | bytes 14155780
  308.4 7.3 copy-start.71
  330.7 31.9 %copy-start.28 = (bf16[512,768]{0,1:T(8,128)(2,1)}, bf16[512,768]{0,1:T(8,128)(2,1)S(1)}, u32[]{:S(2)}) copy-start(bf16[512,768]{0,1:T(8,128)(2,1)S(1)} %get-tuple-element.102) | copy-start | bytes 2359300
  331.7 13.2 %copy-start.13 = (bf16[1024,768]{0,1:T(8,128)(2,1)S(1)}, bf16[1024,768]{0,1:T(8,128)(2,1)}, u32[]{:S(2)}) copy-start(bf16[1024,768]{0,1:T(8,128)(2,1)} %copy.66) | copy-start | bytes 4718596
  344.9 17.8 %copy-start.17 = (pred[512,1024]{1,0:T(8,128)(4,1)S(1)}, pred[512,1024]{1,0:T(8,128)(4,1)}, u32[]{:S(2)}) copy-start(pred[512,1024]{1,0:T(8,128)(4,1)} %get-tuple-element.106) | copy-start | bytes 1572868
  426.0 10.0 %copy-start.2 = (bf16[12,512,1024]{2,1,0:T(8,128)(2,1)S(1)}, bf16[12,512,1024]{2,1,0:T(8,128)(2,1)}, u32[]{:S(2)}) copy-start(bf16[12,512,1024]{2,1,0:T(8,128)(2,1)} %get-tuple-element.131) | copy-start | bytes 37748740
  441.1 105.1 %reduce-scatter.5.cloned.1.call-start = ((), (), s32[]{:S(2)}) async-start(), calls=%async_computation.8 | async-start | bytes 4423680 | tf_op jit(solution)/shard_map/reduce_scatter | solution.py:254
  441.5 9.4 %copy-start.11 = (f32[12,64,1024]{2,1,0:T(8,128)S(1)}, f32[12,64,1024]{2,1,0:T(8,128)}, u32[]{:S(2)}) copy-start(f32[12,64,1024]{2,1,0:T(8,128)} %fusion.75) | copy-start | bytes 9437188
  441.6 9.4 %copy-start.20 = (bf16[512,768]{0,1:T(8,128)(2,1)S(1)}, bf16[512,768]{0,1:T(8,128)(2,1)}, u32[]{:S(2)}) copy-start(bf16[512,768]{0,1:T(8,128)(2,1)} %copy.69) | copy-start | bytes 2359300
  450.9 7.0 copy-start.27
  458.0 15.4 %copy-start.26 = (bf16[12,64,1024]{2,1,0:T(8,128)(2,1)}, bf16[12,64,1024]{2,1,0:T(8,128)(2,1)S(1)}, u32[]{:S(2)}) copy-start(bf16[12,64,1024]{2,1,0:T(8,128)(2,1)S(1)} %multiply_convert_fusion.3) | copy-start | bytes 4718596
  459.8 13.5 %copy-start.31 = (bf16[1024,12,64]{0,2,1:T(8,128)(2,1)}, bf16[1024,12,64]{0,2,1:T(8,128)(2,1)S(1)}, u32[]{:S(2)}) copy-start(bf16[1024,12,64]{0,2,1:T(8,128)(2,1)S(1)} %get-tuple-element.97) | copy-start | bytes 4718596
  459.8 14.6 %copy-start.4 = (bf16[1024,768]{0,1:T(8,128)(2,1)S(1)}, bf16[1024,768]{0,1:T(8,128)(2,1)}, u32[]{:S(2)}) copy-start(bf16[1024,768]{0,1:T(8,128)(2,1)} %copy-done.3) | copy-start | bytes 4718596
  459.9 14.6 %copy-start.40 = (f32[1024]{0:T(1024)S(1)}, f32[1024]{0:T(1024)}, u32[]{:S(2)}) copy-start(f32[1024]{0:T(1024)} %copy-done.39) | copy-start | bytes 12292
  459.9 14.6 %copy-start.42 = (f32[768]{0:T(1024)S(1)}, f32[768]{0:T(1024)}, u32[]{:S(2)}) copy-start(f32[768]{0:T(1024)} %copy-done.41) | copy-start | bytes 9220
  459.9 14.6 %copy-start.44 = (f32[1024]{0:T(1024)S(1)}, f32[1024]{0:T(1024)}, u32[]{:S(2)}) copy-start(f32[1024]{0:T(1024)} %copy-done.43) | copy-start | bytes 12292
  459.9 14.6 %copy-start.57 = (f32[768]{0:T(1024)S(1)}, f32[768]{0:T(1024)}, u32[]{:S(2)}) copy-start(f32[768]{0:T(1024)} %copy-done.56) | copy-start | bytes 9220
  480.4 153.7 %reduce-scatter.11.cloned.1.call-start = ((), (), s32[]{:S(2)}) async-start(), calls=%async_computation.11 | async-start | bytes 5898240 | tf_op jit(solution)/shard_map/reduce_scatter | solution.py:281
  494.0 228.2 %reduce-scatter.9.cloned.1.call-start = ((), (), s32[]{:S(2)}) async-start(), calls=%async_computation.10 | async-start | bytes 5898240 | tf_op jit(solution)/shard_map/reduce_scatter | solution.py:275
  504.4 297.0 %all-reduce.23.cloned.1.call-start = ((), (), s32[]{:S(2)}) async-start(), calls=%async_computation.12 | async-start | bytes 7077888 | tf_op jit(solution)/shard_map/psum | solution.py:291
  734.4 23.7 %copy-start.15 = (bf16[1024,768]{0,1:T(8,128)(2,1)S(1)}, bf16[1024,768]{0,1:T(8,128)(2,1)}, u32[]{:S(2)}) copy-start(bf16[1024,768]{0,1:T(8,128)(2,1)} %copy.71) | copy-start | bytes 4718596
  734.4 23.7 %copy-start.46 = (f32[1024]{0:T(1024)S(1)}, f32[1024]{0:T(1024)}, u32[]{:S(2)}) copy-start(f32[1024]{0:T(1024)} %copy-done.45) | copy-start | bytes 12292
  (34 other events, 79.9 us)
Sparse Core Ops, SparseCore 0:
  9.7 73.0 all-gather.5
  84.4 29.0 all-gather.7
  115.1 88.5 all-gather.9
  205.0 87.8 all-gather.11
  441.2 27.6 reduce-scatter.6
  480.5 65.6 reduce-scatter.4
  548.5 85.4 reduce-scatter.10
  636.4 85.7 reduce-scatter.8
  725.9 75.4 all-reduce.22
where the time goes:
time: 819 us; the launch traced here: 816 us
  waiting for transfers between devices  335 us (41%)
  matrix products  236 us (29%)
  other arithmetic  108 us (13%)
  blocking collectives  67.3 us (8%)
  local copies, waits for them, and re-layouts  51.1 us (6%)
  between operations  16.8 us (2%)
    reduce_scatter x1, waiting for transfers between devices, shards(): lax.psum_scatter(grads[9].astype(jnp.bfloat16), 'shard', scatter_dimensio...  88.1 us
    reduce_scatter x1, waiting for transfers between devices, shards(): lax.psum_scatter(grads[11].astype(jnp.bfloat16), 'shard', scatter_dimensi...  87.8 us
    all_gather x1, waiting for transfers between devices, shards(): lax.all_gather(proj_weight, 'shard', axis=0, tiled=True)  78.1 us
    convert_element_type x1, other arithmetic, attend_backward(): grad_scores = (attn_probs * (grad_probs - inner)).astype(jnp.bfloat16)  41.8 us
    dot_general x2, matrix products, attend_backward(): jnp.einsum('qhd,khd->hqk', grad_block, value_heads, preferred_element_typ...  39.4 us
    unnamed x2, blocking collectives  38.9 us
    psum x1, waiting for transfers between devices, shards(): lax.psum(shares[2].astype(jnp.bfloat16), 'rep').astype(jnp.float32)  35.2 us
    unnamed x175, local copies, waits for them, and re-layouts  31.8 us
  transfers between devices with their start and end apart: 9, of which 7 were waited for; matrix products, arithmetic and copies ran while one was open for 27% of the time, Pallas kernels for 0%

commit v1 on v0

v1 whole, which is shorter than its diff:
```python
import functools
import math

import jax
import jax.numpy as jnp
from jax import lax
from jax.experimental import pallas as pl
from jax.experimental.pallas import tpu as pltpu
from jax.sharding import PartitionSpec as P

HEADS = 12
HEAD_DIM = 64
LOG2E = math.log2(math.e)
NEG = -1e30
BF16 = jnp.bfloat16
F32 = jnp.float32
VMEM_LIMIT = 56 << 20


def dot_nt(a, b):
    return lax.dot_general(a, b, (((1,), (1,)), ((), ())), preferred_element_type=F32)


def dot_nn(a, b):
    return lax.dot_general(a, b, (((1,), (0,)), ((), ())), preferred_element_type=F32)


def dot_tn(a, b):
    return lax.dot_general(a, b, (((0,), (0,)), ((), ())), preferred_element_type=F32)


def params():
    return pltpu.CompilerParams(vmem_limit_bytes=VMEM_LIMIT)


def swap(value, axis, size, mask):
    return lax.ppermute(value, axis, [(i, i ^ mask) for i in range(size)])


def allowed_block(seg_col, seg_row, block, rows):
    keys = (block + 1) * rows
    same = seg_col[:keys, :] == seg_row[:, block * rows : keys]
    causal = lax.broadcasted_iota(jnp.int32, (rows, rows), 0) <= lax.broadcasted_iota(
        jnp.int32, (rows, rows), 1
    )
    if block == 0:
        return same & causal
    return jnp.concatenate([same[: keys - rows], same[keys - rows :] & causal], axis=0)


def attend_kernel(rows, seg_col, seg_row, q_ref, k_ref, v_ref, o_ref, lse_ref):
    length = q_ref.shape[0]
    lane = lax.broadcasted_iota(jnp.int32, (1, 128), 1)
    scale = HEAD_DIM ** (-0.5) * LOG2E
    v_turned = v_ref[...].T
    for block in range(length // rows):
        keys = (block + 1) * rows
        here = slice(block * rows, keys)
        q = q_ref[here, :]
        k = k_ref[:keys, :]
        allowed = allowed_block(seg_col, seg_row, block, rows)
        parts = []
        for head in range(2):
            mine = (lane < 64) if head == 0 else (lane >= 64)
            q_head = jnp.where(mine, q, jnp.zeros_like(q))
            scores = jnp.where(allowed, dot_nt(k, q_head), NEG)
            highest = jnp.max(scores, axis=0, keepdims=True)
            expo = jnp.exp2((scores - highest) * scale)
            summed = jnp.sum(expo, axis=0, keepdims=True)
            v_head = v_turned[head * 64 : (head + 1) * 64, :keys]
            parts.append(dot_nn(v_head, expo.astype(BF16)) * (1.0 / summed))
            lse_ref[head, :, here] = jnp.broadcast_to(
                highest * scale + jnp.log2(summed), (8, rows)
            )
        o_ref[here, :] = jnp.concatenate(parts, axis=0).T.astype(BF16)


def head_specs(length, start):
    groups = HEADS // 2
    return [
        pl.BlockSpec((length, 1), lambda h: (0, 0)),
        pl.BlockSpec((1, length), lambda h: (0, 0)),
        pl.BlockSpec((length, 128), lambda h: (0, start + h)),
        pl.BlockSpec((length, 128), lambda h: (0, groups + start + h)),
        pl.BlockSpec((length, 128), lambda h: (0, 2 * groups + start + h)),
    ]


def attend_forward(qkv, segment, start, count):
    length = qkv.shape[0]
    rows = length // 2
    return pl.pallas_call(
        functools.partial(attend_kernel, rows),
        grid=(count,),
        in_specs=head_specs(length, start),
        out_specs=[
            pl.BlockSpec((length, 128), lambda h: (0, h)),
            pl.BlockSpec((2, 8, length), lambda h: (h, 0, 0)),
        ],
        out_shape=[
            jax.ShapeDtypeStruct((length, 128 * count), BF16),
            jax.ShapeDtypeStruct((2 * count, 8, length), F32),
        ],
        compiler_params=params(),
        cost_estimate=pl.CostEstimate(
            flops=3 * 10**9 * count, bytes_accessed=count << 20, transcendentals=10**6 * count
        ),
        name="attend_forward",
    )(segment.reshape(length, 1), segment.reshape(1, length), qkv, qkv, qkv)


def attend_back_kernel(
    rows, seg_col, seg_row, q_ref, k_ref, v_ref, g_ref, lse_ref, dq_ref, dk_ref, dv_ref, dk_sum, dv_sum
):
    length = q_ref.shape[0]
    lane = lax.broadcasted_iota(jnp.int32, (1, 128), 1)
    scale = HEAD_DIM ** (-0.5) * LOG2E
    blocks = length // rows
    for block in reversed(range(blocks)):
        keys = (block + 1) * rows
        here = slice(block * rows, keys)
        q = q_ref[here, :]
        g = g_ref[here, :]
        k = k_ref[:keys, :]
        v = v_ref[:keys, :]
        allowed = allowed_block(seg_col, seg_row, block, rows)
        dq = dk = dv = None
        for head in range(2):
            mine = (lane < 64) if head == 0 else (lane >= 64)
            q_head = jnp.where(mine, q, jnp.zeros_like(q))
            g_head = jnp.where(mine, g, jnp.zeros_like(g))
            scores = dot_nt(k, q_head) * scale - lse_ref[head, 0:1, here]
            probs = jnp.exp2(jnp.where(allowed, scores, NEG))
            grad_probs = dot_nt(v, g_head)
            inner = jnp.sum(probs * grad_probs, axis=0, keepdims=True)
            grad_scores = (probs * (grad_probs - inner)).astype(BF16)
            dv_head = dot_nn(probs.astype(BF16), g_head)
            dk_head = dot_nn(grad_scores, q_head)
            dq_head = dot_tn(grad_scores, k)
            if head == 0:
                dq, dk, dv = dq_head, dk_head, dv_head
            else:
                dq, dk, dv = jnp.where(lane < 64, dq, dq_head), dk + dk_head, dv + dv_head
        dq_ref[here, :] = (dq * HEAD_DIM ** (-0.5)).astype(BF16)
        if block == blocks - 1:
            dk_sum[...] = dk
            dv_sum[...] = dv
        else:
            dk_sum[:keys, :] += dk
            dv_sum[:keys, :] += dv
    dk_ref[...] = (dk_sum[...] * HEAD_DIM ** (-0.5)).astype(BF16)
    dv_ref[...] = dv_sum[...].astype(BF16)


def attend_backward(qkv, segment, grad, lse, start, count):
    length = qkv.shape[0]
    rows = length // 2
    return pl.pallas_call(
        functools.partial(attend_back_kernel, rows),
        grid=(count,),
        in_specs=head_specs(length, start)
        + [
            pl.BlockSpec((length, 128), lambda h: (0, start + h)),
            pl.BlockSpec((2, 8, length), lambda h: (h, 0, 0)),
        ],
        out_specs=[pl.BlockSpec((length, 128), lambda h: (0, h))] * 3,
        out_shape=[jax.ShapeDtypeStruct((length, 128 * count), BF16)] * 3,
        scratch_shapes=[pltpu.VMEM((length, 128), F32)] * 2,
        compiler_params=params(),
        cost_estimate=pl.CostEstimate(
            flops=6 * 10**9 * count, bytes_accessed=2 * count << 20, transcendentals=10**6 * count
        ),
        name="attend_backward",
    )(segment.reshape(length, 1), segment.reshape(1, length), qkv, qkv, qkv, grad, lse)


def position_to_rel(slot, pieces, first):
    if pieces == 4 and first == 2:
        return (slot & 1) * 2 + slot // 2
    return slot


def place_rows(total, old_ref, outs, spots, pieces, first, by_shard):
    for slot in range(pieces):
        piece = position_to_rel(slot, pieces, first) ^ spots[1]
        for rel_z in range(outs[0].shape[1]):
            rows = outs[0].shape[2]
            owner = 0 if by_shard else rel_z ^ spots[2]
            start = pl.multiple_of((owner * pieces + piece) * rows, 16)
            value = total[pl.ds(start, rows), :]
            if old_ref is not None:
                value = value + old_ref[slot, rel_z].astype(F32)
            size = outs[0].shape[0]
            outs[slot // size][slot % size, rel_z] = value.astype(BF16)


def grad_proj_kernel(pieces, first, add, spots, x_ref, y_ref, *rest):
    total = rest[-1]
    total[...] = dot_tn(x_ref[...], y_ref[...])
    old_ref, outs = (rest[0], rest[1:-1]) if add else (None, rest[:-1])
    place_rows(total, old_ref, outs, spots, pieces, first, True)


def grad_two_kernel(pieces, first, add, tiles, spots, x_ref, y_ref, x2_ref, y2_ref, *rest):
    total = rest[-1]

    @pl.when(pl.program_id(0) < tiles)
    def _():
        total[...] = dot_tn(x_ref[...], y_ref[...])

    @pl.when(pl.program_id(0) >= tiles)
    def _():
        total[...] = dot_tn(x2_ref[...], y2_ref[...])

    old_ref, outs = (rest[0], rest[1:-1]) if add else (None, rest[:-1])
    place_rows(total, old_ref, outs, spots, pieces, first, False)


def grad_heads_kernel(pieces, first, add, spots, x_ref, q_ref, k_ref, v_ref, *rest):
    total = rest[-1]
    joined = jnp.concatenate([q_ref[...], k_ref[...], v_ref[...]], axis=1)
    total[...] = dot_tn(x_ref[...], joined)
    old_ref, outs = (rest[0], rest[1:-1]) if add else (None, rest[:-1])
    place_rows(total, old_ref, outs, spots, pieces, first, False)


def grad_call(kernel, grid, in_specs, operands, block, shape, pieces, scratch, spots, old, flops):
    if old is not None:
        in_specs = in_specs + [block(pieces)]
        operands = operands + [old]
        out_specs = [block(pieces // 2)] * 2
        out_shape = [shape(pieces // 2)] * 2
    else:
        out_specs = block(pieces)
        out_shape = shape(pieces)
    return pl.pallas_call(
        kernel,
        grid_spec=pltpu.PrefetchScalarGridSpec(
            num_scalar_prefetch=1,
            grid=grid,
            in_specs=in_specs,
            out_specs=out_specs,
            scratch_shapes=[scratch],
        ),
        out_shape=out_shape,
        compiler_params=params(),
        cost_estimate=pl.CostEstimate(flops=2 * flops, bytes_accessed=4 << 20, transcendentals=0),
        name="weight_grad",
    )(spots, *operands)


def side_of(add):
    return (lambda s: s[0]) if add else (lambda s: 1 - s[0])


def grad_proj(x, y, spots, shards, pieces, first, old=None):
    length, rows_all = x.shape
    half = y.shape[1] // 2
    rows = rows_all // (shards * pieces)
    side = side_of(old is not None)
    return grad_call(
        functools.partial(grad_proj_kernel, pieces, first, old is not None),
        (shards,),
        [
            pl.BlockSpec((length, rows_all // shards), lambda i, s: (0, i ^ s[2])),
            pl.BlockSpec((length, half), lambda i, s: (0, side(s))),
        ],
        [x, y],
        lambda n: pl.BlockSpec((n, 1, rows, half), lambda i, s: (0, i, 0, 0)),
        lambda n: jax.ShapeDtypeStruct((n, shards, rows, half), BF16),
        pieces,
        pltpu.VMEM((rows_all // shards, half), F32),
        spots,
        old,
        length * rows_all * half,
    )


def grad_two(x, y, x2, y2, spots, shards, pieces, first, old=None):
    length, rows_all = x.shape
    half, half2 = y.shape[1] // 2, y2.shape[1] // 2
    rows = rows_all // (shards * pieces)
    tiles = half // half2
    side = side_of(old is not None)
    return grad_call(
        functools.partial(grad_two_kernel, pieces, first, old is not None, tiles),
        (tiles + 1,),
        [
            pl.BlockSpec((length, rows_all), lambda i, s: (0, 0)),
            pl.BlockSpec(
                (length, half2), lambda i, s: (0, side(s) * tiles + jnp.minimum(i, tiles - 1))
            ),
            pl.BlockSpec((length, rows_all), lambda i, s: (0, 0)),
            pl.BlockSpec((length, half2), lambda i, s: (0, side(s))),
        ],
        [x, y, x2, y2],
        lambda n: pl.BlockSpec((n, shards, rows, half2), lambda i, s: (0, 0, 0, i)),
        lambda n: jax.ShapeDtypeStruct((n, shards, rows, half + half2), BF16),
        pieces,
        pltpu.VMEM((rows_all, half2), F32),
        spots,
        old,
        length * rows_all * (half + half2),
    )


def grad_heads(x, grads, spots, shards, pieces, first, old=None):
    length, rows_all = x.shape
    half = grads[0].shape[1] // 2
    rows = rows_all // (shards * pieces)
    side = side_of(old is not None)
    return grad_call(
        functools.partial(grad_heads_kernel, pieces, first, old is not None),
        (1,),
        [pl.BlockSpec((length, rows_all), lambda i, s: (0, 0))]
        + [pl.BlockSpec((length, half), lambda i, s: (0, side(s)))] * 3,
        [x, *grads],
        lambda n: pl.BlockSpec((n, shards, rows, 3 * half), lambda i, s: (0, 0, 0, 0)),
        lambda n: jax.ShapeDtypeStruct((n, shards, rows, 3 * half), BF16),
        pieces,
        pltpu.VMEM((rows_all, 3 * half), F32),
        spots,
        old,
        length * rows_all * 3 * half,
    )


def assemble_kernel(shards, pieces, rows, column, spots, own_ref, *rest):
    parts = rest[: 2 * pieces]
    full_ref, sems = rest[2 * pieces :]
    core, spot_u, spot_z = spots[0], spots[1], spots[2]
    shard_rows = own_ref.shape[0]
    half = own_ref.shape[1] // 2
    copies = [
        pltpu.make_async_copy(
            own_ref,
            full_ref.at[pl.ds(pl.multiple_of(spot_z * shard_rows, 16), shard_rows), :],
            sems.at[0],
        )
    ]
    for index, part in enumerate(parts):
        side = core if index < pieces else 1 - core
        piece = spot_u ^ (index % pieces)
        for step in range(1, shards):
            start = pl.multiple_of((spot_z ^ step) * shard_rows + piece * rows, 16)
            copies.append(
                pltpu.make_async_copy(
                    part.at[step - 1, pl.ds(0, rows), pl.ds(column, half)],
                    full_ref.at[pl.ds(start, rows), pl.ds(pl.multiple_of(side * half, 128), half)],
                    sems.at[len(copies)],
                )
            )
    for copy in copies:
        copy.start()
    for copy in copies:
        copy.wait()


def assemble(own, parts, column, spots, shards, pieces):
    shard_rows, width = own.shape
    rows = shard_rows // pieces
    anywhere = pl.BlockSpec(memory_space=pl.ANY)
    return pl.pallas_call(
        functools.partial(assemble_kernel, shards, pieces, rows, column),
        in_specs=[pl.BlockSpec(memory_space=pltpu.SMEM)] + [anywhere] * (1 + 2 * pieces),
        out_specs=pl.BlockSpec(memory_space=pltpu.VMEM),
        out_shape=jax.ShapeDtypeStruct((shards * shard_rows, width), BF16),
        scratch_shapes=[pltpu.SemaphoreType.DMA((1 + 2 * pieces * (shards - 1),))],
        compiler_params=params(),
        cost_estimate=pl.CostEstimate(
            flops=0, bytes_accessed=4 * shards * shard_rows * width, transcendentals=0
        ),
        name="assemble",
    )(spots, own, *parts)


def settle_kernel(pieces, every_ref, *outs):
    rows = every_ref.shape[1]
    for index in range(2 * pieces):
        piece, core = index // 2, index % 2
        column = 0
        for out_ref in outs:
            half = out_ref.shape[1] // 2
            out_ref[piece * rows : (piece + 1) * rows, core * half : (core + 1) * half] = every_ref[
                index, :, column : column + half
            ].astype(F32)
            column += half


def settle(every, widths, pieces):
    rows = every.shape[1]
    whole = pl.BlockSpec(memory_space=pltpu.VMEM)
    return pl.pallas_call(
        functools.partial(settle_kernel, pieces),
        in_specs=[whole],
        out_specs=[whole] * len(widths),
        out_shape=[jax.ShapeDtypeStruct((rows * pieces, width), F32) for width in widths],
        compiler_params=params(),
        name="settle",
    )(every)


def settle_heads_kernel(pieces, spots, every_ref, *rest):
    parts, out_ref = rest[: 2 * pieces], rest[2 * pieces]
    core, spot_u = spots[0], spots[1]
    rows = every_ref.shape[1]
    wide, narrow = every_ref.shape[2] // 3, parts[0].shape[1] // 3
    width = out_ref.shape[1] // 3
    for index in range(2 * pieces):
        for kind in range(3):
            column = kind * width + (index % 2) * wide
            out_ref[
                (index // 2) * rows : (index // 2 + 1) * rows, column : column + wide
            ] = every_ref[index, :, kind * wide : (kind + 1) * wide].astype(F32)
    for index, part in enumerate(parts):
        side = core if index < pieces else 1 - core
        start = pl.multiple_of((spot_u ^ (index % pieces)) * rows, 16)
        for kind in range(3):
            column = pl.multiple_of(kind * width + 2 * wide + side * narrow, 128)
            out_ref[pl.ds(start, rows), pl.ds(column, narrow)] = part[
                :, kind * narrow : (kind + 1) * narrow
            ].astype(F32)


def settle_heads(every, parts, spots, pieces):
    rows = every.shape[1]
    columns = 2 * (every.shape[2] + parts[0].shape[1])
    whole = pl.BlockSpec(memory_space=pltpu.VMEM)
    return pl.pallas_call(
        functools.partial(settle_heads_kernel, pieces),
        in_specs=[pl.BlockSpec(memory_space=pltpu.SMEM)] + [whole] * (1 + 2 * pieces),
        out_specs=whole,
        out_shape=jax.ShapeDtypeStruct((rows * pieces, columns), F32),
        compiler_params=params(),
        name="settle_heads",
    )(spots, every, *parts)


def layer_norm(values, gain, shift):
    center = values - jnp.mean(values, axis=-1, keepdims=True)
    spread_of = jnp.mean(center * center, axis=-1, keepdims=True)
    return center * lax.rsqrt(spread_of + 1e-05) * gain + shift


def norm_scale(values, gain):
    center = values - jnp.mean(values, axis=-1, keepdims=True)
    spread_of = jnp.mean(center * center, axis=-1, keepdims=True)
    return center * lax.rsqrt(spread_of + 1e-05) * gain


def gelu_tanh(values):
    return jax.nn.gelu(values, approximate=True)


def column_sum(values):
    return jnp.sum(values.astype(F32), axis=0)


def shards_of(
    reps,
    shards,
    hidden_in,
    segment,
    cotangent,
    ln1_gain,
    ln1_bias,
    qkv_weight,
    query_bias,
    value_bias,
    out_weight,
    out_bias,
    ln2_gain,
    ln2_bias,
    fc_weight,
    fc_bias,
    proj_weight,
    proj_bias,
):
    width = hidden_in.shape[1]
    shard_rows = qkv_weight.shape[0]
    pieces = 4 if shard_rows % 64 == 0 and reps % 8 == 0 else 2
    rep = lax.axis_index("rep")
    spot_z = lax.axis_index("shard")
    core = rep & 1
    spot_u = (rep >> 1) & (pieces - 1)
    spots = jnp.stack([core, spot_u, spot_z]).astype(jnp.int32)

    def own_piece(weight):
        rows, half = weight.shape[0] // pieces, weight.shape[1] // 2
        return lax.dynamic_slice(weight, (spot_u * rows, core * half), (rows, half))

    def across_chips(part, first):
        if pieces == 2:
            return [part, swap(part, "rep", reps, 2)]
        second = 6 - first
        by_first = swap(part, "rep", reps, first)
        by_second = swap(part, "rep", reps, second)
        by_both = swap(by_first, "rep", reps, second)
        if first == 2:
            return [part, by_first, by_second, by_both]
        return [part, by_second, by_first, by_both]

    def across_cores(parts):
        return parts + [swap(part, "rep", reps, 1) for part in parts]

    def along_shard(piece):
        return [swap(piece, "shard", shards, step) for step in range(1, shards)]

    out_half = width // 2
    fc_half = fc_weight.shape[1] // 2
    second_width = out_half + fc_half
    piece_rows = shard_rows // pieces
    qkv_slots = along_shard(own_piece(qkv_weight))
    small = jnp.concatenate(
        [
            ln1_gain,
            ln1_bias,
            query_bias,
            value_bias,
            out_bias,
            ln2_gain,
            ln2_bias,
            proj_bias,
            fc_bias,
        ]
    )
    small_rows = -(-small.shape[0] // second_width)
    small = jnp.pad(small, (0, 16 * second_width - small.shape[0])).reshape(16, second_width)
    second_payload = jnp.concatenate(
        [jnp.concatenate([own_piece(out_weight), own_piece(fc_weight)], axis=1), small], axis=0
    )
    second_slots = along_shard(second_payload)
    qkv_parts = across_chips(jnp.stack(qkv_slots), 2)
    proj_piece, second_slots = lax.optimization_barrier((own_piece(proj_weight), second_slots))
    proj_slots = along_shard(proj_piece)
    qkv_parts = across_cores(qkv_parts)
    second_stack, proj_slots, qkv_parts = lax.optimization_barrier(
        (jnp.stack(second_slots), proj_slots, qkv_parts)
    )
    second_parts = across_chips(second_stack, 2)
    proj_parts = across_chips(jnp.stack(proj_slots), 4)
    second_parts = across_cores(second_parts)
    proj_parts = across_cores(proj_parts)

    rows_of = [small[:small_rows]] + [
        slot[piece_rows : piece_rows + small_rows] for slot in second_slots
    ]
    ordered = []
    for index in range(shards):
        total = jnp.zeros_like(rows_of[0])
        for step, value in enumerate(rows_of):
            total = jnp.where((spot_z ^ step) == index, value, total)
        ordered.append(total.reshape(-1))
    vectors = jnp.stack(ordered).astype(F32)

    def vector(index):
        return vectors[:, index * shard_rows : (index + 1) * shard_rows].reshape(-1)

    gain_one, shift_one, bias_query, bias_value, bias_out, gain_two, shift_two, bias_proj = [
        vector(index) for index in range(8)
    ]
    fc_start = 8 * shard_rows
    bias_fc = vectors[:, fc_start : fc_start + fc_bias.shape[0]].reshape(-1)

    w_qkv = assemble(qkv_weight, qkv_parts, 0, spots, shards, pieces)
    w_out = assemble(out_weight, second_parts, 0, spots, shards, pieces)
    w_fc = assemble(fc_weight, second_parts, out_half, spots, shards, pieces)
    w_proj = assemble(proj_weight, proj_parts, 0, spots, shards, pieces)

    seg_row = segment[0]
    inputs = hidden_in.astype(F32)
    norm_one = layer_norm(inputs, gain_one, shift_one).astype(BF16)
    qkv_bias = jnp.concatenate([bias_query, jnp.zeros_like(bias_query), bias_value])
    qkv = (jnp.dot(norm_one, w_qkv, preferred_element_type=F32) + qkv_bias).astype(BF16)
    attended_one, lse_one = attend_forward(qkv, seg_row, 0, 4)
    attended_two, lse_two = attend_forward(qkv, seg_row, 4, 2)
    attended = jnp.concatenate([attended_one, attended_two], axis=1)
    resid = inputs + jnp.dot(attended, w_out, preferred_element_type=F32) + bias_out
    norm_two = layer_norm(resid, gain_two, shift_two).astype(BF16)
    pre_act = jnp.dot(norm_two, w_fc, preferred_element_type=F32) + bias_fc
    gelu_low = gelu_tanh(pre_act).astype(BF16)

    def reduce_chips(keep, send, first):
        came = swap(send, "rep", reps, first)
        held = keep[0].astype(F32) + came[0].astype(F32)
        if pieces == 2:
            return held
        onward = (keep[1].astype(F32) + came[1].astype(F32)).astype(BF16)
        came = swap(onward, "rep", reps, 6 - first)
        return held + came.astype(F32)

    def reduce_shard(held):
        total = held[0]
        for step in range(1, shards):
            total = total + swap(held[step].astype(BF16), "shard", shards, step).astype(F32)
        mask = 2 * pieces
        while mask < reps:
            total = total + swap(total.astype(BF16), "rep", reps, mask).astype(F32)
            mask *= 2
        return total.astype(BF16)

    def every_owner(piece):
        return lax.all_gather(piece, "rep", axis=0, tiled=False)[: 2 * pieces]

    call = (spots, shards, pieces)
    proj_far = grad_proj(gelu_low, cotangent, *call, 2)
    gelu_low, proj_far = lax.optimization_barrier((gelu_low, proj_far))
    proj_old = swap(proj_far, "rep", reps, 1)
    block_out = (
        resid + jnp.dot(gelu_low, w_proj, preferred_element_type=F32) + bias_proj
    ).astype(BF16)
    gelu_low, block_out = lax.optimization_barrier((gelu_low, block_out))
    proj_keep, proj_send = grad_proj(gelu_low, cotangent, *call, 2, proj_old)
    proj_keep, proj_send, cotangent = lax.optimization_barrier((proj_keep, proj_send, cotangent))
    proj_held = reduce_chips(proj_keep, proj_send, 2)

    grad_out = cotangent.astype(F32)
    d_proj_bias = column_sum(cotangent)
    grad_gelu = jnp.einsum("td,fd->tf", cotangent, w_proj, preferred_element_type=F32)
    _, gelu_pull = jax.vjp(gelu_tanh, pre_act)
    grad_pre = gelu_pull(grad_gelu)[0].astype(BF16)
    d_fc_bias = column_sum(grad_pre)
    grad_norm_two = jnp.einsum("tf,df->td", grad_pre, w_fc, preferred_element_type=F32)
    _, norm_pull_two = jax.vjp(norm_scale, resid, gain_two)
    grad_resid_norm, d_ln2_gain = norm_pull_two(grad_norm_two)
    d_ln2_bias = jnp.sum(grad_norm_two, axis=0)
    grad_resid = grad_out + grad_resid_norm
    grad_branch = grad_resid.astype(BF16)
    d_out_bias = column_sum(grad_branch)
    fc_far = grad_two(norm_two, grad_pre, attended, grad_branch, *call, 4)
    grad_branch, fc_far, proj_held = lax.optimization_barrier((grad_branch, fc_far, proj_held))
    fc_old = swap(fc_far, "rep", reps, 1)
    grad_attended = jnp.einsum(
        "te,de->td", grad_branch, w_out, preferred_element_type=F32
    ).astype(BF16)
    grad_attended, fc_old = lax.optimization_barrier((grad_attended, fc_old))
    fc_keep, fc_send = grad_two(norm_two, grad_pre, attended, grad_branch, *call, 4, fc_old)
    fc_keep, fc_send, grad_attended = lax.optimization_barrier((fc_keep, fc_send, grad_attended))
    fc_held = reduce_chips(fc_keep, fc_send, 4)
    proj_piece = reduce_shard(proj_held)
    heads_one = attend_backward(qkv, seg_row, grad_attended, lse_one, 0, 4)
    heads_one, proj_piece = lax.optimization_barrier((heads_one, proj_piece))
    one_far = grad_heads(norm_one, heads_one, *call, 2)
    one_far, grad_attended = lax.optimization_barrier((one_far, grad_attended))
    one_old = swap(one_far, "rep", reps, 1)
    heads_two = attend_backward(qkv, seg_row, grad_attended, lse_two, 4, 2)
    heads_two, one_old, fc_held = lax.optimization_barrier((heads_two, one_old, fc_held))
    two_far = grad_heads(norm_one, heads_two, *call, 4)
    two_old = swap(two_far, "rep", reps, 1)
    norm_one, two_far = lax.optimization_barrier((norm_one, two_far))
    one_keep, one_send = grad_heads(norm_one, heads_one, *call, 2, one_old)
    two_keep, two_send = grad_heads(norm_one, heads_two, *call, 4, two_old)
    heads_one, heads_two, one_send, two_send = lax.optimization_barrier(
        (heads_one, heads_two, one_send, two_send)
    )
    two_piece = reduce_shard(reduce_chips(two_keep, two_send, 4))
    one_piece = reduce_shard(reduce_chips(one_keep, one_send, 2))
    fc_piece = reduce_shard(fc_held)
    two_parts = across_cores(across_chips(two_piece, 2))
    d_qkv_weight = settle_heads(every_owner(one_piece), two_parts, spots, pieces)
    d_fc_weight, d_out_weight = settle(
        every_owner(fc_piece), (fc_weight.shape[1], width), pieces
    )
    (d_proj_weight,) = settle(every_owner(proj_piece), (width,), pieces)

    grad_queries, grad_keys, grad_values = [
        jnp.concatenate([one, two], axis=1) for one, two in zip(heads_one, heads_two)
    ]
    d_query_bias = column_sum(grad_queries)
    d_value_bias = column_sum(grad_values)
    grad_qkv = jnp.concatenate([grad_queries, grad_keys, grad_values], axis=1)
    grad_norm_one = jnp.einsum("te,de->td", grad_qkv, w_qkv, preferred_element_type=F32)
    _, norm_pull_one = jax.vjp(norm_scale, inputs, gain_one)
    grad_input_norm, d_ln1_gain = norm_pull_one(grad_norm_one)
    d_ln1_bias = jnp.sum(grad_norm_one, axis=0)
    input_grad = (grad_resid + grad_input_norm).astype(BF16)

    small_grads = jnp.stack(
        [
            d_ln1_gain,
            d_ln1_bias,
            d_query_bias,
            d_value_bias,
            d_out_bias,
            d_ln2_gain,
            d_ln2_bias,
            d_proj_bias,
        ]
        + [d_fc_bias[i * width : (i + 1) * width] for i in range(d_fc_bias.shape[0] // width)]
    )
    for axis, size in (("rep", reps), ("shard", shards)):
        mask = 1
        while mask < size:
            small_grads = small_grads + swap(small_grads, axis, size, mask)
            mask *= 2
    mine = lax.dynamic_slice(small_grads[:8], (0, spot_z * shard_rows), (8, shard_rows))
    fc_rows = fc_bias.shape[0]
    d_fc_bias = lax.dynamic_slice(small_grads[8:].reshape(-1), (spot_z * fc_rows,), (fc_rows,))
    return (
        block_out,
        input_grad,
        mine[0],
        mine[1],
        d_qkv_weight,
        mine[2],
        mine[3],
        d_out_weight,
        mine[4],
        mine[5],
        mine[6],
        d_fc_weight,
        d_fc_bias,
        d_proj_weight,
        mine[7],
    )


def solution(mesh):
    tokens = P(("rep", "shard"), None)
    flat = P("shard")
    rows = P("shard", None)
    in_specs = (
        tokens,
        tokens,
        tokens,
        flat,
        flat,
        rows,
        flat,
        flat,
        rows,
        flat,
        flat,
        flat,
        rows,
        flat,
        rows,
        flat,
    )
    out_specs = (
        tokens,
        tokens,
        flat,
        flat,
        rows,
        flat,
        flat,
        rows,
        flat,
        flat,
        flat,
        rows,
        flat,
        rows,
        flat,
    )
    body = functools.partial(shards_of, mesh.shape["rep"], mesh.shape["shard"])
    return jax.shard_map(
        body, mesh=mesh, in_specs=in_specs, out_specs=out_specs, check_vma=False
    )
```

time: 819 us -> 459 us (0.56)
  waiting for transfers between devices: 335 us -> 99.8 us
  matrix products: 236 us -> 66.1 us
  Pallas kernels: 0 us -> 141 us
  other arithmetic: 108 us -> 25.3 us
  starting transfers between devices: 0.94 us -> 69 us
  blocking collectives: 67.3 us -> 10.4 us
  local copies, waits for them, and re-layouts: 51.1 us -> 26.8 us
    reduce_scatter x4 -> x0, waiting for transfers between devices: 181 us -> none  [the longest x1 88.1 us: shards(): lax.psum_scatter(grads[9].astype(jnp.bfloat16), 'shard', scatter_dimensio...]
    dot_general x24 -> x8, matrix products: 236 us -> 66.1 us  [the longest x1 15.2 us: shards_of(): jnp.einsum('td,fd->tf', cotangent, w_proj, preferred_element_type=F32)]
    pallas_call x0 -> x19, Pallas kernels: none -> 141 us  [the longest x8 56.1 us: grad_call(): pl.pallas_call(kernel, grid_spec=pltpu.PrefetchScalarGridSpec(num_scalar_...]
    all_gather x4 -> x2, waiting for transfers between devices: 116 us -> 0.01 us  [every_owner(): return lax.all_gather(piece, 'rep', axis=0, tiled=False)[:2 * pieces]]
    ppermute x0 -> x66, waiting for transfers between devices: none -> 99.8 us  [swap(): return lax.ppermute(value, axis, [(i, i ^ mask) for i in range(size)])]
    ppermute x0 -> x66, starting transfers between devices: none -> 68.9 us  [swap(): return lax.ppermute(value, axis, [(i, i ^ mask) for i in range(size)])]
    convert_element_type x25 -> x11, other arithmetic: 67 us -> 5.88 us  [the longest x4 1.79 us: reduce_chips(): onward = (keep[1].astype(F32) + came[1].astype(F32)).astype(BF16)]
    unnamed x2 -> x0, blocking collectives: 38.9 us -> none
  transfers between devices with their start and end apart: 9 -> 68, of which waited for: 7 -> 23; matrix products, arithmetic and copies ran while one was open for 27% -> 23% of each run, Pallas kernels for 0% -> 26%
where the time goes in v1:
time: 459 us; the launch traced here: 454 us
  Pallas kernels  141 us (31%)
  waiting for transfers between devices  99.8 us (22%)
  starting transfers between devices  69 us (15%)
  matrix products  66.1 us (14%)
  local copies, waits for them, and re-layouts  26.8 us (6%)
  other arithmetic  25.3 us (6%)
  between operations  15.5 us (3%)
  blocking collectives  10.4 us (2%)
    ppermute x66, waiting for transfers between devices, swap(): return lax.ppermute(value, axis, [(i, i ^ mask) for i in range(size)])  99.8 us
    ppermute x66, starting transfers between devices, swap(): return lax.ppermute(value, axis, [(i, i ^ mask) for i in range(size)])  68.9 us
    pallas_call x8, Pallas kernels, grad_call(): pl.pallas_call(kernel, grid_spec=pltpu.PrefetchScalarGridSpec(num_scalar_...  56.1 us
    pallas_call x2, Pallas kernels, attend_backward(): pl.pallas_call(functools.partial(attend_back_kernel, rows), grid=(count,)...  37.4 us
    pallas_call x2, Pallas kernels, attend_forward(): pl.pallas_call(functools.partial(attend_kernel, rows), grid=(count,), in_...  20.4 us
    pallas_call x4, Pallas kernels, assemble(): pl.pallas_call(functools.partial(assemble_kernel, shards, pieces, rows, c...  18.4 us
    dot_general x1, matrix products, shards_of(): jnp.einsum('td,fd->tf', cotangent, w_proj, preferred_element_type=F32)  15.2 us
    dot_general x1, matrix products, shards_of(): pre_act = jnp.dot(norm_two, w_fc, preferred_element_type=F32) + bias_fc  14.1 us
  transfers between devices with their start and end apart: 68, of which 23 were waited for; matrix products, arithmetic and copies ran while one was open for 23% of the time, Pallas kernels for 26%

profile of v1, /device:TPU:0, one launch (start us, length us, event | category | flops | bytes accessed | tf_op | source)
XLA Modules:
  0.0 453.5 jit_solution(2290888754886391217)
XLA Ops:
  7.3 6.2 %concatenate.26 = bf16[2304]{0:T(1024)(128)(2,1)S(1)} concatenate(bf16[192]{0:T(256)(128)(2,1)} %param.19, bf16[192]{0:T(256)(128)(2,1)} %param.20, bf16[192]{0:T(256)(128)(2,1)} %param.22, bf16[192]{0:T(256)(128)(2,1)} %param.23, bf16[192]{0:T(256)(128)(2,1)} %param.25, bf16[192]{0:T(256)(128)(2,1)} %param.26, bf16[192]{0:T(256)(128)(2,1)} %param.27, bf16[192]{0:T(256)(128)(2,1)} %param.31, ...), dimensions={0} | concatenate | bytes 9216 | tf_op jit(solution)/shard_map/concatenate | solution.py:514
  15.3 3.1 collective-permute-start
  18.4 2.6 collective-permute-start.1
  21.9 3.9 collective-permute-start.8
  28.7 12.0 %collective-permute-done.8 = bf16[48,1152]{1,0:T(8,128)(2,1)S(1)} collective-permute-done((bf16[48,1152]{1,0:T(8,128)(2,1)S(1)}, bf16[48,1152]{1,0:T(8,128)(2,1)S(1)}, u32[]{:S(2)}, u32[]{:S(2)}) %collective-permute-start.8) | collective-permute-done | bytes 110624 | tf_op jit(solution)/shard_map/ppermute | solution.py:37
  40.7 10.7 %collective-permute-start.6 = (bf16[48,1152]{1,0:T(8,128)(2,1)S(1)}, bf16[48,1152]{1,0:T(8,128)(2,1)S(1)}, u32[]{:S(2)}, u32[]{:S(2)}) collective-permute-start(bf16[48,1152]{1,0:T(8,128)(2,1)S(1)} %dynamic_slice.21), channel_id=1, source_target_pairs={{0,1},{1,0},{2,3},{3,2},{4,5},{5,4},{6,7},{7,6},{8,9},{9,8},{10,11... | collective-permute-start | bytes 331784 | tf_op jit(solution)/shard_map/ppermute | solution.py:37
  68.1 4.5 collective-permute-done.11.rest_3_
  79.1 2.7 collective-permute-done.5
  82.9 4.7 %assemble.4 = bf16[768,2304]{1,0:T(8,128)(2,1)} custom-call(s32[3]{0:T(128)} %pad_add_fusion.spots, bf16[192,2304]{1,0:T(8,128)(2,1)} %own_ref.4, bf16[3,48,1152]{2,1,0:T(8,128)(2,1)} %copy-done.26, bf16[3,48,1152]{2,1,0:T(8,128)(2,1)} %collective-permute-done.9.rest_1_, bf16[3,48,1152]{2,1,0:T(8,128)(2,1)} %collective-permute-done.10.rest_2_, ...), custom_call_target="tpu_custom_call" | custom-call | bytes 7077888 | tf_op jit(solution)/shard_map/assemble/pallas_call | solution.py:363
  87.6 7.6 %add_convert_fusion.q_ref.k_ref.v_ref = bf16[1024,2304]{1,0:T(8,128)(2,1)} fusion(bf16[1024,768]{1,0:T(8,128)(2,1)S(1)} %fusion.14.x_ref, bf16[768,2304]{1,0:T(8,128)(2,1)} %assemble.4, f32[2304]{0:T(1024)S(1)} %pad_maximum_fusion.4), kind=kOutput, calls=%fused_computation.11 | convolution fusion | flops 3628597248 | bytes 9839616 | tf_op jit(solution)/shard_map/dot_general | solution.py:574
  95.2 4.9 %collective-permute-done.16.rest_1_ = bf16[3,64,1920]{2,1,0:T(8,128)(2,1)S(1)} collective-permute-done((bf16[3,64,1920]{2,1,0:T(8,128)(2,1)}, bf16[3,64,1920]{2,1,0:T(8,128)(2,1)S(1)}, u32[]{:S(2)}, u32[]{:S(2)}) %collective-permute-start.16) | collective-permute-done | bytes 737312 | tf_op jit(solution)/shard_map/ppermute | solution.py:37
  100.6 12.9 %attend_forward.2 = (bf16[1024,512]{1,0:T(8,128)(2,1)}, f32[8,8,1024]{2,1,0:T(8,128)}) custom-call(s32[1024,1]{1,0:T(8,128)} %copy.32.seg_col, s32[1,1024]{1,0:T(1,128)} %seg_row.7, bf16[1024,2304]{1,0:T(8,128)(2,1)} %add_convert_fusion.q_ref.k_ref.v_ref, bf16[1024,2304]{1,0:T(8,128)(2,1)} %add_convert_fusion.q_ref.k_ref.v_ref, ...), custom_call_target="tpu_custom_call" | custom-call | flops 12000000000 | bytes 4194304 | tf_op jit(solution)/shard_map/attend_forward/pallas_call | solution.py:92
  119.2 7.5 %attend_forward.3 = (bf16[1024,256]{1,0:T(8,128)(2,1)}, f32[4,8,1024]{2,1,0:T(8,128)}) custom-call(s32[1024,1]{1,0:T(8,128)} %copy.32.seg_col, s32[1,1024]{1,0:T(1,128)} %seg_row.7, bf16[1024,2304]{1,0:T(8,128)(2,1)} %add_convert_fusion.q_ref.k_ref.v_ref, bf16[1024,2304]{1,0:T(8,128)(2,1)} %add_convert_fusion.q_ref.k_ref.v_ref, ...), custom_call_target="tpu_custom_call" | custom-call | flops 6000000000 | bytes 2097152 | tf_op jit(solution)/shard_map/attend_forward/pallas_call | solution.py:92
  129.2 3.1 assemble.5
  132.3 2.8 fusion.53
  137.3 5.4 %assemble.6 = bf16[768,3072]{1,0:T(8,128)(2,1)} custom-call(s32[3]{0:T(128)} %pad_add_fusion.spots, bf16[192,3072]{1,0:T(8,128)(2,1)} %own_ref.6, bf16[3,64,1920]{2,1,0:T(8,128)(2,1)} %pad_maximum_fusion.rest_0_, bf16[3,64,1920]{2,1,0:T(8,128)(2,1)} %copy-done.18, bf16[3,64,1920]{2,1,0:T(8,128)(2,1)} %copy-done.19, bf16[3,64,1920]{2,1,0:T(8,128)(2,1)} %copy-done.21, ...), custom_call_target="tpu_custom_call" | custom-call | bytes 9437184 | tf_op jit(solution)/shard_map/assemble/pallas_call | solution.py:363
  142.7 14.1 %multiply_convert_fusion = (bf16[1024,3072]{1,0:T(8,128)(2,1)}, f32[1024,3072]{1,0:T(8,128)}) fusion(f32[3072]{0:T(1024)S(1)} %add.249, bf16[1024,768]{1,0:T(8,128)(2,1)S(1)} %add_convert_fusion.3.x_ref, bf16[768,3072]{1,0:T(8,128)(2,1)} %assemble.6), kind=kOutput, calls=%fused_computation.10 | convolution fusion | flops 4863295488 | bytes 25178112 | tf_op jit(solution)/shard_map/dot_general | solution.py:580
  156.9 8.1 %weight_grad.8 = bf16[4,4,192,384]{3,2,1,0:T(8,128)(2,1)} custom-call(s32[3]{0:T(128)} %pad_add_fusion.spots, bf16[1024,3072]{1,0:T(8,128)(2,1)} %get-tuple-element.106.x_ref, bf16[1024,768]{1,0:T(8,128)(2,1)} %y_ref.3), custom_call_target="tpu_custom_call" | custom-call | flops 2415919104 | bytes 4194304 | tf_op jit(solution)/shard_map/weight_grad/pallas_call | solution.py:236
  167.5 10.4 %collective-permute-done.23.rest_1_ = bf16[3,192,384]{2,1,0:T(8,128)(2,1)S(1)} collective-permute-done((bf16[3,192,384]{2,1,0:T(8,128)(2,1)S(1)}, bf16[3,192,384]{2,1,0:T(8,128)(2,1)S(1)}, u32[]{:S(2)}, u32[]{:S(2)}) %collective-permute-start.23) | collective-permute-done | bytes 442400 | tf_op jit(solution)/shard_map/ppermute | solution.py:37
  178.0 9.1 %collective-permute-done.25.rest_3_ = bf16[3,192,384]{2,1,0:T(8,128)(2,1)S(1)} collective-permute-done((bf16[3,192,384]{2,1,0:T(8,128)(2,1)}, bf16[3,192,384]{2,1,0:T(8,128)(2,1)S(1)}, u32[]{:S(2)}, u32[]{:S(2)}) %collective-permute-start.25) | collective-permute-done | bytes 442400 | tf_op jit(solution)/shard_map/ppermute | solution.py:37
  189.0 5.3 %assemble.7 = bf16[3072,768]{1,0:T(8,128)(2,1)} custom-call(s32[3]{0:T(128)} %pad_add_fusion.spots, bf16[768,768]{1,0:T(8,128)(2,1)} %own_ref.7, bf16[3,192,384]{2,1,0:T(8,128)(2,1)} %copy-done.24, bf16[3,192,384]{2,1,0:T(8,128)(2,1)} %copy-done.32, bf16[3,192,384]{2,1,0:T(8,128)(2,1)} %collective-permute-done.24.rest_2_, bf16[3,192,384]{2,1,0:T(8,128)(2,1)} %copy-done.33, ...), custom_call_target="tpu_custom_call" | custom-call | bytes 9437184 | tf_op jit(solution)/shard_map/assemble/pallas_call | solution.py:363
  194.3 9.4 %add_convert_fusion.2 = bf16[1024,768]{1,0:T(8,128)(2,1)} fusion(f32[1024,768]{1,0:T(8,128)S(1)} %copy-done.3, bf16[1024,3072]{1,0:T(8,128)(2,1)} %get-tuple-element.106.x_ref, bf16[3072,768]{1,0:T(8,128)(2,1)} %assemble.7, f32[768]{0:T(1024)S(1)} %add.255), kind=kOutput, calls=%fused_computation.37 | convolution fusion | flops 4834197504 | bytes 15731712 | tf_op jit(solution)/shard_map/dot_general | solution.py:610
  203.7 8.8 %weight_grad.9 = (bf16[2,4,192,384]{3,2,1,0:T(8,128)(2,1)}, bf16[2,4,192,384]{3,2,1,0:T(8,128)(2,1)}) custom-call(s32[3]{0:T(128)} %pad_add_fusion.spots, bf16[1024,3072]{1,0:T(8,128)(2,1)} %get-tuple-element.106.x_ref, bf16[1024,768]{1,0:T(8,128)(2,1)} %y_ref.3, bf16[4,4,192,384]{3,2,1,0:T(8,128)(2,1)} %collective-permute-done.30.rest_0_), custom_call_target="tpu_custom_call" | custom-call | flops 2415919104 | bytes 4194304 | tf_op jit(solution)/shard_map/weight_grad/pallas_call | solution.py:236
  213.1 15.2 %convert_reduce_fusion = (f32[3072]{0:T(1024)S(1)}, bf16[1024,3072]{1,0:T(8,128)(2,1)S(1)}) fusion(f32[1024,3072]{1,0:T(8,128)} %get-tuple-element.217, f32[3072]{0:T(1024)S(1)} %add.249, bf16[1024,768]{1,0:T(8,128)(2,1)S(1)} %copy-done.7, bf16[3072,768]{1,0:T(8,128)(2,1)} %assemble.7), kind=kOutput, calls=%fused_computation.9 | convolution fusion | flops 4904186880 | bytes 25190400 | tf_op jit(solution)/shard_map/td,fd->tf/dot_general | solution.py:619
  228.3 10.2 %multiply_reduce_fusion = (f32[768]{0:T(1024)S(1)}, f32[1024]{0:T(1024)S(1)}, f32[768]{0:T(1024)S(1)}, f32[1024,768]{1,0:T(8,128)S(1)}) fusion(f32[1024,768]{1,0:T(8,128)S(1)} %copy-done.3, f32[1024]{0:T(1024)S(1)} %fusion.43, f32[1024]{0:T(1024)S(1)} %broadcast_multiply_fusion, f32[768]{0:T(1024)S(1)} %mul.205, ...), kind=kOutput, calls=%fused_computation.31 | convolution fusion | flops 4838126592 | bytes 17323008 | tf_op jit(solution)/shard_map/tf,df->td/dot_general | solution.py:623
  244.2 9.8 %weight_grad.10 = bf16[4,4,48,1920]{3,2,1,0:T(8,128)(2,1)} custom-call(s32[3]{0:T(128)} %pad_add_fusion.spots, bf16[1024,768]{1,0:T(8,128)(2,1)} %copy-done.10, bf16[1024,3072]{1,0:T(8,128)(2,1)} %copy-done.6, bf16[1024,768]{1,0:T(8,128)(2,1)} %copy-done.12, bf16[1024,768]{1,0:T(8,128)(2,1)} %get-tuple-element.113.y2_ref), custom_call_target="tpu_custom_call" | custom-call | flops 3019898880 | bytes 4194304 | tf_op jit(solution)/shard_map/weight_grad/pallas_call | solution.py:236
  258.7 2.8 collective-permute-start.35
  261.5 2.6 convolution_convert_fusion.g_ref
  265.7 9.0 %collective-permute-done.35 = bf16[192,384]{1,0:T(8,128)(2,1)S(1)} collective-permute-done((bf16[192,384]{1,0:T(8,128)(2,1)S(1)}, bf16[192,384]{1,0:T(8,128)(2,1)S(1)}, u32[]{:S(2)}, u32[]{:S(2)}) %collective-permute-start.35) | collective-permute-done | bytes 147488 | tf_op jit(solution)/shard_map/ppermute | solution.py:37
  275.4 10.2 %weight_grad.11 = (bf16[2,4,48,1920]{3,2,1,0:T(8,128)(2,1)}, bf16[2,4,48,1920]{3,2,1,0:T(8,128)(2,1)}) custom-call(s32[3]{0:T(128)} %pad_add_fusion.spots, bf16[1024,768]{1,0:T(8,128)(2,1)} %copy-done.10, bf16[1024,3072]{1,0:T(8,128)(2,1)} %copy-done.6, bf16[1024,768]{1,0:T(8,128)(2,1)} %copy-done.12, bf16[1024,768]{1,0:T(8,128)(2,1)} %get-tuple-element.113.y2_ref, ...), custom_call_target="tpu_custom_call" | custom-call | flops 3019898880 | bytes 4194304 | tf_op jit(solution)/shard_map/weight_grad/pallas_call | solution.py:236
  287.2 24.0 %attend_backward.2 = (bf16[1024,512]{1,0:T(8,128)(2,1)}, bf16[1024,512]{1,0:T(8,128)(2,1)}, bf16[1024,512]{1,0:T(8,128)(2,1)}) custom-call(s32[1024,1]{1,0:T(8,128)} %copy.32.seg_col, s32[1,1024]{1,0:T(1,128)} %seg_row.7, bf16[1024,2304]{1,0:T(8,128)(2,1)} %add_convert_fusion.q_ref.k_ref.v_ref, bf16[1024,2304]{1,0:T(8,128)(2,1)} %add_convert_fusion.q_ref.k_ref.v_ref, ...), custom_call_target="tpu_custom_call" | custom-call | flops 24000000000 | bytes 8388608 | tf_op jit(solution)/shard_map/attend_backward/pallas_call | solution.py:158
  311.1 5.1 %weight_grad.12 = bf16[4,4,48,768]{3,2,1,0:T(8,128)(2,1)} custom-call(s32[3]{0:T(128)} %pad_add_fusion.spots, bf16[1024,768]{1,0:T(8,128)(2,1)} %copy-done.1, bf16[1024,512]{1,0:T(8,128)(2,1)} %get-tuple-element.143.q_ref, bf16[1024,512]{1,0:T(8,128)(2,1)} %get-tuple-element.145.k_ref, bf16[1024,512]{1,0:T(8,128)(2,1)} %get-tuple-element.147.v_ref), custom_call_target="tpu_custom_call" | custom-call | flops 1207959552 | bytes 4194304 | tf_op jit(solution)/shard_map/weight_grad/pallas_call | solution.py:236
  316.3 3.9 collective-permute-done.38
  323.1 13.4 %attend_backward.3 = (bf16[1024,256]{1,0:T(8,128)(2,1)}, bf16[1024,256]{1,0:T(8,128)(2,1)}, bf16[1024,256]{1,0:T(8,128)(2,1)}) custom-call(s32[1024,1]{1,0:T(8,128)} %copy.32.seg_col, s32[1,1024]{1,0:T(1,128)} %seg_row.7, bf16[1024,2304]{1,0:T(8,128)(2,1)} %add_convert_fusion.q_ref.k_ref.v_ref, bf16[1024,2304]{1,0:T(8,128)(2,1)} %add_convert_fusion.q_ref.k_ref.v_ref, ...), custom_call_target="tpu_custom_call" | custom-call | flops 12000000000 | bytes 4194304 | tf_op jit(solution)/shard_map/attend_backward/pallas_call | solution.py:158
  336.5 7.6 %collective-permute-done.39 = bf16[4,48,1920]{2,1,0:T(8,128)(2,1)S(1)} collective-permute-done((bf16[4,48,1920]{2,1,0:T(8,128)(2,1)S(1)}, bf16[4,48,1920]{2,1,0:T(8,128)(2,1)S(1)}, u32[]{:S(2)}, u32[]{:S(2)}) %collective-permute-start.39) | collective-permute-done | bytes 737312 | tf_op jit(solution)/shard_map/ppermute | solution.py:37
  347.3 2.8 collective-permute-start.63
  350.2 4.1 weight_grad.13
  354.3 5.4 %weight_grad.14 = (bf16[2,4,48,768]{3,2,1,0:T(8,128)(2,1)}, bf16[2,4,48,768]{3,2,1,0:T(8,128)(2,1)}) custom-call(s32[3]{0:T(128)} %pad_add_fusion.spots, bf16[1024,768]{1,0:T(8,128)(2,1)} %copy-done.1, bf16[1024,512]{1,0:T(8,128)(2,1)} %get-tuple-element.143.q_ref, bf16[1024,512]{1,0:T(8,128)(2,1)} %get-tuple-element.145.k_ref, ...), custom_call_target="tpu_custom_call" | custom-call | flops 1207959552 | bytes 4194304 | tf_op jit(solution)/shard_map/weight_grad/pallas_call | solution.py:236
  362.1 4.5 weight_grad.15
  369.4 4.1 fusion.46
  376.9 2.5 convert_reduce_fusion.2
  380.7 6.2 %collective-permute-done.51 = bf16[2,4,48,384]{3,2,1,0:T(8,128)(2,1)S(1)} collective-permute-done((bf16[2,4,48,384]{3,2,1,0:T(8,128)(2,1)S(1)}, bf16[2,4,48,384]{3,2,1,0:T(8,128)(2,1)S(1)}, u32[]{:S(2)}, u32[]{:S(2)}) %collective-permute-start.51) | collective-permute-done | bytes 294944 | tf_op jit(solution)/shard_map/ppermute | solution.py:37
  391.1 11.0 %collective-permute-done.42 = f32[12,768]{1,0:T(8,128)S(1)} collective-permute-done((f32[12,768]{1,0:T(8,128)S(1)}, f32[12,768]{1,0:T(8,128)S(1)}, u32[]{:S(2)}, u32[]{:S(2)}) %collective-permute-start.42) | collective-permute-done | bytes 36896 | tf_op jit(solution)/shard_map/ppermute | solution.py:37
  402.6 3.7 collective-permute-done.43
  416.7 2.8 settle.3
  423.6 2.7 collective-permute-start.48
  429.7 10.4 %all-gather = bf16[384,768]{1,0:T(8,128)(2,1)} all-gather(bf16[48,768]{1,0:T(8,128)(2,1)S(1)} %fusion.33), channel_id=2, replica_groups=mesh['rep'=8,'shard'=4] {'rep'}, dimensions={0}, use_global_device_ids=true | all-gather | bytes 663552 | tf_op jit(solution)/shard_map/all_gather | solution.py:603
  443.3 3.1 settle.2
  (346 shorter events, 101.0 us)
Async XLA Ops:
  7.2 409.5 %all-gather.8.cloned.1.call-start = ((), (), s32[]{:S(2)}) async-start(), calls=%async_computation.1 | async-start | bytes 1327104 | tf_op jit(solution)/shard_map/all_gather | solution.py:603
  15.3 42.5 %collective-permute-start = (bf16[64,1920]{1,0:T(8,128)(2,1)S(1)}, bf16[64,1920]{1,0:T(8,128)(2,1)S(1)}, u32[]{:S(2)}, u32[]{:S(2)}) collective-permute-start(bf16[64,1920]{1,0:T(8,128)(2,1)S(1)} %pad_maximum_fusion.3), channel_id=1, source_target_pairs={{0,1},{1,0},{2,3},{3,2},{4,5},{5,4},{6,7},{7,6},{8,9},{9,8},{10,11... | collective-permute-start | bytes 737288 | tf_op jit(solution)/shard_map/ppermute | solution.py:37
  18.4 39.5 %collective-permute-start.1 = (bf16[64,1920]{1,0:T(8,128)(2,1)S(1)}, bf16[64,1920]{1,0:T(8,128)(2,1)S(1)}, u32[]{:S(2)}, u32[]{:S(2)}) collective-permute-start(bf16[64,1920]{1,0:T(8,128)(2,1)S(1)} %pad_maximum_fusion.3), channel_id=1, source_target_pairs={{0,2},{1,3},{2,0},{3,1},{4,6},{5,7},{6,4},{7,5},{8,10},{9,11},{10,... | collective-permute-start | bytes 737288 | tf_op jit(solution)/shard_map/ppermute | solution.py:37
  21.0 36.9 %collective-permute-start.2 = (bf16[64,1920]{1,0:T(8,128)(2,1)S(1)}, bf16[64,1920]{1,0:T(8,128)(2,1)S(1)}, u32[]{:S(2)}, u32[]{:S(2)}) collective-permute-start(bf16[64,1920]{1,0:T(8,128)(2,1)S(1)} %pad_maximum_fusion.3), channel_id=1, source_target_pairs={{0,3},{1,2},{2,1},{3,0},{4,7},{5,6},{6,5},{7,4},{8,11},{9,10},{10,... | collective-permute-start | bytes 737288 | tf_op jit(solution)/shard_map/ppermute | solution.py:37
  21.9 18.8 %collective-permute-start.8 = (bf16[48,1152]{1,0:T(8,128)(2,1)S(1)}, bf16[48,1152]{1,0:T(8,128)(2,1)S(1)}, u32[]{:S(2)}, u32[]{:S(2)}) collective-permute-start(bf16[48,1152]{1,0:T(8,128)(2,1)S(1)} %dynamic_slice.21), channel_id=1, source_target_pairs={{0,3},{1,2},{2,1},{3,0},{4,7},{5,6},{6,5},{7,4},{8,11},{9,10},{10,... | collective-permute-start | bytes 331784 | tf_op jit(solution)/shard_map/ppermute | solution.py:37
  25.8 28.9 %collective-permute-start.7 = (bf16[48,1152]{1,0:T(8,128)(2,1)S(1)}, bf16[48,1152]{1,0:T(8,128)(2,1)S(1)}, u32[]{:S(2)}, u32[]{:S(2)}) collective-permute-start(bf16[48,1152]{1,0:T(8,128)(2,1)S(1)} %dynamic_slice.21), channel_id=1, source_target_pairs={{0,2},{1,3},{2,0},{3,1},{4,6},{5,7},{6,4},{7,5},{8,10},{9,11},{10,... | collective-permute-start | bytes 331784 | tf_op jit(solution)/shard_map/ppermute | solution.py:37
  40.7 14.0 %collective-permute-start.6 = (bf16[48,1152]{1,0:T(8,128)(2,1)S(1)}, bf16[48,1152]{1,0:T(8,128)(2,1)S(1)}, u32[]{:S(2)}, u32[]{:S(2)}) collective-permute-start(bf16[48,1152]{1,0:T(8,128)(2,1)S(1)} %dynamic_slice.21), channel_id=1, source_target_pairs={{0,1},{1,0},{2,3},{3,2},{4,5},{5,4},{6,7},{7,6},{8,9},{9,8},{10,11... | collective-permute-start | bytes 331784 | tf_op jit(solution)/shard_map/ppermute | solution.py:37
  56.3 11.2 %collective-permute-start.10 = (bf16[3,48,1152]{2,1,0:T(8,128)(2,1)S(1)}, bf16[3,48,1152]{2,1,0:T(8,128)(2,1)}, u32[]{:S(2)}, u32[]{:S(2)}) collective-permute-start(bf16[3,48,1152]{2,1,0:T(8,128)(2,1)S(1)} %pad_maximum_fusion.2.rest_0_), channel_id=1, source_target_pairs={{0,16},{4,20},{8,24},{12,28},{16,0},{20,4},{24,8},{28,12},{1,17},{... | collective-permute-start | bytes 995336 | tf_op jit(solution)/shard_map/ppermute | solution.py:37
  57.9 23.9 %collective-permute-start.12 = (bf16[3,48,1152]{2,1,0:T(8,128)(2,1)S(1)}, bf16[3,48,1152]{2,1,0:T(8,128)(2,1)}, u32[]{:S(2)}, u32[]{:S(2)}) collective-permute-start(bf16[3,48,1152]{2,1,0:T(8,128)(2,1)S(1)} %pad_maximum_fusion.2.rest_0_), channel_id=1, source_target_pairs={{0,4},{4,0},{8,12},{12,8},{16,20},{20,16},{24,28},{28,24},{1,5},{5... | collective-permute-start | bytes 995336 | tf_op jit(solution)/shard_map/ppermute | solution.py:37
  57.9 9.7 %collective-permute-start.3 = (bf16[192,384]{1,0:T(8,128)(2,1)}, bf16[192,384]{1,0:T(8,128)(2,1)}, u32[]{:S(2)}, u32[]{:S(2)}) collective-permute-start(bf16[192,384]{1,0:T(8,128)(2,1)} %dynamic_slice.18), channel_id=1, source_target_pairs={{0,1},{1,0},{2,3},{3,2},{4,5},{5,4},{6,7},{7,6},{8,9},{9,8},{10,11... | collective-permute-start | bytes 442376 | tf_op jit(solution)/shard_map/ppermute | solution.py:37
  59.5 13.8 %collective-permute-start.4 = (bf16[192,384]{1,0:T(8,128)(2,1)}, bf16[192,384]{1,0:T(8,128)(2,1)}, u32[]{:S(2)}, u32[]{:S(2)}) collective-permute-start(bf16[192,384]{1,0:T(8,128)(2,1)} %dynamic_slice.18), channel_id=1, source_target_pairs={{0,2},{1,3},{2,0},{3,1},{4,6},{5,7},{6,4},{7,5},{8,10},{9,11},{10,... | collective-permute-start | bytes 442376 | tf_op jit(solution)/shard_map/ppermute | solution.py:37
  62.6 10.0 %collective-permute-start.11 = (bf16[3,48,1152]{2,1,0:T(8,128)(2,1)}, bf16[3,48,1152]{2,1,0:T(8,128)(2,1)}, u32[]{:S(2)}, u32[]{:S(2)}) collective-permute-start(bf16[3,48,1152]{2,1,0:T(8,128)(2,1)} %collective-permute-done.9.rest_1_), channel_id=1, source_target_pairs={{0,16},{4,20},{8,24},{12,28},{16,0},{20,4},{24,8},{28,12},{1,17},{... | collective-permute-start | bytes 995336 | tf_op jit(solution)/shard_map/ppermute | solution.py:37
  67.6 14.2 %collective-permute-start.13 = (bf16[3,48,1152]{2,1,0:T(8,128)(2,1)}, bf16[3,48,1152]{2,1,0:T(8,128)(2,1)}, u32[]{:S(2)}, u32[]{:S(2)}) collective-permute-start(bf16[3,48,1152]{2,1,0:T(8,128)(2,1)} %collective-permute-done.9.rest_1_), channel_id=1, source_target_pairs={{0,4},{4,0},{8,12},{12,8},{16,20},{20,16},{24,28},{28,24},{1,5},{5... | collective-permute-start | bytes 995336 | tf_op jit(solution)/shard_map/ppermute | solution.py:37
  67.6 14.2 %collective-permute-start.14 = (bf16[3,48,1152]{2,1,0:T(8,128)(2,1)}, bf16[3,48,1152]{2,1,0:T(8,128)(2,1)}, u32[]{:S(2)}, u32[]{:S(2)}) collective-permute-start(bf16[3,48,1152]{2,1,0:T(8,128)(2,1)} %collective-permute-done.10.rest_2_), channel_id=1, source_target_pairs={{0,4},{4,0},{8,12},{12,8},{16,20},{20,16},{24,28},{28,24},{1,5},{5... | collective-permute-start | bytes 995336 | tf_op jit(solution)/shard_map/ppermute | solution.py:37
  81.8 18.3 %collective-permute-start.16 = (bf16[3,64,1920]{2,1,0:T(8,128)(2,1)}, bf16[3,64,1920]{2,1,0:T(8,128)(2,1)S(1)}, u32[]{:S(2)}, u32[]{:S(2)}) collective-permute-start(bf16[3,64,1920]{2,1,0:T(8,128)(2,1)} %pad_maximum_fusion.rest_0_), channel_id=1, source_target_pairs={{0,8},{4,12},{8,0},{12,4},{16,24},{20,28},{24,16},{28,20},{1,9},{5... | collective-permute-start | bytes 2211848 | tf_op jit(solution)/shard_map/ppermute | solution.py:37
  82.4 32.5 %collective-permute-start.17 = (bf16[3,64,1920]{2,1,0:T(8,128)(2,1)}, bf16[3,64,1920]{2,1,0:T(8,128)(2,1)S(1)}, u32[]{:S(2)}, u32[]{:S(2)}) collective-permute-start(bf16[3,64,1920]{2,1,0:T(8,128)(2,1)} %pad_maximum_fusion.rest_0_), channel_id=1, source_target_pairs={{0,16},{4,20},{8,24},{12,28},{16,0},{20,4},{24,8},{28,12},{1,17},{... | collective-permute-start | bytes 2211848 | tf_op jit(solution)/shard_map/ppermute | solution.py:37
  82.9 44.9 %collective-permute-start.19 = (bf16[3,64,1920]{2,1,0:T(8,128)(2,1)}, bf16[3,64,1920]{2,1,0:T(8,128)(2,1)S(1)}, u32[]{:S(2)}, u32[]{:S(2)}) collective-permute-start(bf16[3,64,1920]{2,1,0:T(8,128)(2,1)} %pad_maximum_fusion.rest_0_), channel_id=1, source_target_pairs={{0,4},{4,0},{8,12},{12,8},{16,20},{20,16},{24,28},{28,24},{1,5},{5... | collective-permute-start | bytes 2211848 | tf_op jit(solution)/shard_map/ppermute | solution.py:37
  100.1 17.2 %collective-permute-start.18 = (bf16[3,64,1920]{2,1,0:T(8,128)(2,1)S(1)}, bf16[3,64,1920]{2,1,0:T(8,128)(2,1)S(1)}, u32[]{:S(2)}, u32[]{:S(2)}) collective-permute-start(bf16[3,64,1920]{2,1,0:T(8,128)(2,1)S(1)} %collective-permute-done.16.rest_1_), channel_id=1, source_target_pairs={{0,16},{4,20},{8,24},{12,28},{16,0},{20,4},{24,8},{28,12},{1,17},{... | collective-permute-start | bytes 2211848 | tf_op jit(solution)/shard_map/ppermute | solution.py:37
  114.8 13.0 %collective-permute-start.20 = (bf16[3,64,1920]{2,1,0:T(8,128)(2,1)S(1)}, bf16[3,64,1920]{2,1,0:T(8,128)(2,1)S(1)}, u32[]{:S(2)}, u32[]{:S(2)}) collective-permute-start(bf16[3,64,1920]{2,1,0:T(8,128)(2,1)S(1)} %collective-permute-done.16.rest_1_), channel_id=1, source_target_pairs={{0,4},{4,0},{8,12},{12,8},{16,20},{20,16},{24,28},{28,24},{1,5},{5... | collective-permute-start | bytes 2211848 | tf_op jit(solution)/shard_map/ppermute | solution.py:37
  114.9 13.0 %collective-permute-start.21 = (bf16[3,64,1920]{2,1,0:T(8,128)(2,1)S(1)}, bf16[3,64,1920]{2,1,0:T(8,128)(2,1)S(1)}, u32[]{:S(2)}, u32[]{:S(2)}) collective-permute-start(bf16[3,64,1920]{2,1,0:T(8,128)(2,1)S(1)} %collective-permute-done.17.rest_2_), channel_id=1, source_target_pairs={{0,4},{4,0},{8,12},{12,8},{16,20},{20,16},{24,28},{28,24},{1,5},{5... | collective-permute-start | bytes 2211848 | tf_op jit(solution)/shard_map/ppermute | solution.py:37
  117.3 10.6 %collective-permute-start.22 = (bf16[3,64,1920]{2,1,0:T(8,128)(2,1)S(1)}, bf16[3,64,1920]{2,1,0:T(8,128)(2,1)}, u32[]{:S(2)}, u32[]{:S(2)}) collective-permute-start(bf16[3,64,1920]{2,1,0:T(8,128)(2,1)S(1)} %collective-permute-done.18.rest_3_), channel_id=1, source_target_pairs={{0,4},{4,0},{8,12},{12,8},{16,20},{20,16},{24,28},{28,24},{1,5},{5... | collective-permute-start | bytes 2211848 | tf_op jit(solution)/shard_map/ppermute | solution.py:37
  118.7 46.9 %collective-permute-start.24 = (bf16[3,192,384]{2,1,0:T(8,128)(2,1)S(1)}, bf16[3,192,384]{2,1,0:T(8,128)(2,1)}, u32[]{:S(2)}, u32[]{:S(2)}) collective-permute-start(bf16[3,192,384]{2,1,0:T(8,128)(2,1)S(1)} %pad_maximum_fusion.1.rest_0_), channel_id=1, source_target_pairs={{0,16},{4,20},{8,24},{12,28},{16,0},{20,4},{24,8},{28,12},{1,17},{... | collective-permute-start | bytes 1327112 | tf_op jit(solution)/shard_map/ppermute | solution.py:37
  165.0 38.7 %collective-permute-start.30 = (bf16[4,4,192,384]{3,2,1,0:T(8,128)(2,1)}, bf16[4,4,192,384]{3,2,1,0:T(8,128)(2,1)}, u32[]{:S(2)}, u32[]{:S(2)}) collective-permute-start(bf16[4,4,192,384]{3,2,1,0:T(8,128)(2,1)} %weight_grad.8), channel_id=1, source_target_pairs={{0,4},{4,0},{8,12},{12,8},{16,20},{20,16},{24,28},{28,24},{1,5},{5... | collective-permute-start | bytes 7077896 | tf_op jit(solution)/shard_map/ppermute | solution.py:37
  165.0 13.0 %collective-permute-start.23 = (bf16[3,192,384]{2,1,0:T(8,128)(2,1)S(1)}, bf16[3,192,384]{2,1,0:T(8,128)(2,1)S(1)}, u32[]{:S(2)}, u32[]{:S(2)}) collective-permute-start(bf16[3,192,384]{2,1,0:T(8,128)(2,1)S(1)} %pad_maximum_fusion.1.rest_0_), channel_id=1, source_target_pairs={{0,8},{4,12},{8,0},{12,4},{16,24},{20,28},{24,16},{28,20},{1,9},{5... | collective-permute-start | bytes 1327112 | tf_op jit(solution)/shard_map/ppermute | solution.py:37
  165.5 21.5 %collective-permute-start.25 = (bf16[3,192,384]{2,1,0:T(8,128)(2,1)}, bf16[3,192,384]{2,1,0:T(8,128)(2,1)S(1)}, u32[]{:S(2)}, u32[]{:S(2)}) collective-permute-start(bf16[3,192,384]{2,1,0:T(8,128)(2,1)} %collective-permute-done.24.rest_2_), channel_id=1, source_target_pairs={{0,8},{4,12},{8,0},{12,4},{16,24},{20,28},{24,16},{28,20},{1,9},{5... | collective-permute-start | bytes 1327112 | tf_op jit(solution)/shard_map/ppermute | solution.py:37
  167.0 20.1 %collective-permute-start.26 = (bf16[3,192,384]{2,1,0:T(8,128)(2,1)S(1)}, bf16[3,192,384]{2,1,0:T(8,128)(2,1)S(1)}, u32[]{:S(2)}, u32[]{:S(2)}) collective-permute-start(bf16[3,192,384]{2,1,0:T(8,128)(2,1)S(1)} %pad_maximum_fusion.1.rest_0_), channel_id=1, source_target_pairs={{0,4},{4,0},{8,12},{12,8},{16,20},{20,16},{24,28},{28,24},{1,5},{5... | collective-permute-start | bytes 1327112 | tf_op jit(solution)/shard_map/ppermute | solution.py:37
  167.0 20.1 %collective-permute-start.28 = (bf16[3,192,384]{2,1,0:T(8,128)(2,1)}, bf16[3,192,384]{2,1,0:T(8,128)(2,1)}, u32[]{:S(2)}, u32[]{:S(2)}) collective-permute-start(bf16[3,192,384]{2,1,0:T(8,128)(2,1)} %collective-permute-done.24.rest_2_), channel_id=1, source_target_pairs={{0,4},{4,0},{8,12},{12,8},{16,20},{20,16},{24,28},{28,24},{1,5},{5... | collective-permute-start | bytes 1327112 | tf_op jit(solution)/shard_map/ppermute | solution.py:37
  212.5 28.2 %collective-permute-start.31 = (bf16[2,4,192,384]{3,2,1,0:T(8,128)(2,1)}, bf16[2,4,192,384]{3,2,1,0:T(8,128)(2,1)S(1)}, u32[]{:S(2)}, u32[]{:S(2)}) collective-permute-start(bf16[2,4,192,384]{3,2,1,0:T(8,128)(2,1)} %get-tuple-element.112), channel_id=1, source_target_pairs={{0,8},{4,12},{8,0},{12,4},{16,24},{20,28},{24,16},{28,20},{1,9},{5... | collective-permute-start | bytes 3538952 | tf_op jit(solution)/shard_map/ppermute | solution.py:37
  240.9 14.7 %collective-permute-start.32 = (bf16[4,192,384]{2,1,0:T(8,128)(2,1)S(1)}, bf16[4,192,384]{2,1,0:T(8,128)(2,1)}, u32[]{:S(2)}, u32[]{:S(2)}) collective-permute-start(bf16[4,192,384]{2,1,0:T(8,128)(2,1)S(1)} %fusion.21), channel_id=1, source_target_pairs={{0,16},{4,20},{8,24},{12,28},{16,0},{20,4},{24,8},{28,12},{1,17},{... | collective-permute-start | bytes 1769480 | tf_op jit(solution)/shard_map/ppermute | solution.py:37
  256.9 18.5 %collective-permute-start.33 = (bf16[4,4,48,1920]{3,2,1,0:T(8,128)(2,1)}, bf16[4,4,48,1920]{3,2,1,0:T(8,128)(2,1)}, u32[]{:S(2)}, u32[]{:S(2)}) collective-permute-start(bf16[4,4,48,1920]{3,2,1,0:T(8,128)(2,1)} %weight_grad.10), channel_id=1, source_target_pairs={{0,4},{4,0},{8,12},{12,8},{16,20},{20,16},{24,28},{28,24},{1,5},{5... | collective-permute-start | bytes 8847368 | tf_op jit(solution)/shard_map/ppermute | solution.py:37
  258.7 16.0 %collective-permute-start.35 = (bf16[192,384]{1,0:T(8,128)(2,1)S(1)}, bf16[192,384]{1,0:T(8,128)(2,1)S(1)}, u32[]{:S(2)}, u32[]{:S(2)}) collective-permute-start(bf16[192,384]{1,0:T(8,128)(2,1)S(1)} %get-tuple-element.183), channel_id=1, source_target_pairs={{0,2},{1,3},{2,0},{3,1},{4,6},{5,7},{6,4},{7,5},{8,10},{9,11},{10,... | collective-permute-start | bytes 442376 | tf_op jit(solution)/shard_map/ppermute | solution.py:37
  261.4 13.2 %collective-permute-start.34 = (bf16[192,384]{1,0:T(8,128)(2,1)S(1)}, bf16[192,384]{1,0:T(8,128)(2,1)S(1)}, u32[]{:S(2)}, u32[]{:S(2)}) collective-permute-start(bf16[192,384]{1,0:T(8,128)(2,1)S(1)} %get-tuple-element.181), channel_id=1, source_target_pairs={{0,1},{1,0},{2,3},{3,2},{4,5},{5,4},{6,7},{7,6},{8,9},{9,8},{10,11... | collective-permute-start | bytes 442376 | tf_op jit(solution)/shard_map/ppermute | solution.py:37
  285.6 34.6 %collective-permute-start.38 = (bf16[2,4,48,1920]{3,2,1,0:T(8,128)(2,1)}, bf16[2,4,48,1920]{3,2,1,0:T(8,128)(2,1)}, u32[]{:S(2)}, u32[]{:S(2)}) collective-permute-start(bf16[2,4,48,1920]{3,2,1,0:T(8,128)(2,1)} %get-tuple-element.135), channel_id=1, source_target_pairs={{0,16},{4,20},{8,24},{12,28},{16,0},{20,4},{24,8},{28,12},{1,17},{... | collective-permute-start | bytes 4423688 | tf_op jit(solution)/shard_map/ppermute | solution.py:37
  316.2 29.3 %collective-permute-start.37 = (bf16[4,4,48,768]{3,2,1,0:T(8,128)(2,1)}, bf16[4,4,48,768]{3,2,1,0:T(8,128)(2,1)}, u32[]{:S(2)}, u32[]{:S(2)}) collective-permute-start(bf16[4,4,48,768]{3,2,1,0:T(8,128)(2,1)} %weight_grad.12), channel_id=1, source_target_pairs={{0,4},{4,0},{8,12},{12,8},{16,20},{20,16},{24,28},{28,24},{1,5},{5... | collective-permute-start | bytes 3538952 | tf_op jit(solution)/shard_map/ppermute | solution.py:37
  316.2 127.1 %all-gather.6.cloned.1.call-start = ((), (), s32[]{:S(2)}) async-start(), calls=%async_computation | async-start | bytes 1658880 | tf_op jit(solution)/shard_map/all_gather | solution.py:603
  321.8 22.4 %collective-permute-start.39 = (bf16[4,48,1920]{2,1,0:T(8,128)(2,1)S(1)}, bf16[4,48,1920]{2,1,0:T(8,128)(2,1)S(1)}, u32[]{:S(2)}, u32[]{:S(2)}) collective-permute-start(bf16[4,48,1920]{2,1,0:T(8,128)(2,1)S(1)} %fusion.20), channel_id=1, source_target_pairs={{0,8},{4,12},{8,0},{12,4},{16,24},{20,28},{24,16},{28,20},{1,9},{5... | collective-permute-start | bytes 2211848 | tf_op jit(solution)/shard_map/ppermute | solution.py:37
  345.7 14.1 %collective-permute-start.65 = (bf16[48,1920]{1,0:T(8,128)(2,1)S(1)}, bf16[48,1920]{1,0:T(8,128)(2,1)S(1)}, u32[]{:S(2)}, u32[]{:S(2)}) collective-permute-start(bf16[48,1920]{1,0:T(8,128)(2,1)S(1)} %get-tuple-element.175), channel_id=1, source_target_pairs={{0,3},{1,2},{2,1},{3,0},{4,7},{5,6},{6,5},{7,4},{8,11},{9,10},{10,... | collective-permute-start | bytes 552968 | tf_op jit(solution)/shard_map/ppermute | solution.py:37
  347.3 14.0 %collective-permute-start.64 = (bf16[48,1920]{1,0:T(8,128)(2,1)S(1)}, bf16[48,1920]{1,0:T(8,128)(2,1)S(1)}, u32[]{:S(2)}, u32[]{:S(2)}) collective-permute-start(bf16[48,1920]{1,0:T(8,128)(2,1)S(1)} %get-tuple-element.176), channel_id=1, source_target_pairs={{0,2},{1,3},{2,0},{3,1},{4,6},{5,7},{6,4},{7,5},{8,10},{9,11},{10,... | collective-permute-start | bytes 552968 | tf_op jit(solution)/shard_map/ppermute | solution.py:37
  347.3 14.0 %collective-permute-start.63 = (bf16[48,1920]{1,0:T(8,128)(2,1)S(1)}, bf16[48,1920]{1,0:T(8,128)(2,1)S(1)}, u32[]{:S(2)}, u32[]{:S(2)}) collective-permute-start(bf16[48,1920]{1,0:T(8,128)(2,1)S(1)} %get-tuple-element.174), channel_id=1, source_target_pairs={{0,1},{1,0},{2,3},{3,2},{4,5},{5,4},{6,7},{7,6},{8,9},{9,8},{10,11... | collective-permute-start | bytes 552968 | tf_op jit(solution)/shard_map/ppermute | solution.py:37
  375.5 11.4 %collective-permute-start.51 = (bf16[2,4,48,384]{3,2,1,0:T(8,128)(2,1)S(1)}, bf16[2,4,48,384]{3,2,1,0:T(8,128)(2,1)S(1)}, u32[]{:S(2)}, u32[]{:S(2)}) collective-permute-start(bf16[2,4,48,384]{3,2,1,0:T(8,128)(2,1)S(1)} %copy-done.60), channel_id=1, source_target_pairs={{0,16},{4,20},{8,24},{12,28},{16,0},{20,4},{24,8},{28,12},{1,17},{... | collective-permute-start | bytes 884744 | tf_op jit(solution)/shard_map/ppermute | solution.py:37
  379.4 32.3 %collective-permute-start.46 = (bf16[2,4,48,768]{3,2,1,0:T(8,128)(2,1)}, bf16[2,4,48,768]{3,2,1,0:T(8,128)(2,1)S(1)}, u32[]{:S(2)}, u32[]{:S(2)}) collective-permute-start(bf16[2,4,48,768]{3,2,1,0:T(8,128)(2,1)} %get-tuple-element.150), channel_id=1, source_target_pairs={{0,8},{4,12},{8,0},{12,4},{16,24},{20,28},{24,16},{28,20},{1,9},{5... | collective-permute-start | bytes 1769480 | tf_op jit(solution)/shard_map/ppermute | solution.py:37
  387.0 19.3 %collective-permute-start.52 = (bf16[4,48,384]{2,1,0:T(8,128)(2,1)S(1)}, bf16[4,48,384]{2,1,0:T(8,128)(2,1)S(1)}, u32[]{:S(2)}, u32[]{:S(2)}) collective-permute-start(bf16[4,48,384]{2,1,0:T(8,128)(2,1)S(1)} %fusion.29), channel_id=1, source_target_pairs={{0,8},{4,12},{8,0},{12,4},{16,24},{20,28},{24,16},{28,20},{1,9},{5... | collective-permute-start | bytes 442376 | tf_op jit(solution)/shard_map/ppermute | solution.py:37
  390.8 11.3 %collective-permute-start.42 = (f32[12,768]{1,0:T(8,128)S(1)}, f32[12,768]{1,0:T(8,128)S(1)}, u32[]{:S(2)}, u32[]{:S(2)}) collective-permute-start(f32[12,768]{1,0:T(8,128)S(1)} %add.271), channel_id=1, source_target_pairs={{0,8},{4,12},{8,0},{12,4},{16,24},{20,28},{24,16},{28,20},{1,9},{5... | collective-permute-start | bytes 110600 | tf_op jit(solution)/shard_map/ppermute | solution.py:37
  411.8 9.8 %collective-permute-start.47 = (bf16[4,48,768]{2,1,0:T(8,128)(2,1)S(1)}, bf16[4,48,768]{2,1,0:T(8,128)(2,1)S(1)}, u32[]{:S(2)}, u32[]{:S(2)}) collective-permute-start(bf16[4,48,768]{2,1,0:T(8,128)(2,1)S(1)} %fusion.25), channel_id=1, source_target_pairs={{0,16},{4,20},{8,24},{12,28},{16,0},{20,4},{24,8},{28,12},{1,17},{... | collective-permute-start | bytes 884744 | tf_op jit(solution)/shard_map/ppermute | solution.py:37
  427.7 12.5 %collective-permute-start.59 = (bf16[48,384]{1,0:T(8,128)(2,1)S(1)}, bf16[48,384]{1,0:T(8,128)(2,1)S(1)}, u32[]{:S(2)}, u32[]{:S(2)}) collective-permute-start(bf16[48,384]{1,0:T(8,128)(2,1)S(1)} %fusion.37.rest_0_), channel_id=1, source_target_pairs={{0,4},{4,0},{8,12},{12,8},{16,20},{20,16},{24,28},{28,24},{1,5},{5... | collective-permute-start | bytes 110600 | tf_op jit(solution)/shard_map/ppermute | solution.py:37
  427.7 12.4 %collective-permute-start.60 = (bf16[48,384]{1,0:T(8,128)(2,1)S(1)}, bf16[48,384]{1,0:T(8,128)(2,1)S(1)}, u32[]{:S(2)}, u32[]{:S(2)}) collective-permute-start(bf16[48,384]{1,0:T(8,128)(2,1)S(1)} %collective-permute-done.56.rest_1_), channel_id=1, source_target_pairs={{0,4},{4,0},{8,12},{12,8},{16,20},{20,16},{24,28},{28,24},{1,5},{5... | collective-permute-start | bytes 110600 | tf_op jit(solution)/shard_map/ppermute | solution.py:37
  428.2 12.0 %collective-permute-start.61 = (bf16[48,384]{1,0:T(8,128)(2,1)S(1)}, bf16[48,384]{1,0:T(8,128)(2,1)S(1)}, u32[]{:S(2)}, u32[]{:S(2)}) collective-permute-start(bf16[48,384]{1,0:T(8,128)(2,1)S(1)} %collective-permute-done.57.rest_2_), channel_id=1, source_target_pairs={{0,4},{4,0},{8,12},{12,8},{16,20},{20,16},{24,28},{28,24},{1,5},{5... | collective-permute-start | bytes 110600 | tf_op jit(solution)/shard_map/ppermute | solution.py:37
  429.6 10.5 %collective-permute-start.62 = (bf16[48,384]{1,0:T(8,128)(2,1)S(1)}, bf16[48,384]{1,0:T(8,128)(2,1)S(1)}, u32[]{:S(2)}, u32[]{:S(2)}) collective-permute-start(bf16[48,384]{1,0:T(8,128)(2,1)S(1)} %collective-permute-done.58.rest_3_), channel_id=1, source_target_pairs={{0,4},{4,0},{8,12},{12,8},{16,20},{20,16},{24,28},{28,24},{1,5},{5... | collective-permute-start | bytes 110600 | tf_op jit(solution)/shard_map/ppermute | solution.py:37
  (81 other events, 708.4 us)
Sparse Core Ops, SparseCore 0:
  316.3 26.9 all-gather.7
  362.2 28.4 all-gather.5

commit v2 on v1

v2 whole, which is shorter than its diff:
```python
import functools
import math

import jax
import jax.numpy as jnp
from jax import lax
from jax.experimental import pallas as pl
from jax.experimental.pallas import tpu as pltpu
from jax.sharding import PartitionSpec as P

HEADS = 12
HEAD_DIM = 64
LOG2E = math.log2(math.e)
NEG = -1e30
BF16 = jnp.bfloat16
F32 = jnp.float32
VMEM_LIMIT = 56 << 20
SMALL_COST = pl.CostEstimate(flops=10**6, bytes_accessed=10**5, transcendentals=0)


def dot_nt(a, b):
    return lax.dot_general(a, b, (((1,), (1,)), ((), ())), preferred_element_type=F32)


def dot_nn(a, b):
    return lax.dot_general(a, b, (((1,), (0,)), ((), ())), preferred_element_type=F32)


def dot_tn(a, b):
    return lax.dot_general(a, b, (((0,), (0,)), ((), ())), preferred_element_type=F32)


def params():
    return pltpu.CompilerParams(vmem_limit_bytes=VMEM_LIMIT)


def swap(value, axis, size, mask):
    return lax.ppermute(value, axis, [(i, i ^ mask) for i in range(size)])


def allowed_block(seg_col, seg_row, block, rows):
    keys = (block + 1) * rows
    same = seg_col[:keys, :] == seg_row[:, block * rows : keys]
    causal = lax.broadcasted_iota(jnp.int32, (rows, rows), 0) <= lax.broadcasted_iota(
        jnp.int32, (rows, rows), 1
    )
    if block == 0:
        return same & causal
    return jnp.concatenate([same[: keys - rows], same[keys - rows :] & causal], axis=0)


def attend_kernel(rows, seg_col, seg_row, q_ref, k_ref, v_ref, o_ref, lse_ref):
    length = q_ref.shape[0]
    lane = lax.broadcasted_iota(jnp.int32, (1, 128), 1)
    scale = HEAD_DIM ** (-0.5) * LOG2E
    v_turned = v_ref[...].T
    for block in range(length // rows):
        keys = (block + 1) * rows
        here = slice(block * rows, keys)
        q = q_ref[here, :]
        k = k_ref[:keys, :]
        allowed = allowed_block(seg_col, seg_row, block, rows)
        parts = []
        for head in range(2):
            mine = (lane < 64) if head == 0 else (lane >= 64)
            q_head = jnp.where(mine, q, jnp.zeros_like(q))
            scores = jnp.where(allowed, dot_nt(k, q_head), NEG)
            highest = jnp.max(scores, axis=0, keepdims=True)
            expo = jnp.exp2((scores - highest) * scale)
            summed = jnp.sum(expo, axis=0, keepdims=True)
            v_head = v_turned[head * 64 : (head + 1) * 64, :keys]
            parts.append(dot_nn(v_head, expo.astype(BF16)) * (1.0 / summed))
            lse_ref[head, :, here] = jnp.broadcast_to(
                highest * scale + jnp.log2(summed), (8, rows)
            )
        o_ref[here, :] = jnp.concatenate(parts, axis=0).T.astype(BF16)


def head_specs(length, start):
    groups = HEADS // 2
    return [
        pl.BlockSpec((length, 1), lambda h: (0, 0)),
        pl.BlockSpec((1, length), lambda h: (0, 0)),
        pl.BlockSpec((length, 128), lambda h: (0, start + h)),
        pl.BlockSpec((length, 128), lambda h: (0, groups + start + h)),
        pl.BlockSpec((length, 128), lambda h: (0, 2 * groups + start + h)),
    ]


def attend_forward(qkv, segment, start, count):
    length = qkv.shape[0]
    rows = length // 2
    return pl.pallas_call(
        functools.partial(attend_kernel, rows),
        grid=(count,),
        in_specs=head_specs(length, start),
        out_specs=[
            pl.BlockSpec((length, 128), lambda h: (0, h)),
            pl.BlockSpec((2, 8, length), lambda h: (h, 0, 0)),
        ],
        out_shape=[
            jax.ShapeDtypeStruct((length, 128 * count), BF16),
            jax.ShapeDtypeStruct((2 * count, 8, length), F32),
        ],
        compiler_params=params(),
        cost_estimate=SMALL_COST,
        name="attend_forward",
    )(segment.reshape(length, 1), segment.reshape(1, length), qkv, qkv, qkv)


def attend_back_kernel(
    rows, seg_col, seg_row, q_ref, k_ref, v_ref, g_ref, lse_ref, dq_ref, dk_ref, dv_ref, sums_ref, dk_sum, dv_sum
):
    length = q_ref.shape[0]
    lane = lax.broadcasted_iota(jnp.int32, (1, 128), 1)
    scale = HEAD_DIM ** (-0.5) * LOG2E
    blocks = length // rows
    for block in reversed(range(blocks)):
        keys = (block + 1) * rows
        here = slice(block * rows, keys)
        q = q_ref[here, :]
        g = g_ref[here, :]
        k = k_ref[:keys, :]
        v = v_ref[:keys, :]
        allowed = allowed_block(seg_col, seg_row, block, rows)
        dq = dk = dv = None
        for head in range(2):
            mine = (lane < 64) if head == 0 else (lane >= 64)
            q_head = jnp.where(mine, q, jnp.zeros_like(q))
            g_head = jnp.where(mine, g, jnp.zeros_like(g))
            scores = dot_nt(k, q_head) * scale - lse_ref[head, 0:1, here]
            probs = jnp.exp2(jnp.where(allowed, scores, NEG))
            grad_probs = dot_nt(v, g_head)
            inner = jnp.sum(probs * grad_probs, axis=0, keepdims=True)
            grad_scores = (probs * (grad_probs - inner)).astype(BF16)
            dv_head = dot_nn(probs.astype(BF16), g_head)
            dk_head = dot_nn(grad_scores, q_head)
            dq_head = dot_tn(grad_scores, k)
            if head == 0:
                dq, dk, dv = dq_head, dk_head, dv_head
            else:
                dq, dk, dv = jnp.where(lane < 64, dq, dq_head), dk + dk_head, dv + dv_head
        dq_ref[here, :] = (dq * HEAD_DIM ** (-0.5)).astype(BF16)
        if block == blocks - 1:
            dk_sum[...] = dk
            dv_sum[...] = dv
        else:
            dk_sum[:keys, :] += dk
            dv_sum[:keys, :] += dv
    dk_ref[...] = (dk_sum[...] * HEAD_DIM ** (-0.5)).astype(BF16)
    dv_ref[...] = dv_sum[...].astype(BF16)
    sums_ref[0:1, :] = jnp.sum(dq_ref[...].astype(F32), axis=0, keepdims=True)
    sums_ref[1:2, :] = jnp.sum(dv_ref[...].astype(F32), axis=0, keepdims=True)
    sums_ref[2:8, :] = jnp.zeros((6, 128), F32)


def attend_backward(qkv, segment, grad, lse, start, count):
    length = qkv.shape[0]
    rows = length // 2
    return pl.pallas_call(
        functools.partial(attend_back_kernel, rows),
        grid=(count,),
        in_specs=head_specs(length, start)
        + [
            pl.BlockSpec((length, 128), lambda h: (0, start + h)),
            pl.BlockSpec((2, 8, length), lambda h: (h, 0, 0)),
        ],
        out_specs=[pl.BlockSpec((length, 128), lambda h: (0, h))] * 3
        + [pl.BlockSpec((8, 128), lambda h: (0, h))],
        out_shape=[jax.ShapeDtypeStruct((length, 128 * count), BF16)] * 3
        + [jax.ShapeDtypeStruct((8, 128 * count), F32)],
        scratch_shapes=[pltpu.VMEM((length, 128), F32)] * 2,
        compiler_params=params(),
        cost_estimate=SMALL_COST,
        name="attend_backward",
    )(segment.reshape(length, 1), segment.reshape(1, length), qkv, qkv, qkv, grad, lse)


def position_to_rel(slot, pieces, first):
    if pieces == 4 and first == 2:
        return (slot & 1) * 2 + slot // 2
    return slot


def place_rows(total, out_ref, spots, pieces, first, by_shard):
    shards_here, rows = out_ref.shape[1:3]
    for slot in range(pieces):
        piece = position_to_rel(slot, pieces, first) ^ spots[1]
        for rel_z in range(shards_here):
            owner = 0 if by_shard else rel_z ^ spots[2]
            start = pl.multiple_of((owner * pieces + piece) * rows, 16)
            out_ref[slot, rel_z] = total[pl.ds(start, rows), :].astype(BF16)


def grad_kernel(pieces, first, by_shard, spots, x_ref, far_y, near_y, far_ref, near_ref, total):
    for y_ref, out_ref in ((far_y, far_ref), (near_y, near_ref)):
        total[...] = dot_tn(x_ref[...], y_ref[...])
        place_rows(total, out_ref, spots, pieces, first, by_shard)


def grad_heads_kernel(pieces, first, extra, spots, x_ref, *rest):
    far_y, near_y = rest[:3], rest[3:6]
    far_ref, near_ref, total = rest[-3:]
    for side, (y_refs, out_ref) in enumerate(((far_y, far_ref), (near_y, near_ref))):
        joined = jnp.concatenate([y_ref[...] for y_ref in y_refs], axis=1)
        columns = joined.shape[1]
        total[:, :columns] = dot_tn(x_ref[...], joined)
        if extra:
            total[:, columns:] = dot_tn(rest[6][...], rest[7 + side][...])
        place_rows(total, out_ref, spots, pieces, first, False)


def grad_call(kernel, grid, in_specs, operands, out_spec, shape, scratch, spots):
    length, rows = operands[0].shape[0], shape[0] * shape[1] * shape[2]
    return pl.pallas_call(
        kernel,
        grid_spec=pltpu.PrefetchScalarGridSpec(
            num_scalar_prefetch=1,
            grid=grid,
            in_specs=in_specs,
            out_specs=[out_spec] * 2,
            scratch_shapes=[pltpu.VMEM(scratch, F32)],
        ),
        out_shape=[jax.ShapeDtypeStruct(shape, BF16)] * 2,
        compiler_params=params(),
        cost_estimate=SMALL_COST,
        name="weight_grad",
    )(spots, *operands)


def grad_proj(x, y, spots, shards, pieces, first):
    length, rows_all = x.shape
    half = y.shape[1] // 2
    rows = rows_all // (shards * pieces)
    return grad_call(
        functools.partial(grad_kernel, pieces, first, True),
        (shards,),
        [
            pl.BlockSpec((length, rows_all // shards), lambda i, s: (0, i ^ s[2])),
            pl.BlockSpec((length, half), lambda i, s: (0, 1 - s[0])),
            pl.BlockSpec((length, half), lambda i, s: (0, s[0])),
        ],
        [x, y, y],
        pl.BlockSpec((pieces, 1, rows, half), lambda i, s: (0, i, 0, 0)),
        (pieces, shards, rows, half),
        (rows_all // shards, half),
        spots,
    )


def grad_fc(x, y, spots, shards, pieces, first):
    length, rows_all = x.shape
    tile = rows_all // 2
    half = y.shape[1] // 2
    tiles = half // tile
    rows = rows_all // (shards * pieces)
    return grad_call(
        functools.partial(grad_kernel, pieces, first, False),
        (tiles,),
        [
            pl.BlockSpec((length, rows_all), lambda i, s: (0, 0)),
            pl.BlockSpec((length, tile), lambda i, s: (0, (1 - s[0]) * tiles + i)),
            pl.BlockSpec((length, tile), lambda i, s: (0, s[0] * tiles + i)),
        ],
        [x, y, y],
        pl.BlockSpec((pieces, shards, rows, tile), lambda i, s: (0, 0, 0, i)),
        (pieces, shards, rows, half),
        (rows_all, tile),
        spots,
    )


def grad_heads(x, grads, spots, shards, pieces, first, extra=()):
    length, rows_all = x.shape
    half = grads[0].shape[1] // 2
    rows = rows_all // (shards * pieces)
    columns = 3 * half
    far = pl.BlockSpec((length, half), lambda i, s: (0, 1 - s[0]))
    near = pl.BlockSpec((length, half), lambda i, s: (0, s[0]))
    in_specs = [pl.BlockSpec((length, rows_all), lambda i, s: (0, 0))] + [far] * 3 + [near] * 3
    operands = [x, *grads, *grads]
    if extra:
        half2 = extra[1].shape[1] // 2
        columns += half2
        in_specs += [
            pl.BlockSpec((length, rows_all), lambda i, s: (0, 0)),
            pl.BlockSpec((length, half2), lambda i, s: (0, 1 - s[0])),
            pl.BlockSpec((length, half2), lambda i, s: (0, s[0])),
        ]
        operands += [extra[0], extra[1], extra[1]]
    shape = (pieces, shards, rows, columns)
    return grad_call(
        functools.partial(grad_heads_kernel, pieces, first, bool(extra)),
        (1,),
        in_specs,
        operands,
        pl.BlockSpec(shape, lambda i, s: (0, 0, 0, 0)),
        shape,
        (rows_all, columns),
        spots,
    )


def piece_copies(full_ref, own_ref, parts, column, spots, sems, shards, pieces):
    core, spot_u, spot_z = spots[0], spots[1], spots[2]
    shard_rows = own_ref.shape[0]
    half = own_ref.shape[1] // 2
    rows = shard_rows // pieces
    copies = [
        pltpu.make_async_copy(
            own_ref,
            full_ref.at[pl.ds(pl.multiple_of(spot_z * shard_rows, 16), shard_rows), :],
            sems.at[0],
        )
    ]
    for index, part in enumerate(parts):
        side = core if index < pieces else 1 - core
        piece = spot_u ^ (index % pieces)
        for step in range(1, shards):
            start = pl.multiple_of((spot_z ^ step) * shard_rows + piece * rows, 16)
            copies.append(
                pltpu.make_async_copy(
                    part.at[step - 1, pl.ds(0, rows), pl.ds(column, half)],
                    full_ref.at[pl.ds(start, rows), pl.ds(pl.multiple_of(side * half, 128), half)],
                    sems.at[len(copies)],
                )
            )
    return copies


def at_first(work):
    @pl.when(pl.program_id(0) == 0)
    def _():
        work()


def start_all(copies):
    for copy in copies:
        copy.start()


def wait_all(copies):
    for copy in copies:
        copy.wait()


def row_call(kernel, name, steps, spots, rows_in, whole_in, parts_in, outs, sem_sets, sem_count):
    length = rows_in[0].shape[0]
    rows = length // steps

    def by_rows(width):
        return pl.BlockSpec((rows, width), lambda i, s: (i, 0))

    def whole(shape):
        return pl.BlockSpec(shape, lambda i, s: (0,) * len(shape))

    anywhere = pl.BlockSpec(memory_space=pl.ANY)
    return pl.pallas_call(
        kernel,
        grid_spec=pltpu.PrefetchScalarGridSpec(
            num_scalar_prefetch=1,
            grid=(steps,),
            in_specs=[by_rows(item.shape[1]) for item in rows_in]
            + [whole(item.shape) for item in whole_in]
            + [anywhere] * len(parts_in),
            out_specs=[
                by_rows(shape[1]) if tiled else whole(shape) for shape, _, tiled in outs
            ],
            scratch_shapes=[pltpu.SemaphoreType.DMA((sem_count,))] * sem_sets,
        ),
        out_shape=[jax.ShapeDtypeStruct(shape, dtype) for shape, dtype, _ in outs],
        compiler_params=params(),
        cost_estimate=SMALL_COST,
        name=name,
    )(spots, *rows_in, *whole_in, *parts_in)


def normed_rows(values):
    center = values - jnp.mean(values, axis=-1, keepdims=True)
    scale = lax.rsqrt(jnp.mean(center * center, axis=-1, keepdims=True) + 1e-05)
    return center * scale, scale


def norm_back(grad, values, gain):
    normed, scale = normed_rows(values)
    scaled = grad * gain
    inner = scaled - jnp.mean(scaled, axis=-1, keepdims=True)
    inner = inner - normed * jnp.mean(scaled * normed, axis=-1, keepdims=True)
    return scale * inner, normed


GAIN_ONE, SHIFT_ONE, BIAS_Q, BIAS_V, BIAS_OUT, GAIN_TWO, SHIFT_TWO, BIAS_PROJ = range(8)
GELU_SCALE = math.sqrt(2 / math.pi)
GELU_CUBE = 0.044715


def row_of(ref, index):
    return ref[index : index + 1, :]


def qkv_kernel(shards, pieces, spots, x_ref, vec_ref, own_ref, *rest):
    parts = rest[: 2 * pieces]
    w_ref, norm_ref, qkv_ref, sems = rest[2 * pieces :]
    copies = piece_copies(w_ref, own_ref, parts, 0, spots, sems, shards, pieces)
    at_first(lambda: start_all(copies))
    normed, _ = normed_rows(x_ref[...].astype(F32))
    norm_one = (normed * row_of(vec_ref, GAIN_ONE) + row_of(vec_ref, SHIFT_ONE)).astype(BF16)
    norm_ref[...] = norm_one
    at_first(lambda: wait_all(copies))
    width = norm_one.shape[1]
    for kind, row in enumerate((BIAS_Q, None, BIAS_V)):
        here = slice(kind * width, (kind + 1) * width)
        value = dot_nn(norm_one, w_ref[:, here])
        if row is not None:
            value = value + row_of(vec_ref, row)
        qkv_ref[:, here] = value.astype(BF16)


def fc_kernel(shards, pieces, spots, att_ref, x_ref, vec_ref, bias_ref, own_out, own_fc, *rest):
    parts = rest[: 2 * pieces]
    wo_ref, wf_ref, resid_ref, norm_ref, pre_ref, gelu_ref, sems_out, sems_fc = rest[2 * pieces :]
    half = own_out.shape[1] // 2
    copies_out = piece_copies(wo_ref, own_out, parts, 0, spots, sems_out, shards, pieces)
    copies_fc = piece_copies(wf_ref, own_fc, parts, half, spots, sems_fc, shards, pieces)
    at_first(lambda: start_all(copies_out + copies_fc))
    at_first(lambda: wait_all(copies_out))
    resid = x_ref[...].astype(F32) + dot_nn(att_ref[...], wo_ref[...]) + row_of(vec_ref, BIAS_OUT)
    resid_ref[...] = resid
    normed, _ = normed_rows(resid)
    norm_two = (normed * row_of(vec_ref, GAIN_TWO) + row_of(vec_ref, SHIFT_TWO)).astype(BF16)
    norm_ref[...] = norm_two
    at_first(lambda: wait_all(copies_fc))
    width = norm_two.shape[1]
    for tile in range(pre_ref.shape[1] // width):
        here = slice(tile * width, (tile + 1) * width)
        pre = dot_nn(norm_two, wf_ref[:, here]) + bias_ref[:, here]
        pre_ref[:, here] = pre
        curve = jnp.tanh(GELU_SCALE * (pre + GELU_CUBE * pre * pre * pre))
        gelu_ref[:, here] = (0.5 * pre * (1.0 + curve)).astype(BF16)


def proj_kernel(shards, pieces, spots, gelu_ref, resid_ref, vec_ref, own_ref, *rest):
    parts = rest[: 2 * pieces]
    w_ref, out_ref, sems = rest[2 * pieces :]
    copies = piece_copies(w_ref, own_ref, parts, 0, spots, sems, shards, pieces)
    at_first(lambda: start_all(copies))
    at_first(lambda: wait_all(copies))
    out_ref[...] = (
        resid_ref[...] + dot_nn(gelu_ref[...], w_ref[...]) + row_of(vec_ref, BIAS_PROJ)
    ).astype(BF16)


def clear_first(ref):
    def work():
        ref[...] = jnp.zeros_like(ref)

    at_first(work)


def column_sums(values):
    return jnp.sum(values, axis=0, keepdims=True)


def back_gelu_kernel(spots, g_ref, pre_ref, w_ref, grad_ref, fc_sums, proj_sums):
    clear_first(fc_sums)
    clear_first(proj_sums)
    grad = g_ref[...]
    proj_sums[0:1, :] += column_sums(grad.astype(F32))
    width = grad.shape[1]
    for tile in range(pre_ref.shape[1] // width):
        here = slice(tile * width, (tile + 1) * width)
        pre = pre_ref[:, here]
        square = pre * pre
        curve = jnp.tanh(GELU_SCALE * (pre + GELU_CUBE * square * pre))
        slope = 0.5 * (1.0 + curve) + (0.5 * GELU_SCALE) * pre * (1.0 - curve * curve) * (
            1.0 + (3.0 * GELU_CUBE) * square
        )
        grad_pre = (dot_nt(grad, w_ref[here, :]) * slope).astype(BF16)
        grad_ref[:, here] = grad_pre
        fc_sums[0:1, here] += column_sums(grad_pre.astype(F32))


def back_norm_kernel(
    spots, pre_ref, resid_ref, g_ref, vec_ref, wf_ref, wo_ref, sum_ref, low_ref, att_ref, sums_ref
):
    clear_first(sums_ref)
    grad = dot_nt(pre_ref[...], wf_ref[...])
    inner, normed = norm_back(grad, resid_ref[...], row_of(vec_ref, GAIN_TWO))
    total = g_ref[...].astype(F32) + inner
    sum_ref[...] = total
    low = total.astype(BF16)
    low_ref[...] = low
    sums_ref[0:1, :] += column_sums(low.astype(F32))
    sums_ref[1:2, :] += column_sums(grad * normed)
    sums_ref[2:3, :] += column_sums(grad)
    att_ref[...] = dot_nt(low, wo_ref[...]).astype(BF16)


def settle_kernel(pieces, every_ref, *outs):
    rows = every_ref.shape[1]
    for index in range(2 * pieces):
        piece, core = index // 2, index % 2
        column = 0
        for out_ref in outs:
            half = out_ref.shape[1] // 2
            out_ref[piece * rows : (piece + 1) * rows, core * half : (core + 1) * half] = every_ref[
                index, :, column : column + half
            ].astype(F32)
            column += half


def settle(every, widths, pieces):
    rows = every.shape[1]
    whole = pl.BlockSpec(memory_space=pltpu.VMEM)
    return pl.pallas_call(
        functools.partial(settle_kernel, pieces),
        in_specs=[whole],
        out_specs=[whole] * len(widths),
        out_shape=[jax.ShapeDtypeStruct((rows * pieces, width), F32) for width in widths],
        compiler_params=params(),
        name="settle",
    )(every)


def settle_last_kernel(pieces, wide, spots, *rest):
    parts, qkv_ref, out_ref = rest[: 2 * pieces], rest[-2], rest[-1]
    core, spot_u = spots[0], spots[1]
    rows = parts[0].shape[0]
    width = out_ref.shape[1]
    narrow = width // 2 - wide
    for index, part in enumerate(parts):
        side = core if index < pieces else 1 - core
        here = pl.ds(pl.multiple_of((spot_u ^ (index % pieces)) * rows, 16), rows)
        source = 0
        for base, size in ((0, wide), (2 * wide, narrow)):
            for kind in range(3):
                column = pl.multiple_of(kind * width + base + side * size, 128)
                qkv_ref[here, pl.ds(column, size)] = part[:, source : source + size].astype(F32)
                source += size
            if base == 0:
                column = pl.multiple_of(side * (width // 2), 128)
                out_ref[here, pl.ds(column, width // 2)] = part[
                    :, source : source + width // 2
                ].astype(F32)
                source += width // 2


def settle_last(parts, spots, pieces, wide, width):
    rows = parts[0].shape[0]
    whole = pl.BlockSpec(memory_space=pltpu.VMEM)
    return pl.pallas_call(
        functools.partial(settle_last_kernel, pieces, wide),
        in_specs=[pl.BlockSpec(memory_space=pltpu.SMEM)] + [whole] * (2 * pieces),
        out_specs=[whole] * 2,
        out_shape=[
            jax.ShapeDtypeStruct((rows * pieces, columns), F32) for columns in (3 * width, width)
        ],
        compiler_params=params(),
        name="settle_last",
    )(spots, *parts)


def back_product(w_ref, grads, start):
    total = None
    width = w_ref.shape[0]
    for kind, grad in enumerate(grads):
        first = kind * width + start
        part = dot_nt(grad[...], w_ref[:, first : first + grad.shape[1]])
        total = part if total is None else total + part
    return total


def back_one_kernel(w_ref, q_ref, k_ref, v_ref, out_ref):
    out_ref[...] = back_product(w_ref, (q_ref, k_ref, v_ref), 0)


def back_two_kernel(
    start, w_ref, q_ref, k_ref, v_ref, part_ref, x_ref, vec_ref, resid_ref, out_ref, sums_ref
):
    clear_first(sums_ref)
    grad = part_ref[...] + back_product(w_ref, (q_ref, k_ref, v_ref), start)
    inner, normed = norm_back(grad, x_ref[...].astype(F32), row_of(vec_ref, GAIN_ONE))
    out_ref[...] = (resid_ref[...] + inner).astype(BF16)
    sums_ref[0:1, :] += column_sums(grad * normed)
    sums_ref[1:2, :] += column_sums(grad)


def back_one(w, grads):
    length, width = grads[0].shape[0], w.shape[0]
    rows = length // 4
    return pl.pallas_call(
        back_one_kernel,
        grid=(4,),
        in_specs=[pl.BlockSpec(w.shape, lambda i: (0, 0))]
        + [pl.BlockSpec((rows, grads[0].shape[1]), lambda i: (i, 0))] * 3,
        out_specs=pl.BlockSpec((rows, width), lambda i: (i, 0)),
        out_shape=jax.ShapeDtypeStruct((length, width), F32),
        compiler_params=params(),
        cost_estimate=SMALL_COST,
        name="back_one",
    )(w, *grads)


def back_two(w, grads, start, part, values, vectors, resid):
    length, width = values.shape
    rows = length // 4
    block = pl.BlockSpec((rows, width), lambda i: (i, 0))
    return pl.pallas_call(
        functools.partial(back_two_kernel, start),
        grid=(4,),
        in_specs=[pl.BlockSpec(w.shape, lambda i: (0, 0))]
        + [pl.BlockSpec((rows, grads[0].shape[1]), lambda i: (i, 0))] * 3
        + [block, block, pl.BlockSpec((8, width), lambda i: (0, 0)), block],
        out_specs=[block, pl.BlockSpec((8, width), lambda i: (0, 0))],
        out_shape=[
            jax.ShapeDtypeStruct((length, width), BF16),
            jax.ShapeDtypeStruct((8, width), F32),
        ],
        compiler_params=params(),
        cost_estimate=SMALL_COST,
        name="back_two",
    )(w, *grads, part, values, vectors, resid)


def pack_kernel(ln1_ref, one_ref, two_ref, resid_ref, proj_ref, fc_ref, out_ref):
    width = out_ref.shape[1]
    wide = one_ref.shape[1]
    out_ref[0:2, :] = ln1_ref[0:2, :]
    out_ref[2:4, :wide] = one_ref[0:2, :]
    out_ref[2:4, wide:] = two_ref[0:2, :]
    out_ref[4:7, :] = resid_ref[0:3, :]
    out_ref[7:8, :] = proj_ref[0:1, :]
    count = fc_ref.shape[1] // width
    for index in range(count):
        out_ref[8 + index : 9 + index, :] = fc_ref[0:1, index * width : (index + 1) * width]
    out_ref[8 + count : 16, :] = jnp.zeros((8 - count, width), F32)


def pack(*sums):
    whole = pl.BlockSpec(memory_space=pltpu.VMEM)
    return pl.pallas_call(
        pack_kernel,
        in_specs=[whole] * len(sums),
        out_specs=whole,
        out_shape=jax.ShapeDtypeStruct((16, sums[0].shape[1]), F32),
        compiler_params=params(),
        cost_estimate=SMALL_COST,
        name="pack",
    )(*sums)


def shards_of(
    reps,
    shards,
    hidden_in,
    segment,
    cotangent,
    ln1_gain,
    ln1_bias,
    qkv_weight,
    query_bias,
    value_bias,
    out_weight,
    out_bias,
    ln2_gain,
    ln2_bias,
    fc_weight,
    fc_bias,
    proj_weight,
    proj_bias,
):
    width = hidden_in.shape[1]
    shard_rows = qkv_weight.shape[0]
    pieces = 4 if shard_rows % 64 == 0 and reps % 8 == 0 else 2
    rep = lax.axis_index("rep")
    spot_z = lax.axis_index("shard")
    core = rep & 1
    spot_u = (rep >> 1) & (pieces - 1)
    spots = jnp.stack([core, spot_u, spot_z]).astype(jnp.int32)

    def own_piece(weight):
        rows, half = weight.shape[0] // pieces, weight.shape[1] // 2
        return lax.dynamic_slice(weight, (spot_u * rows, core * half), (rows, half))

    def across_chips(part, first):
        if pieces == 2:
            return [part, swap(part, "rep", reps, 2)]
        second = 6 - first
        by_first = swap(part, "rep", reps, first)
        by_second = swap(part, "rep", reps, second)
        by_both = swap(part, "rep", reps, 6)
        if first == 2:
            return [part, by_first, by_second, by_both]
        return [part, by_second, by_first, by_both]

    def across_cores(parts):
        return parts + [swap(part, "rep", reps, 1) for part in parts]

    def along_shard(piece):
        return [swap(piece, "shard", shards, step) for step in range(1, shards)]

    piece_rows = shard_rows // pieces
    flat = [
        ln1_gain,
        ln1_bias,
        query_bias,
        value_bias,
        out_bias,
        ln2_gain,
        ln2_bias,
        proj_bias,
        fc_bias,
    ]
    flat_size = sum(item.shape[0] for item in flat)
    qkv_half = qkv_weight.shape[1] // 2
    small_rows = -(-flat_size // qkv_half)
    small = jnp.zeros((small_rows * qkv_half,), BF16)
    offset = 0
    for item in flat:
        size = item.shape[0]
        small = small + jnp.pad(item, (offset, small.shape[0] - offset - size))
        offset += size
    small = small.reshape(small_rows, qkv_half)
    tie = lax.optimization_barrier
    qkv_payload = jnp.concatenate(
        [own_piece(qkv_weight), jnp.pad(small, ((0, 16 - small_rows), (0, 0)))], axis=0
    )
    second_payload = jnp.concatenate([own_piece(out_weight), own_piece(fc_weight)], axis=1)
    qkv_slots = along_shard(qkv_payload)
    qkv_slots, second_payload = tie((qkv_slots, second_payload))
    qkv_parts = across_chips(jnp.stack([slot[:piece_rows] for slot in qkv_slots]), 2)
    second_slots = along_shard(second_payload)
    qkv_parts, proj_piece = tie((qkv_parts, own_piece(proj_weight)))
    qkv_parts = across_cores(qkv_parts)
    second_stack, qkv_parts, proj_piece = tie((jnp.stack(second_slots), qkv_parts, proj_piece))
    second_parts = across_chips(second_stack, 2)
    proj_slots = along_shard(proj_piece)

    rows_of = [small] + [slot[piece_rows : piece_rows + small_rows] for slot in qkv_slots]
    ordered = []
    for index in range(shards):
        total = jnp.zeros_like(rows_of[0])
        for step, value in enumerate(rows_of):
            total = jnp.where((spot_z ^ step) == index, value, total)
        ordered.append(total.reshape(-1)[:flat_size])
    vectors = jnp.stack(ordered).astype(F32)
    bias_fc = vectors[:, 8 * shard_rows :].reshape(1, -1)
    vectors = vectors[:, : 8 * shard_rows].reshape(shards, 8, shard_rows)
    vectors = vectors.transpose(1, 0, 2).reshape(8, width)

    seg_row = segment[0]
    length = hidden_in.shape[0]
    ff = fc_weight.shape[1]
    steps = 4
    sem_count = 1 + 2 * pieces * (shards - 1)
    kernel_of = lambda body: functools.partial(body, shards, pieces)
    w_qkv, norm_one, qkv = row_call(
        kernel_of(qkv_kernel),
        "qkv",
        steps,
        spots,
        [hidden_in],
        [vectors],
        [qkv_weight, *qkv_parts],
        [
            ((width, 3 * width), BF16, False),
            ((length, width), BF16, True),
            ((length, 3 * width), BF16, True),
        ],
        1,
        sem_count,
    )
    attended_one, lse_one = attend_forward(qkv, seg_row, 0, 4)
    attended_one, proj_slots, qkv = tie((attended_one, proj_slots, qkv))
    proj_parts = across_chips(jnp.stack(proj_slots), 4)
    attended_two, lse_two = attend_forward(qkv, seg_row, 4, 2)
    attended_two, second_parts = tie((attended_two, second_parts))
    second_parts = across_cores(second_parts)
    attended = jnp.concatenate([attended_one, attended_two], axis=1)
    w_out, w_fc, resid, norm_two, pre_act, gelu_low = row_call(
        kernel_of(fc_kernel),
        "fc",
        steps,
        spots,
        [attended, hidden_in],
        [vectors, bias_fc],
        [out_weight, fc_weight, *second_parts],
        [
            ((width, width), BF16, False),
            ((width, ff), BF16, False),
            ((length, width), F32, True),
            ((length, width), BF16, True),
            ((length, ff), F32, True),
            ((length, ff), BF16, True),
        ],
        2,
        sem_count,
    )

    half_pieces = pieces // 2

    def summed(near, old):
        return near.astype(F32) + old.astype(F32)

    def sent_part(near, old):
        return summed(near[half_pieces:], old[half_pieces:]).astype(BF16)

    def after_first(near, old, came):
        kept = summed(near[:half_pieces], old[:half_pieces]) + came.astype(F32)
        return kept[0], kept[half_pieces - 1].astype(BF16)

    def second_swap(onward, mask):
        return jnp.zeros_like(onward) if pieces == 2 else swap(onward, "rep", reps, mask)

    def shard_swaps(held):
        low = held.astype(BF16)
        return [swap(low[step], "shard", shards, step) for step in range(1, shards)]

    def shard_total(held, came):
        total = held[0]
        for value in came:
            total = total + value.astype(F32)
        mask = 2 * pieces
        while mask < reps:
            total = total + swap(total.astype(BF16), "rep", reps, mask).astype(F32)
            mask *= 2
        return total.astype(BF16)

    def every_owner(piece):
        return lax.all_gather(piece, "rep", axis=0, tiled=False)[: 2 * pieces]

    call = (spots, shards, pieces)
    first_of = 2 if pieces == 2 else 4
    gelu_low, proj_parts = tie((gelu_low, proj_parts))
    proj_parts = across_cores(proj_parts)
    proj_far, proj_near = grad_proj(gelu_low, cotangent, *call, 2)
    gelu_low, proj_far, proj_near, proj_parts = tie((gelu_low, proj_far, proj_near, proj_parts))
    proj_old = swap(proj_far, "rep", reps, 1)
    w_proj, block_out = row_call(
        kernel_of(proj_kernel),
        "proj",
        steps,
        spots,
        [gelu_low, resid],
        [vectors],
        [proj_weight, *proj_parts],
        [((width * 4, width), BF16, False), ((length, width), BF16, True)],
        1,
        sem_count,
    )
    w_proj, proj_old = tie((w_proj, proj_old))
    proj_send = sent_part(proj_near, proj_old)
    proj_send, w_proj = tie((proj_send, w_proj))
    proj_came = swap(proj_send, "rep", reps, 2)
    grad_pre, fc_sums, proj_sums = row_call(
        back_gelu_kernel,
        "back_gelu",
        steps,
        spots,
        [cotangent, pre_act],
        [w_proj],
        [],
        [((length, ff), BF16, True), ((8, ff), F32, False), ((8, width), F32, False)],
        0,
        0,
    )
    fc_far, fc_near = grad_fc(norm_two, grad_pre, *call, first_of)
    grad_pre, fc_far, fc_near, proj_came = tie((grad_pre, fc_far, fc_near, proj_came))
    fc_old = swap(fc_far, "rep", reps, 1)
    proj_held, proj_onward = after_first(proj_near, proj_old, proj_came)
    grad_pre, proj_onward = tie((grad_pre, proj_onward))
    proj_came = second_swap(proj_onward, 4)
    grad_resid, grad_branch, grad_attended, resid_sums = row_call(
        back_norm_kernel,
        "back_norm",
        steps,
        spots,
        [grad_pre, resid, cotangent],
        [vectors, w_fc, w_out],
        [],
        [
            ((length, width), F32, True),
            ((length, width), BF16, True),
            ((length, width), BF16, True),
            ((8, width), F32, False),
        ],
        0,
        0,
    )
    grad_attended, fc_old = tie((grad_attended, fc_old))
    fc_send = sent_part(fc_near, fc_old)
    grad_attended, fc_send, proj_came = tie((grad_attended, fc_send, proj_came))
    fc_came = swap(fc_send, "rep", reps, first_of)
    *heads_one, sums_one = attend_backward(qkv, seg_row, grad_attended, lse_one, 0, 4)
    heads_one, fc_came, grad_attended, proj_came = tie(
        (heads_one, fc_came, grad_attended, proj_came)
    )
    proj_held = proj_held + proj_came.astype(F32)
    proj_shards = shard_swaps(proj_held)
    fc_held, fc_onward = after_first(fc_near, fc_old, fc_came)
    fc_onward, heads_one = tie((fc_onward, heads_one))
    fc_came = second_swap(fc_onward, 2)
    one_far, one_near = grad_heads(norm_one, heads_one, *call, first_of, (attended, grad_branch))
    heads_one, one_far, one_near, proj_shards = tie((heads_one, one_far, one_near, proj_shards))
    one_old = swap(one_far, "rep", reps, 1)
    proj_piece = shard_total(proj_held, proj_shards)
    proj_piece, heads_one = tie((proj_piece, heads_one))
    part_one = back_one(w_qkv, heads_one)
    part_one, one_old, grad_attended, fc_came = tie((part_one, one_old, grad_attended, fc_came))
    one_send = sent_part(one_near, one_old)
    fc_held = fc_held + fc_came.astype(F32)
    one_send, grad_attended, fc_held = tie((one_send, grad_attended, fc_held))
    one_came = swap(one_send, "rep", reps, first_of)
    fc_shards = shard_swaps(fc_held)
    *heads_two, sums_two = attend_backward(qkv, seg_row, grad_attended, lse_two, 4, 2)
    heads_two, fc_shards = tie((heads_two, fc_shards))
    two_far, two_near = grad_heads(norm_one, heads_two, *call, 2)
    heads_two, two_far, two_near, one_came = tie((heads_two, two_far, two_near, one_came))
    two_old = swap(two_far, "rep", reps, 1)
    one_held, one_onward = after_first(one_near, one_old, one_came)
    fc_piece = shard_total(fc_held, fc_shards)
    two_old, one_onward, heads_two, fc_piece = tie((two_old, one_onward, heads_two, fc_piece))
    one_came = second_swap(one_onward, 2)
    two_send = sent_part(two_near, two_old)
    two_send, heads_two = tie((two_send, heads_two))
    two_came = swap(two_send, "rep", reps, 2)
    input_grad, ln1_sums = back_two(
        w_qkv, heads_two, 128 * 4, part_one, hidden_in, vectors, grad_resid
    )
    small_grads = pack(ln1_sums, sums_one, sums_two, resid_sums, proj_sums, fc_sums)
    masks = [("rep", reps, 1 << i) for i in range(reps.bit_length() - 1)]
    masks += [("shard", shards, 1 << i) for i in range(shards.bit_length() - 1)]

    def vector_step(total, count=1):
        for _ in range(count):
            axis, size, mask = masks.pop(0)
            total = total + swap(total, axis, size, mask)
        return total

    two_came, one_came, small_grads = tie((two_came, one_came, small_grads))
    two_held, two_onward = after_first(two_near, two_old, two_came)
    two_onward, small_grads = tie((two_onward, small_grads))
    two_came = second_swap(two_onward, 4)
    one_held = one_held + one_came.astype(F32)
    small_grads = vector_step(small_grads)
    two_came, one_held, small_grads = tie((two_came, one_held, small_grads))
    last_held = jnp.concatenate([one_held, two_held + two_came.astype(F32)], axis=-1)
    last_shards = shard_swaps(last_held)
    small_grads = vector_step(small_grads, 2)
    last_shards, small_grads = tie((last_shards, small_grads))
    last_parts = across_chips(shard_total(last_held, last_shards), 2)
    small_grads = vector_step(small_grads, len(masks))
    last_parts, small_grads, every_fc, every_proj = tie(
        (last_parts, small_grads, every_owner(fc_piece), every_owner(proj_piece))
    )
    last_parts = across_cores(last_parts)
    (d_fc_weight,) = settle(every_fc, (fc_weight.shape[1],), pieces)
    (d_proj_weight,) = settle(every_proj, (width,), pieces)
    d_qkv_weight, d_out_weight = settle_last(
        last_parts, spots, pieces, heads_one[0].shape[1] // 2, width
    )
    mine = lax.dynamic_slice(small_grads[:8], (0, spot_z * shard_rows), (8, shard_rows))
    fc_rows = fc_bias.shape[0]
    fc_row = small_grads[8 : 8 + ff // width].reshape(-1)
    d_fc_bias = lax.dynamic_slice(fc_row, (spot_z * fc_rows,), (fc_rows,))
    return (
        block_out,
        input_grad,
        mine[0],
        mine[1],
        d_qkv_weight,
        mine[2],
        mine[3],
        d_out_weight,
        mine[4],
        mine[5],
        mine[6],
        d_fc_weight,
        d_fc_bias,
        d_proj_weight,
        mine[7],
    )


def solution(mesh):
    tokens = P(("rep", "shard"), None)
    flat = P("shard")
    rows = P("shard", None)
    in_specs = (
        tokens,
        tokens,
        tokens,
        flat,
        flat,
        rows,
        flat,
        flat,
        rows,
        flat,
        flat,
        flat,
        rows,
        flat,
        rows,
        flat,
    )
    out_specs = (
        tokens,
        tokens,
        flat,
        flat,
        rows,
        flat,
        flat,
        rows,
        flat,
        flat,
        flat,
        rows,
        flat,
        rows,
        flat,
    )
    body = functools.partial(shards_of, mesh.shape["rep"], mesh.shape["shard"])
    return jax.shard_map(
        body, mesh=mesh, in_specs=in_specs, out_specs=out_specs, check_vma=False
    )
```

time: 459 us -> 376 us (0.82)
  matrix products: 66.1 us -> 0 us
  Pallas kernels: 141 us -> 195 us
  waiting for transfers between devices: 99.8 us -> 55.5 us
  blocking collectives: 10.4 us -> 0 us
  local copies, waits for them, and re-layouts: 26.8 us -> 20 us
  other arithmetic: 25.3 us -> 20.1 us
    pallas_call x5 -> x9, Pallas kernels: 20.9 us -> 94.1 us  [the longest x5 73.9 us: row_call(): pl.pallas_call(kernel, grid_spec=pltpu.PrefetchScalarGridSpec(num_scalar_...]
    dot_general x8 -> x0, matrix products: 66.1 us -> none  [the longest x1 15.2 us: shards_of(): jnp.einsum('td,fd->tf', cotangent, w_proj, preferred_element_type=F32)]
    ppermute x66 -> x63, waiting for transfers between devices: 99.8 us -> 55.4 us  [swap(): return lax.ppermute(value, axis, [(i, i ^ mask) for i in range(size)])]
    pallas_call x8 -> x4, Pallas kernels: 56.1 us -> 37.4 us  [grad_call(): pl.pallas_call(kernel, grid_spec=pltpu.PrefetchScalarGridSpec(num_scalar_...]
    reduce_sum x8 -> x0, other arithmetic: 10.9 us -> none  [the longest x3 4.7 us: column_sum(): return jnp.sum(values.astype(F32), axis=0)]
    all_gather x1 -> x0, blocking collectives: 10.4 us -> none  [every_owner(): return lax.all_gather(piece, 'rep', axis=0, tiled=False)[:2 * pieces]]
    add x7 -> x13, other arithmetic: 2.65 us -> 10 us  [the longest x4 6.81 us: after_first(): kept = summed(near[:half_pieces], old[:half_pieces]) + came.astype(F32)]
    concatenate x2 -> x0, local copies, waits for them, and re-layouts: 6.24 us -> none  [the longest x1 6.21 us: shards_of(): jnp.concatenate([ln1_gain, ln1_bias, query_bias, value_bias, out_bias, ln...]
  transfers between devices with their start and end apart: 68 -> 65, of which waited for: 23 -> 16; matrix products, arithmetic and copies ran while one was open for 23% -> 6% of each run, Pallas kernels for 26% -> 52%
where the time goes in v2:
time: 376 us; the launch traced here: 372 us
  Pallas kernels  195 us (52%)
  starting transfers between devices  65.7 us (17%)
  waiting for transfers between devices  55.5 us (15%)
  other arithmetic  20.1 us (5%)
  local copies, waits for them, and re-layouts  20 us (5%)
  between operations  15.3 us (4%)
    pallas_call x5, Pallas kernels, row_call(): pl.pallas_call(kernel, grid_spec=pltpu.PrefetchScalarGridSpec(num_scalar_...  73.9 us
    ppermute x63, starting transfers between devices, swap(): return lax.ppermute(value, axis, [(i, i ^ mask) for i in range(size)])  65.6 us
    ppermute x63, waiting for transfers between devices, swap(): return lax.ppermute(value, axis, [(i, i ^ mask) for i in range(size)])  55.4 us
    pallas_call x2, Pallas kernels, attend_backward(): pl.pallas_call(functools.partial(attend_back_kernel, rows), grid=(count,)...  37.6 us
    pallas_call x4, Pallas kernels, grad_call(): pl.pallas_call(kernel, grid_spec=pltpu.PrefetchScalarGridSpec(num_scalar_...  37.4 us
    pallas_call x2, Pallas kernels, attend_forward(): pl.pallas_call(functools.partial(attend_kernel, rows), grid=(count,), in_...  20.5 us
    unnamed x102, local copies, waits for them, and re-layouts  10.8 us
    pallas_call x1, Pallas kernels, back_two(): pl.pallas_call(functools.partial(back_two_kernel, start), grid=(4,), in_s...  8.43 us
  transfers between devices with their start and end apart: 65, of which 16 were waited for; matrix products, arithmetic and copies ran while one was open for 6% of the time, Pallas kernels for 52%

profile of v2, /device:TPU:0, one launch (start us, length us, event | category | flops | bytes accessed | tf_op | source)
XLA Modules:
  0.0 371.9 jit_solution(565773877628351689)
XLA Ops:
  9.1 3.1 collective-permute-start
  12.2 2.6 collective-permute-start.1
  18.0 8.1 %collective-permute-done.1 = bf16[64,1152]{1,0:T(8,128)(2,1)S(1)} collective-permute-done((bf16[64,1152]{1,0:T(8,128)(2,1)S(1)}, bf16[64,1152]{1,0:T(8,128)(2,1)S(1)}, u32[]{:S(2)}, u32[]{:S(2)}) %collective-permute-start.1) | collective-permute-done | bytes 147488 | tf_op jit(solution)/shard_map/ppermute | solution.py:38
  30.5 2.3 collective-permute-start.3
  34.8 1.6 dynamic_slice.21
  37.6 2.4 collective-permute-start.5
  40.0 2.3 collective-permute-done.7.rest_2_
  43.0 4.1 %collective-permute-done.4 = bf16[48,1920]{1,0:T(8,128)(2,1)S(1)} collective-permute-done((bf16[48,1920]{1,0:T(8,128)(2,1)S(1)}, bf16[48,1920]{1,0:T(8,128)(2,1)S(1)}, u32[]{:S(2)}, u32[]{:S(2)}) %collective-permute-start.4) | collective-permute-done | bytes 184352 | tf_op jit(solution)/shard_map/ppermute | solution.py:38
  54.2 2.4 collective-permute-start.13
  58.5 2.4 collective-permute-done.13
  60.9 3.3 collective-permute-start.15
  65.0 11.0 %qkv.1 = (bf16[768,2304]{1,0:T(8,128)(2,1)}, bf16[1024,768]{1,0:T(8,128)(2,1)}, bf16[1024,2304]{1,0:T(8,128)(2,1)}) custom-call(s32[3]{0:T(128)} %pad_add_fusion.1.spots, bf16[1024,768]{1,0:T(8,128)(2,1)} %x_ref.5, f32[8,768]{1,0:T(8,128)} %reshape.51.vec_ref, bf16[192,2304]{1,0:T(8,128)(2,1)} %own_ref.2, bf16[3,48,1152]{2,1,0:T(8,128)(2,1)} %copy-done.8, ...), custom_call_target="tpu_custom_call" | custom-call | flops 1000000 | bytes 100000 | tf_op jit(solution)/shard_map/qkv/pallas_call | solution.py:358
  76.0 12.9 %attend_forward.2 = (bf16[1024,512]{1,0:T(8,128)(2,1)}, f32[8,8,1024]{2,1,0:T(8,128)}) custom-call(s32[1024,1]{1,0:T(8,128)} %copy.32.seg_col, s32[1,1024]{1,0:T(1,128)} %seg_row.7, bf16[1024,2304]{1,0:T(8,128)(2,1)} %get-tuple-element.208.q_ref.k_ref.v_ref, bf16[1024,2304]{1,0:T(8,128)(2,1)} %get-tuple-element.208.q_ref.k_ref.v_ref, ...), custom_call_target="tpu_custom_call" | custom-call | flops 1000000 | bytes 100000 | tf_op jit(solution)/shard_map/attend_forward/pallas_call | solution.py:93
  89.0 7.6 %attend_forward.3 = (bf16[1024,256]{1,0:T(8,128)(2,1)}, f32[4,8,1024]{2,1,0:T(8,128)}) custom-call(s32[1024,1]{1,0:T(8,128)} %copy.32.seg_col, s32[1,1024]{1,0:T(1,128)} %seg_row.7, bf16[1024,2304]{1,0:T(8,128)(2,1)} %get-tuple-element.208.q_ref.k_ref.v_ref, bf16[1024,2304]{1,0:T(8,128)(2,1)} %get-tuple-element.208.q_ref.k_ref.v_ref, ...), custom_call_target="tpu_custom_call" | custom-call | flops 1000000 | bytes 100000 | tf_op jit(solution)/shard_map/attend_forward/pallas_call | solution.py:93
  104.7 19.3 %fc.1 = (bf16[768,768]{1,0:T(8,128)(2,1)}, bf16[768,3072]{1,0:T(8,128)(2,1)}, f32[1024,768]{1,0:T(8,128)}, bf16[1024,768]{1,0:T(8,128)(2,1)}, f32[1024,3072]{1,0:T(8,128)}, /*index=5*/bf16[1024,3072]{1,0:T(8,128)(2,1)}) custom-call(s32[3]{0:T(128)} %pad_add_fusion.1.spots, bf16[1024,768]{1,0:T(8,128)(2,1)} %copy-done, bf16[1024,768]{1,0:T(8,128)(2,1)} %x_ref.5, ...), custom_call_target="tpu_custom_call" | custom-call | flops 1000000 | bytes 100000 | tf_op jit(solution)/shard_map/fc/pallas_call | solution.py:358
  125.1 11.4 %weight_grad.4 = (bf16[4,4,192,384]{3,2,1,0:T(8,128)(2,1)}, bf16[4,4,192,384]{3,2,1,0:T(8,128)(2,1)}) custom-call(s32[3]{0:T(128)} %pad_add_fusion.1.spots, bf16[1024,3072]{1,0:T(8,128)(2,1)} %get-tuple-element.227.x_ref.gelu_ref, bf16[1024,768]{1,0:T(8,128)(2,1)} %g_ref.3, bf16[1024,768]{1,0:T(8,128)(2,1)} %g_ref.3), custom_call_target="tpu_custom_call" | custom-call | flops 1000000 | bytes 100000 | tf_op jit(solution)/shard_map/weight_grad/pallas_call | solution.py:215
  137.9 12.1 %proj.1 = (bf16[3072,768]{1,0:T(8,128)(2,1)}, bf16[1024,768]{1,0:T(8,128)(2,1)}) custom-call(s32[3]{0:T(128)} %pad_add_fusion.1.spots, bf16[1024,3072]{1,0:T(8,128)(2,1)} %get-tuple-element.227.x_ref.gelu_ref, f32[1024,768]{1,0:T(8,128)} %get-tuple-element.228.resid_ref, f32[8,768]{1,0:T(8,128)} %reshape.51.vec_ref, bf16[768,768]{1,0:T(8,128)(2,1)} %own_ref.3, ...), custom_call_target="tpu_custom_call" | custom-call | flops 1000000 | bytes 100000 | tf_op jit(solution)/shard_map/proj/pallas_call | solution.py:358
  152.5 15.8 %back_gelu.1 = (bf16[1024,3072]{1,0:T(8,128)(2,1)}, f32[8,3072]{1,0:T(8,128)}, f32[8,768]{1,0:T(8,128)}) custom-call(s32[3]{0:T(128)} %pad_add_fusion.1.spots, bf16[1024,768]{1,0:T(8,128)(2,1)} %g_ref.3, f32[1024,3072]{1,0:T(8,128)} %get-tuple-element.239.pre_ref, bf16[3072,768]{1,0:T(8,128)(2,1)} %get-tuple-element.245.w_ref), custom_call_target="tpu_custom_call" | custom-call | flops 1000000 | bytes 100000 | tf_op jit(solution)/shard_map/back_gelu/pallas_call | solution.py:358
  168.2 11.1 %weight_grad.5 = (bf16[4,4,48,1536]{3,2,1,0:T(8,128)(2,1)}, bf16[4,4,48,1536]{3,2,1,0:T(8,128)(2,1)}) custom-call(s32[3]{0:T(128)} %pad_add_fusion.1.spots, bf16[1024,768]{1,0:T(8,128)(2,1)} %get-tuple-element.247.x_ref, bf16[1024,3072]{1,0:T(8,128)(2,1)} %get-tuple-element.254.far_y.near_y.pre_ref, bf16[1024,3072]{1,0:T(8,128)(2,1)} %get-tuple-element.254.far_y.near_y.pre_ref), custom_call_target="tpu_custom_call" | custom-call | flops 1000000 | bytes 100000 | tf_op jit(solution)/shard_map/weight_grad/pallas_call | solution.py:215
  179.4 1.7 convert_add_fusion.1
  183.4 15.8 %back_norm.1 = (f32[1024,768]{1,0:T(8,128)}, bf16[1024,768]{1,0:T(8,128)(2,1)}, bf16[1024,768]{1,0:T(8,128)(2,1)}, f32[8,768]{1,0:T(8,128)}) custom-call(s32[3]{0:T(128)} %pad_add_fusion.1.spots, bf16[1024,3072]{1,0:T(8,128)(2,1)} %get-tuple-element.254.far_y.near_y.pre_ref, f32[1024,768]{1,0:T(8,128)} %get-tuple-element.228.resid_ref, ...), custom_call_target="tpu_custom_call" | custom-call | flops 1000000 | bytes 100000 | tf_op jit(solution)/shard_map/back_norm/pallas_call | solution.py:358
  201.1 24.4 %attend_backward.2 = (bf16[1024,512]{1,0:T(8,128)(2,1)}, bf16[1024,512]{1,0:T(8,128)(2,1)}, bf16[1024,512]{1,0:T(8,128)(2,1)}, f32[8,512]{1,0:T(8,128)}) custom-call(s32[1024,1]{1,0:T(8,128)} %copy.32.seg_col, s32[1,1024]{1,0:T(1,128)} %seg_row.7, bf16[1024,2304]{1,0:T(8,128)(2,1)} %get-tuple-element.208.q_ref.k_ref.v_ref, ...), custom_call_target="tpu_custom_call" | custom-call | flops 1000000 | bytes 100000 | tf_op jit(solution)/shard_map/attend_backward/pallas_call | solution.py:160
  225.5 3.3 collective-permute-done.34
  228.8 2.0 convert_add_fusion
  233.8 2.8 collective-permute-start.37
  236.7 9.7 %weight_grad.6 = (bf16[4,4,48,1152]{3,2,1,0:T(8,128)(2,1)}, bf16[4,4,48,1152]{3,2,1,0:T(8,128)(2,1)}) custom-call(s32[3]{0:T(128)} %pad_add_fusion.1.spots, bf16[1024,768]{1,0:T(8,128)(2,1)} %get-tuple-element.276.x_ref, bf16[1024,512]{1,0:T(8,128)(2,1)} %get-tuple-element.288.rest_0_.rest_3_.q_ref, ...), custom_call_target="tpu_custom_call" | custom-call | flops 1000000 | bytes 100000 | tf_op jit(solution)/shard_map/weight_grad/pallas_call | solution.py:215
  248.4 7.2 %back_one.1.part_ref = f32[1024,768]{1,0:T(8,128)} custom-call(bf16[768,2304]{1,0:T(8,128)(2,1)} %get-tuple-element.238.w_ref, bf16[1024,512]{1,0:T(8,128)(2,1)} %get-tuple-element.288.rest_0_.rest_3_.q_ref, bf16[1024,512]{1,0:T(8,128)(2,1)} %get-tuple-element.289.rest_1_.rest_4_.k_ref, bf16[1024,512]{1,0:T(8,128)(2,1)} %get-tuple-element.290.rest_2_.rest_5_.v_ref), custom_call_target="tpu_custom_call" | custom-call | flops 1000000 | bytes 100000 | tf_op jit(solution)/shard_map/back_one/pallas_call | solution.py:591
  255.6 6.6 %collective-permute-done.39 = bf16[4,48,1536]{2,1,0:T(8,128)(2,1)S(1)} collective-permute-done((bf16[4,48,1536]{2,1,0:T(8,128)(2,1)S(1)}, bf16[4,48,1536]{2,1,0:T(8,128)(2,1)S(1)}, u32[]{:S(2)}, u32[]{:S(2)}) %collective-permute-start.39) | collective-permute-done | bytes 589856 | tf_op jit(solution)/shard_map/ppermute | solution.py:38
  267.0 2.0 collective-permute-start.40
  269.6 1.8 collective-permute-start.42
  271.5 13.2 %attend_backward.3 = (bf16[1024,256]{1,0:T(8,128)(2,1)}, bf16[1024,256]{1,0:T(8,128)(2,1)}, bf16[1024,256]{1,0:T(8,128)(2,1)}, f32[8,256]{1,0:T(8,128)}) custom-call(s32[1024,1]{1,0:T(8,128)} %copy.32.seg_col, s32[1,1024]{1,0:T(1,128)} %seg_row.7, bf16[1024,2304]{1,0:T(8,128)(2,1)} %get-tuple-element.208.q_ref.k_ref.v_ref, ...), custom_call_target="tpu_custom_call" | custom-call | flops 1000000 | bytes 100000 | tf_op jit(solution)/shard_map/attend_backward/pallas_call | solution.py:160
  284.8 5.2 %weight_grad.7 = (bf16[4,4,48,384]{3,2,1,0:T(8,128)(2,1)}, bf16[4,4,48,384]{3,2,1,0:T(8,128)(2,1)}) custom-call(s32[3]{0:T(128)} %pad_add_fusion.1.spots, bf16[1024,768]{1,0:T(8,128)(2,1)} %get-tuple-element.276.x_ref, bf16[1024,256]{1,0:T(8,128)(2,1)} %get-tuple-element.322.rest_0_.rest_3_.q_ref, ...), custom_call_target="tpu_custom_call" | custom-call | flops 1000000 | bytes 100000 | tf_op jit(solution)/shard_map/weight_grad/pallas_call | solution.py:215
  291.6 2.0 convert_add_fusion.2
  296.7 8.4 %back_two.1 = (bf16[1024,768]{1,0:T(8,128)(2,1)}, f32[8,768]{1,0:T(8,128)}) custom-call(bf16[768,2304]{1,0:T(8,128)(2,1)} %get-tuple-element.238.w_ref, bf16[1024,256]{1,0:T(8,128)(2,1)} %get-tuple-element.322.rest_0_.rest_3_.q_ref, bf16[1024,256]{1,0:T(8,128)(2,1)} %get-tuple-element.323.rest_1_.rest_4_.k_ref, ...), custom_call_target="tpu_custom_call" | custom-call | flops 1000000 | bytes 100000 | tf_op jit(solution)/shard_map/back_two/pallas_call | solution.py:608
  305.1 1.6 pack.1
  306.7 7.6 %collective-permute-done.45 = bf16[2,4,48,384]{3,2,1,0:T(8,128)(2,1)} collective-permute-done((bf16[2,4,48,384]{3,2,1,0:T(8,128)(2,1)}, bf16[2,4,48,384]{3,2,1,0:T(8,128)(2,1)}, u32[]{:S(2)}, u32[]{:S(2)}) %collective-permute-start.45) | collective-permute-done | bytes 294944 | tf_op jit(solution)/shard_map/ppermute | solution.py:38
  318.2 6.4 %collective-permute-done.47 = bf16[4,48,384]{2,1,0:T(8,128)(2,1)S(1)} collective-permute-done((bf16[4,48,384]{2,1,0:T(8,128)(2,1)S(1)}, bf16[4,48,384]{2,1,0:T(8,128)(2,1)S(1)}, u32[]{:S(2)}, u32[]{:S(2)}) %collective-permute-start.47) | collective-permute-done | bytes 147488 | tf_op jit(solution)/shard_map/ppermute | solution.py:38
  326.1 3.1 collective-permute-start.51
  329.9 3.3 collective-permute-done.52
  334.9 2.6 collective-permute-done.53
  339.5 2.6 collective-permute-start.55
  342.7 2.4 collective-permute-start.57
  345.1 2.1 collective-permute-done.57
  347.2 2.2 collective-permute-start.58
  349.3 2.9 collective-permute-done.58
  353.4 2.8 settle.2
  356.3 2.8 settle.3
  361.9 2.9 settle_last.1
  (263 shorter events, 69.3 us)
Async XLA Ops:
  7.2 345.1 %all-gather.7.cloned.1.call-start = ((), (), s32[]{:S(2)}) async-start(), calls=%async_computation.1 | async-start | bytes 1327104 | tf_op jit(solution)/shard_map/all_gather | solution.py:830
  9.1 8.9 %collective-permute-start = (bf16[64,1152]{1,0:T(8,128)(2,1)S(1)}, bf16[64,1152]{1,0:T(8,128)(2,1)S(1)}, u32[]{:S(2)}, u32[]{:S(2)}) collective-permute-start(bf16[64,1152]{1,0:T(8,128)(2,1)S(1)} %fusion.22), channel_id=1, source_target_pairs={{0,1},{1,0},{2,3},{3,2},{4,5},{5,4},{6,7},{7,6},{8,9},{9,8},{10,11... | collective-permute-start | bytes 442376 | tf_op jit(solution)/shard_map/ppermute | solution.py:38
  12.2 14.0 %collective-permute-start.1 = (bf16[64,1152]{1,0:T(8,128)(2,1)S(1)}, bf16[64,1152]{1,0:T(8,128)(2,1)S(1)}, u32[]{:S(2)}, u32[]{:S(2)}) collective-permute-start(bf16[64,1152]{1,0:T(8,128)(2,1)S(1)} %fusion.22), channel_id=1, source_target_pairs={{0,2},{1,3},{2,0},{3,1},{4,6},{5,7},{6,4},{7,5},{8,10},{9,11},{10,... | collective-permute-start | bytes 442376 | tf_op jit(solution)/shard_map/ppermute | solution.py:38
  14.8 11.4 %collective-permute-start.2 = (bf16[64,1152]{1,0:T(8,128)(2,1)S(1)}, bf16[64,1152]{1,0:T(8,128)(2,1)S(1)}, u32[]{:S(2)}, u32[]{:S(2)}) collective-permute-start(bf16[64,1152]{1,0:T(8,128)(2,1)S(1)} %fusion.22), channel_id=1, source_target_pairs={{0,3},{1,2},{2,1},{3,0},{4,7},{5,6},{6,5},{7,4},{8,11},{9,10},{10,... | collective-permute-start | bytes 442376 | tf_op jit(solution)/shard_map/ppermute | solution.py:38
  26.9 10.7 %collective-permute-start.6 = (bf16[3,48,1152]{2,1,0:T(8,128)(2,1)S(1)}, bf16[3,48,1152]{2,1,0:T(8,128)(2,1)S(1)}, u32[]{:S(2)}, u32[]{:S(2)}) collective-permute-start(bf16[3,48,1152]{2,1,0:T(8,128)(2,1)S(1)} %pad_maximum_fusion.3.rest_0_), channel_id=1, source_target_pairs={{0,8},{4,12},{8,0},{12,4},{16,24},{20,28},{24,16},{28,20},{1,9},{5... | collective-permute-start | bytes 995336 | tf_op jit(solution)/shard_map/ppermute | solution.py:38
  28.5 13.9 %collective-permute-start.7 = (bf16[3,48,1152]{2,1,0:T(8,128)(2,1)S(1)}, bf16[3,48,1152]{2,1,0:T(8,128)(2,1)S(1)}, u32[]{:S(2)}, u32[]{:S(2)}) collective-permute-start(bf16[3,48,1152]{2,1,0:T(8,128)(2,1)S(1)} %pad_maximum_fusion.3.rest_0_), channel_id=1, source_target_pairs={{0,16},{4,20},{8,24},{12,28},{16,0},{20,4},{24,8},{28,12},{1,17},{... | collective-permute-start | bytes 995336 | tf_op jit(solution)/shard_map/ppermute | solution.py:38
  30.0 12.4 %collective-permute-start.8 = (bf16[3,48,1152]{2,1,0:T(8,128)(2,1)S(1)}, bf16[3,48,1152]{2,1,0:T(8,128)(2,1)S(1)}, u32[]{:S(2)}, u32[]{:S(2)}) collective-permute-start(bf16[3,48,1152]{2,1,0:T(8,128)(2,1)S(1)} %pad_maximum_fusion.3.rest_0_), channel_id=1, source_target_pairs={{0,24},{4,28},{8,16},{12,20},{16,8},{20,12},{24,0},{28,4},{1,25},{... | collective-permute-start | bytes 995336 | tf_op jit(solution)/shard_map/ppermute | solution.py:38
  30.5 12.5 %collective-permute-start.3 = (bf16[48,1920]{1,0:T(8,128)(2,1)S(1)}, bf16[48,1920]{1,0:T(8,128)(2,1)S(1)}, u32[]{:S(2)}, u32[]{:S(2)}) collective-permute-start(bf16[48,1920]{1,0:T(8,128)(2,1)S(1)} %pad_maximum_fusion.4), channel_id=1, source_target_pairs={{0,1},{1,0},{2,3},{3,2},{4,5},{5,4},{6,7},{7,6},{8,9},{9,8},{10,11... | collective-permute-start | bytes 552968 | tf_op jit(solution)/shard_map/ppermute | solution.py:38
  32.8 14.4 %collective-permute-start.4 = (bf16[48,1920]{1,0:T(8,128)(2,1)S(1)}, bf16[48,1920]{1,0:T(8,128)(2,1)S(1)}, u32[]{:S(2)}, u32[]{:S(2)}) collective-permute-start(bf16[48,1920]{1,0:T(8,128)(2,1)S(1)} %pad_maximum_fusion.4), channel_id=1, source_target_pairs={{0,2},{1,3},{2,0},{3,1},{4,6},{5,7},{6,4},{7,5},{8,10},{9,11},{10,... | collective-permute-start | bytes 552968 | tf_op jit(solution)/shard_map/ppermute | solution.py:38
  37.6 10.4 %collective-permute-start.5 = (bf16[48,1920]{1,0:T(8,128)(2,1)S(1)}, bf16[48,1920]{1,0:T(8,128)(2,1)S(1)}, u32[]{:S(2)}, u32[]{:S(2)}) collective-permute-start(bf16[48,1920]{1,0:T(8,128)(2,1)S(1)} %pad_maximum_fusion.4), channel_id=1, source_target_pairs={{0,3},{1,2},{2,1},{3,0},{4,7},{5,6},{6,5},{7,4},{8,11},{9,10},{10,... | collective-permute-start | bytes 552968 | tf_op jit(solution)/shard_map/ppermute | solution.py:38
  50.5 46.0 %collective-permute-start.16 = (bf16[3,48,1920]{2,1,0:T(8,128)(2,1)S(1)}, bf16[3,48,1920]{2,1,0:T(8,128)(2,1)S(1)}, u32[]{:S(2)}, u32[]{:S(2)}) collective-permute-start(bf16[3,48,1920]{2,1,0:T(8,128)(2,1)S(1)} %pad_maximum_fusion.1.rest_0_), channel_id=1, source_target_pairs={{0,8},{4,12},{8,0},{12,4},{16,24},{20,28},{24,16},{28,20},{1,9},{5... | collective-permute-start | bytes 1658888 | tf_op jit(solution)/shard_map/ppermute | solution.py:38
  52.0 44.6 %collective-permute-start.17 = (bf16[3,48,1920]{2,1,0:T(8,128)(2,1)S(1)}, bf16[3,48,1920]{2,1,0:T(8,128)(2,1)S(1)}, u32[]{:S(2)}, u32[]{:S(2)}) collective-permute-start(bf16[3,48,1920]{2,1,0:T(8,128)(2,1)S(1)} %pad_maximum_fusion.1.rest_0_), channel_id=1, source_target_pairs={{0,16},{4,20},{8,24},{12,28},{16,0},{20,4},{24,8},{28,12},{1,17},{... | collective-permute-start | bytes 1658888 | tf_op jit(solution)/shard_map/ppermute | solution.py:38
  53.5 43.1 %collective-permute-start.18 = (bf16[3,48,1920]{2,1,0:T(8,128)(2,1)S(1)}, bf16[3,48,1920]{2,1,0:T(8,128)(2,1)S(1)}, u32[]{:S(2)}, u32[]{:S(2)}) collective-permute-start(bf16[3,48,1920]{2,1,0:T(8,128)(2,1)S(1)} %pad_maximum_fusion.1.rest_0_), channel_id=1, source_target_pairs={{0,24},{4,28},{8,16},{12,20},{16,8},{20,12},{24,0},{28,4},{1,25},{... | collective-permute-start | bytes 1658888 | tf_op jit(solution)/shard_map/ppermute | solution.py:38
  57.5 31.5 %collective-permute-start.14 = (bf16[192,384]{1,0:T(8,128)(2,1)}, bf16[192,384]{1,0:T(8,128)(2,1)}, u32[]{:S(2)}, u32[]{:S(2)}) collective-permute-start(bf16[192,384]{1,0:T(8,128)(2,1)} %dynamic_slice.21), channel_id=1, source_target_pairs={{0,2},{1,3},{2,0},{3,1},{4,6},{5,7},{6,4},{7,5},{8,10},{9,11},{10,... | collective-permute-start | bytes 442376 | tf_op jit(solution)/shard_map/ppermute | solution.py:38
  60.9 28.0 %collective-permute-start.15 = (bf16[192,384]{1,0:T(8,128)(2,1)}, bf16[192,384]{1,0:T(8,128)(2,1)}, u32[]{:S(2)}, u32[]{:S(2)}) collective-permute-start(bf16[192,384]{1,0:T(8,128)(2,1)} %dynamic_slice.21), channel_id=1, source_target_pairs={{0,3},{1,2},{2,1},{3,0},{4,7},{5,6},{6,5},{7,4},{8,11},{9,10},{10,... | collective-permute-start | bytes 442376 | tf_op jit(solution)/shard_map/ppermute | solution.py:38
  98.8 25.2 %collective-permute-start.23 = (bf16[3,192,384]{2,1,0:T(8,128)(2,1)S(1)}, bf16[3,192,384]{2,1,0:T(8,128)(2,1)S(1)}, u32[]{:S(2)}, u32[]{:S(2)}) collective-permute-start(bf16[3,192,384]{2,1,0:T(8,128)(2,1)S(1)} %pad_maximum_fusion.2.rest_0_), channel_id=1, source_target_pairs={{0,8},{4,12},{8,0},{12,4},{16,24},{20,28},{24,16},{28,20},{1,9},{5... | collective-permute-start | bytes 1327112 | tf_op jit(solution)/shard_map/ppermute | solution.py:38
  99.9 24.1 %collective-permute-start.24 = (bf16[3,192,384]{2,1,0:T(8,128)(2,1)S(1)}, bf16[3,192,384]{2,1,0:T(8,128)(2,1)S(1)}, u32[]{:S(2)}, u32[]{:S(2)}) collective-permute-start(bf16[3,192,384]{2,1,0:T(8,128)(2,1)S(1)} %pad_maximum_fusion.2.rest_0_), channel_id=1, source_target_pairs={{0,16},{4,20},{8,24},{12,28},{16,0},{20,4},{24,8},{28,12},{1,17},{... | collective-permute-start | bytes 1327112 | tf_op jit(solution)/shard_map/ppermute | solution.py:38
  101.4 22.6 %collective-permute-start.25 = (bf16[3,192,384]{2,1,0:T(8,128)(2,1)S(1)}, bf16[3,192,384]{2,1,0:T(8,128)(2,1)}, u32[]{:S(2)}, u32[]{:S(2)}) collective-permute-start(bf16[3,192,384]{2,1,0:T(8,128)(2,1)S(1)} %pad_maximum_fusion.2.rest_0_), channel_id=1, source_target_pairs={{0,24},{4,28},{8,16},{12,20},{16,8},{20,12},{24,0},{28,4},{1,25},{... | collective-permute-start | bytes 1327112 | tf_op jit(solution)/shard_map/ppermute | solution.py:38
  124.0 12.6 %collective-permute-start.26 = (bf16[3,192,384]{2,1,0:T(8,128)(2,1)S(1)}, bf16[3,192,384]{2,1,0:T(8,128)(2,1)S(1)}, u32[]{:S(2)}, u32[]{:S(2)}) collective-permute-start(bf16[3,192,384]{2,1,0:T(8,128)(2,1)S(1)} %pad_maximum_fusion.2.rest_0_), channel_id=1, source_target_pairs={{0,4},{4,0},{8,12},{12,8},{16,20},{20,16},{24,28},{28,24},{1,5},{5... | collective-permute-start | bytes 1327112 | tf_op jit(solution)/shard_map/ppermute | solution.py:38
  124.1 12.5 %collective-permute-start.27 = (bf16[3,192,384]{2,1,0:T(8,128)(2,1)S(1)}, bf16[3,192,384]{2,1,0:T(8,128)(2,1)S(1)}, u32[]{:S(2)}, u32[]{:S(2)}) collective-permute-start(bf16[3,192,384]{2,1,0:T(8,128)(2,1)S(1)} %collective-permute-done.23.rest_1_), channel_id=1, source_target_pairs={{0,4},{4,0},{8,12},{12,8},{16,20},{20,16},{24,28},{28,24},{1,5},{5... | collective-permute-start | bytes 1327112 | tf_op jit(solution)/shard_map/ppermute | solution.py:38
  124.6 12.0 %collective-permute-start.28 = (bf16[3,192,384]{2,1,0:T(8,128)(2,1)S(1)}, bf16[3,192,384]{2,1,0:T(8,128)(2,1)S(1)}, u32[]{:S(2)}, u32[]{:S(2)}) collective-permute-start(bf16[3,192,384]{2,1,0:T(8,128)(2,1)S(1)} %collective-permute-done.24.rest_2_), channel_id=1, source_target_pairs={{0,4},{4,0},{8,12},{12,8},{16,20},{20,16},{24,28},{28,24},{1,5},{5... | collective-permute-start | bytes 1327112 | tf_op jit(solution)/shard_map/ppermute | solution.py:38
  124.7 12.0 %collective-permute-start.29 = (bf16[3,192,384]{2,1,0:T(8,128)(2,1)}, bf16[3,192,384]{2,1,0:T(8,128)(2,1)S(1)}, u32[]{:S(2)}, u32[]{:S(2)}) collective-permute-start(bf16[3,192,384]{2,1,0:T(8,128)(2,1)} %collective-permute-done.25.rest_3_), channel_id=1, source_target_pairs={{0,4},{4,0},{8,12},{12,8},{16,20},{20,16},{24,28},{28,24},{1,5},{5... | collective-permute-start | bytes 1327112 | tf_op jit(solution)/shard_map/ppermute | solution.py:38
  136.7 13.3 %collective-permute-start.30 = (bf16[4,4,192,384]{3,2,1,0:T(8,128)(2,1)}, bf16[4,4,192,384]{3,2,1,0:T(8,128)(2,1)S(1)}, u32[]{:S(2)}, u32[]{:S(2)}) collective-permute-start(bf16[4,4,192,384]{3,2,1,0:T(8,128)(2,1)} %get-tuple-element.242), channel_id=1, source_target_pairs={{0,4},{4,0},{8,12},{12,8},{16,20},{20,16},{24,28},{28,24},{1,5},{5... | collective-permute-start | bytes 7077896 | tf_op jit(solution)/shard_map/ppermute | solution.py:38
  151.4 28.0 %collective-permute-start.31 = (bf16[2,4,192,384]{3,2,1,0:T(8,128)(2,1)S(1)}, bf16[2,4,192,384]{3,2,1,0:T(8,128)(2,1)S(1)}, u32[]{:S(2)}, u32[]{:S(2)}) collective-permute-start(bf16[2,4,192,384]{3,2,1,0:T(8,128)(2,1)S(1)} %add_convert_fusion.1), channel_id=1, source_target_pairs={{0,8},{4,12},{8,0},{12,4},{16,24},{20,28},{24,16},{28,20},{1,9},{5... | collective-permute-start | bytes 3538952 | tf_op jit(solution)/shard_map/ppermute | solution.py:38
  179.4 19.8 %collective-permute-start.32 = (bf16[4,4,48,1536]{3,2,1,0:T(8,128)(2,1)}, bf16[4,4,48,1536]{3,2,1,0:T(8,128)(2,1)S(1)}, u32[]{:S(2)}, u32[]{:S(2)}) collective-permute-start(bf16[4,4,48,1536]{3,2,1,0:T(8,128)(2,1)} %get-tuple-element.258), channel_id=1, source_target_pairs={{0,4},{4,0},{8,12},{12,8},{16,20},{20,16},{24,28},{28,24},{1,5},{5... | collective-permute-start | bytes 7077896 | tf_op jit(solution)/shard_map/ppermute | solution.py:38
  181.9 18.7 %collective-permute-start.33 = (bf16[4,192,384]{2,1,0:T(8,128)(2,1)}, bf16[4,192,384]{2,1,0:T(8,128)(2,1)}, u32[]{:S(2)}, u32[]{:S(2)}) collective-permute-start(bf16[4,192,384]{2,1,0:T(8,128)(2,1)} %fusion.4), channel_id=1, source_target_pairs={{0,16},{4,20},{8,24},{12,28},{16,0},{20,4},{24,8},{28,12},{1,17},{... | collective-permute-start | bytes 1769480 | tf_op jit(solution)/shard_map/ppermute | solution.py:38
  200.6 28.2 %collective-permute-start.34 = (bf16[2,4,48,1536]{3,2,1,0:T(8,128)(2,1)S(1)}, bf16[2,4,48,1536]{3,2,1,0:T(8,128)(2,1)}, u32[]{:S(2)}, u32[]{:S(2)}) collective-permute-start(bf16[2,4,48,1536]{3,2,1,0:T(8,128)(2,1)S(1)} %add_convert_fusion), channel_id=1, source_target_pairs={{0,16},{4,20},{8,24},{12,28},{16,0},{20,4},{24,8},{28,12},{1,17},{... | collective-permute-start | bytes 3538952 | tf_op jit(solution)/shard_map/ppermute | solution.py:38
  232.2 14.2 %collective-permute-start.35 = (bf16[192,384]{1,0:T(8,128)(2,1)S(1)}, bf16[192,384]{1,0:T(8,128)(2,1)S(1)}, u32[]{:S(2)}, u32[]{:S(2)}) collective-permute-start(bf16[192,384]{1,0:T(8,128)(2,1)S(1)} %get-tuple-element.369), channel_id=1, source_target_pairs={{0,1},{1,0},{2,3},{3,2},{4,5},{5,4},{6,7},{7,6},{8,9},{9,8},{10,11... | collective-permute-start | bytes 442376 | tf_op jit(solution)/shard_map/ppermute | solution.py:38
  232.2 14.2 %collective-permute-start.36 = (bf16[192,384]{1,0:T(8,128)(2,1)S(1)}, bf16[192,384]{1,0:T(8,128)(2,1)S(1)}, u32[]{:S(2)}, u32[]{:S(2)}) collective-permute-start(bf16[192,384]{1,0:T(8,128)(2,1)S(1)} %get-tuple-element.368), channel_id=1, source_target_pairs={{0,2},{1,3},{2,0},{3,1},{4,6},{5,7},{6,4},{7,5},{8,10},{9,11},{10,... | collective-permute-start | bytes 442376 | tf_op jit(solution)/shard_map/ppermute | solution.py:38
  233.8 12.6 %collective-permute-start.37 = (bf16[192,384]{1,0:T(8,128)(2,1)S(1)}, bf16[192,384]{1,0:T(8,128)(2,1)S(1)}, u32[]{:S(2)}, u32[]{:S(2)}) collective-permute-start(bf16[192,384]{1,0:T(8,128)(2,1)S(1)} %get-tuple-element.367), channel_id=1, source_target_pairs={{0,3},{1,2},{2,1},{3,0},{4,7},{5,6},{6,5},{7,4},{8,11},{9,10},{10,... | collective-permute-start | bytes 442376 | tf_op jit(solution)/shard_map/ppermute | solution.py:38
  246.4 16.6 %collective-permute-start.38 = (bf16[4,4,48,1152]{3,2,1,0:T(8,128)(2,1)}, bf16[4,4,48,1152]{3,2,1,0:T(8,128)(2,1)}, u32[]{:S(2)}, u32[]{:S(2)}) collective-permute-start(bf16[4,4,48,1152]{3,2,1,0:T(8,128)(2,1)} %get-tuple-element.291), channel_id=1, source_target_pairs={{0,4},{4,0},{8,12},{12,8},{16,20},{20,16},{24,28},{28,24},{1,5},{5... | collective-permute-start | bytes 5308424 | tf_op jit(solution)/shard_map/ppermute | solution.py:38
  246.5 15.7 %collective-permute-start.39 = (bf16[4,48,1536]{2,1,0:T(8,128)(2,1)S(1)}, bf16[4,48,1536]{2,1,0:T(8,128)(2,1)S(1)}, u32[]{:S(2)}, u32[]{:S(2)}) collective-permute-start(bf16[4,48,1536]{2,1,0:T(8,128)(2,1)S(1)} %fusion.5), channel_id=1, source_target_pairs={{0,8},{4,12},{8,0},{12,4},{16,24},{20,28},{24,16},{28,20},{1,9},{5... | collective-permute-start | bytes 1769480 | tf_op jit(solution)/shard_map/ppermute | solution.py:38
  265.7 25.0 %collective-permute-start.43 = (bf16[2,4,48,1152]{3,2,1,0:T(8,128)(2,1)S(1)}, bf16[2,4,48,1152]{3,2,1,0:T(8,128)(2,1)S(1)}, u32[]{:S(2)}, u32[]{:S(2)}) collective-permute-start(bf16[2,4,48,1152]{3,2,1,0:T(8,128)(2,1)S(1)} %add_convert_fusion.2), channel_id=1, source_target_pairs={{0,16},{4,20},{8,24},{12,28},{16,0},{20,4},{24,8},{28,12},{1,17},{... | collective-permute-start | bytes 2654216 | tf_op jit(solution)/shard_map/ppermute | solution.py:38
  267.0 17.7 %collective-permute-start.40 = (bf16[48,1536]{1,0:T(8,128)(2,1)}, bf16[48,1536]{1,0:T(8,128)(2,1)S(1)}, u32[]{:S(2)}, u32[]{:S(2)}) collective-permute-start(bf16[48,1536]{1,0:T(8,128)(2,1)} %get-tuple-element.366), channel_id=1, source_target_pairs={{0,1},{1,0},{2,3},{3,2},{4,5},{5,4},{6,7},{7,6},{8,9},{9,8},{10,11... | collective-permute-start | bytes 442376 | tf_op jit(solution)/shard_map/ppermute | solution.py:38
  269.0 15.7 %collective-permute-start.41 = (bf16[48,1536]{1,0:T(8,128)(2,1)}, bf16[48,1536]{1,0:T(8,128)(2,1)S(1)}, u32[]{:S(2)}, u32[]{:S(2)}) collective-permute-start(bf16[48,1536]{1,0:T(8,128)(2,1)} %get-tuple-element.365), channel_id=1, source_target_pairs={{0,2},{1,3},{2,0},{3,1},{4,6},{5,7},{6,4},{7,5},{8,10},{9,11},{10,... | collective-permute-start | bytes 442376 | tf_op jit(solution)/shard_map/ppermute | solution.py:38
  269.6 15.2 %collective-permute-start.42 = (bf16[48,1536]{1,0:T(8,128)(2,1)S(1)}, bf16[48,1536]{1,0:T(8,128)(2,1)S(1)}, u32[]{:S(2)}, u32[]{:S(2)}) collective-permute-start(bf16[48,1536]{1,0:T(8,128)(2,1)S(1)} %get-tuple-element.364), channel_id=1, source_target_pairs={{0,3},{1,2},{2,1},{3,0},{4,7},{5,6},{6,5},{7,4},{8,11},{9,10},{10,... | collective-permute-start | bytes 442376 | tf_op jit(solution)/shard_map/ppermute | solution.py:38
  271.4 80.9 %all-gather.5.cloned.1.call-start = ((), (), s32[]{:S(2)}) async-start(), calls=%async_computation | async-start | bytes 1327104 | tf_op jit(solution)/shard_map/all_gather | solution.py:830
  293.8 20.5 %collective-permute-start.46 = (bf16[4,48,1152]{2,1,0:T(8,128)(2,1)S(1)}, bf16[4,48,1152]{2,1,0:T(8,128)(2,1)}, u32[]{:S(2)}, u32[]{:S(2)}) collective-permute-start(bf16[4,48,1152]{2,1,0:T(8,128)(2,1)S(1)} %fusion.6), channel_id=1, source_target_pairs={{0,8},{4,12},{8,0},{12,4},{16,24},{20,28},{24,16},{28,20},{1,9},{5... | collective-permute-start | bytes 1327112 | tf_op jit(solution)/shard_map/ppermute | solution.py:38
  295.7 18.6 %collective-permute-start.45 = (bf16[2,4,48,384]{3,2,1,0:T(8,128)(2,1)}, bf16[2,4,48,384]{3,2,1,0:T(8,128)(2,1)}, u32[]{:S(2)}, u32[]{:S(2)}) collective-permute-start(bf16[2,4,48,384]{3,2,1,0:T(8,128)(2,1)} %add_convert_fusion.3), channel_id=1, source_target_pairs={{0,8},{4,12},{8,0},{12,4},{16,24},{20,28},{24,16},{28,20},{1,9},{5... | collective-permute-start | bytes 884744 | tf_op jit(solution)/shard_map/ppermute | solution.py:38
  315.5 9.1 %collective-permute-start.47 = (bf16[4,48,384]{2,1,0:T(8,128)(2,1)S(1)}, bf16[4,48,384]{2,1,0:T(8,128)(2,1)S(1)}, u32[]{:S(2)}, u32[]{:S(2)}) collective-permute-start(bf16[4,48,384]{2,1,0:T(8,128)(2,1)S(1)} %fusion.23), channel_id=1, source_target_pairs={{0,16},{4,20},{8,24},{12,28},{16,0},{20,4},{24,8},{28,12},{1,17},{... | collective-permute-start | bytes 442376 | tf_op jit(solution)/shard_map/ppermute | solution.py:38
  324.7 12.7 %collective-permute-start.49 = (bf16[48,1536]{1,0:T(8,128)(2,1)S(1)}, bf16[48,1536]{1,0:T(8,128)(2,1)S(1)}, u32[]{:S(2)}, u32[]{:S(2)}) collective-permute-start(bf16[48,1536]{1,0:T(8,128)(2,1)S(1)} %get-tuple-element.363), channel_id=1, source_target_pairs={{0,1},{1,0},{2,3},{3,2},{4,5},{5,4},{6,7},{7,6},{8,9},{9,8},{10,11... | collective-permute-start | bytes 442376 | tf_op jit(solution)/shard_map/ppermute | solution.py:38
  325.6 13.2 %collective-permute-start.50 = (bf16[48,1536]{1,0:T(8,128)(2,1)S(1)}, bf16[48,1536]{1,0:T(8,128)(2,1)S(1)}, u32[]{:S(2)}, u32[]{:S(2)}) collective-permute-start(bf16[48,1536]{1,0:T(8,128)(2,1)S(1)} %get-tuple-element.362), channel_id=1, source_target_pairs={{0,2},{1,3},{2,0},{3,1},{4,6},{5,7},{6,4},{7,5},{8,10},{9,11},{10,... | collective-permute-start | bytes 442376 | tf_op jit(solution)/shard_map/ppermute | solution.py:38
  326.1 12.6 %collective-permute-start.51 = (bf16[48,1536]{1,0:T(8,128)(2,1)S(1)}, bf16[48,1536]{1,0:T(8,128)(2,1)S(1)}, u32[]{:S(2)}, u32[]{:S(2)}) collective-permute-start(bf16[48,1536]{1,0:T(8,128)(2,1)S(1)} %get-tuple-element.361), channel_id=1, source_target_pairs={{0,3},{1,2},{2,1},{3,0},{4,7},{5,6},{6,5},{7,4},{8,11},{9,10},{10,... | collective-permute-start | bytes 442376 | tf_op jit(solution)/shard_map/ppermute | solution.py:38
  338.8 13.4 %collective-permute-start.54 = (bf16[48,1536]{1,0:T(8,128)(2,1)S(1)}, bf16[48,1536]{1,0:T(8,128)(2,1)S(1)}, u32[]{:S(2)}, u32[]{:S(2)}) collective-permute-start(bf16[48,1536]{1,0:T(8,128)(2,1)S(1)} %fusion.12.rest_0_), channel_id=1, source_target_pairs={{0,8},{4,12},{8,0},{12,4},{16,24},{20,28},{24,16},{28,20},{1,9},{5... | collective-permute-start | bytes 442376 | tf_op jit(solution)/shard_map/ppermute | solution.py:38
  339.5 12.8 %collective-permute-start.55 = (bf16[48,1536]{1,0:T(8,128)(2,1)S(1)}, bf16[48,1536]{1,0:T(8,128)(2,1)S(1)}, u32[]{:S(2)}, u32[]{:S(2)}) collective-permute-start(bf16[48,1536]{1,0:T(8,128)(2,1)S(1)} %fusion.12.rest_0_), channel_id=1, source_target_pairs={{0,16},{4,20},{8,24},{12,28},{16,0},{20,4},{24,8},{28,12},{1,17},{... | collective-permute-start | bytes 442376 | tf_op jit(solution)/shard_map/ppermute | solution.py:38
  342.0 10.3 %collective-permute-start.56 = (bf16[48,1536]{1,0:T(8,128)(2,1)S(1)}, bf16[48,1536]{1,0:T(8,128)(2,1)S(1)}, u32[]{:S(2)}, u32[]{:S(2)}) collective-permute-start(bf16[48,1536]{1,0:T(8,128)(2,1)S(1)} %fusion.12.rest_0_), channel_id=1, source_target_pairs={{0,24},{4,28},{8,16},{12,20},{16,8},{20,12},{24,0},{28,4},{1,25},{... | collective-permute-start | bytes 442376 | tf_op jit(solution)/shard_map/ppermute | solution.py:38
  352.3 8.1 %collective-permute-start.59 = (bf16[48,1536]{1,0:T(8,128)(2,1)S(1)}, bf16[48,1536]{1,0:T(8,128)(2,1)S(1)}, u32[]{:S(2)}, u32[]{:S(2)}) collective-permute-start(bf16[48,1536]{1,0:T(8,128)(2,1)S(1)} %fusion.12.rest_0_), channel_id=1, source_target_pairs={{0,4},{4,0},{8,12},{12,8},{16,20},{20,16},{24,28},{28,24},{1,5},{5... | collective-permute-start | bytes 442376 | tf_op jit(solution)/shard_map/ppermute | solution.py:38
  352.4 8.1 %collective-permute-start.60 = (bf16[48,1536]{1,0:T(8,128)(2,1)S(1)}, bf16[48,1536]{1,0:T(8,128)(2,1)S(1)}, u32[]{:S(2)}, u32[]{:S(2)}) collective-permute-start(bf16[48,1536]{1,0:T(8,128)(2,1)S(1)} %collective-permute-done.54.rest_1_), channel_id=1, source_target_pairs={{0,4},{4,0},{8,12},{12,8},{16,20},{20,16},{24,28},{28,24},{1,5},{5... | collective-permute-start | bytes 442376 | tf_op jit(solution)/shard_map/ppermute | solution.py:38
  (65 other events, 479.6 us)
Sparse Core Ops, SparseCore 0:
  271.6 24.9 all-gather.6
  298.5 27.9 all-gather.4

commit v3 on v2

--- a/solution.py
+++ b/solution.py
@@ -418,7 +418,7 @@
 
 def fc_kernel(shards, pieces, spots, att_ref, x_ref, vec_ref, bias_ref, own_out, own_fc, *rest):
     parts = rest[: 2 * pieces]
-    wo_ref, wf_ref, resid_ref, norm_ref, pre_ref, gelu_ref, sems_out, sems_fc = rest[2 * pieces :]
+    wo_ref, wf_ref, resid_ref, norm_ref, slope_ref, gelu_ref, sems_out, sems_fc = rest[2 * pieces :]
     half = own_out.shape[1] // 2
     copies_out = piece_copies(wo_ref, own_out, parts, 0, spots, sems_out, shards, pieces)
     copies_fc = piece_copies(wf_ref, own_fc, parts, half, spots, sems_fc, shards, pieces)
@@ -431,12 +431,16 @@
     norm_ref[...] = norm_two
     at_first(lambda: wait_all(copies_fc))
     width = norm_two.shape[1]
-    for tile in range(pre_ref.shape[1] // width):
+    for tile in range(slope_ref.shape[1] // width):
         here = slice(tile * width, (tile + 1) * width)
         pre = dot_nn(norm_two, wf_ref[:, here]) + bias_ref[:, here]
-        pre_ref[:, here] = pre
-        curve = jnp.tanh(GELU_SCALE * (pre + GELU_CUBE * pre * pre * pre))
-        gelu_ref[:, here] = (0.5 * pre * (1.0 + curve)).astype(BF16)
+        square = pre * pre
+        curve = jnp.tanh(pre * (GELU_SCALE + (GELU_SCALE * GELU_CUBE) * square))
+        above = 0.5 + 0.5 * curve
+        gelu_ref[:, here] = (pre * above).astype(BF16)
+        bend = pre * (0.5 - 0.5 * curve * curve)
+        slope = above + bend * (GELU_SCALE + (3.0 * GELU_SCALE * GELU_CUBE) * square)
+        slope_ref[:, here] = slope.astype(BF16)
 
 
 def proj_kernel(shards, pieces, spots, gelu_ref, resid_ref, vec_ref, own_ref, *rest):
@@ -461,21 +465,15 @@
     return jnp.sum(values, axis=0, keepdims=True)
 
 
-def back_gelu_kernel(spots, g_ref, pre_ref, w_ref, grad_ref, fc_sums, proj_sums):
+def back_gelu_kernel(spots, g_ref, slope_ref, w_ref, grad_ref, fc_sums, proj_sums):
     clear_first(fc_sums)
     clear_first(proj_sums)
     grad = g_ref[...]
     proj_sums[0:1, :] += column_sums(grad.astype(F32))
     width = grad.shape[1]
-    for tile in range(pre_ref.shape[1] // width):
+    for tile in range(slope_ref.shape[1] // width):
         here = slice(tile * width, (tile + 1) * width)
-        pre = pre_ref[:, here]
-        square = pre * pre
-        curve = jnp.tanh(GELU_SCALE * (pre + GELU_CUBE * square * pre))
-        slope = 0.5 * (1.0 + curve) + (0.5 * GELU_SCALE) * pre * (1.0 - curve * curve) * (
-            1.0 + (3.0 * GELU_CUBE) * square
-        )
-        grad_pre = (dot_nt(grad, w_ref[here, :]) * slope).astype(BF16)
+        grad_pre = (dot_nt(grad, w_ref[here, :]) * slope_ref[:, here].astype(F32)).astype(BF16)
         grad_ref[:, here] = grad_pre
         fc_sums[0:1, here] += column_sums(grad_pre.astype(F32))
 
@@ -730,12 +728,6 @@
     qkv_slots, second_payload = tie((qkv_slots, second_payload))
     qkv_parts = across_chips(jnp.stack([slot[:piece_rows] for slot in qkv_slots]), 2)
     second_slots = along_shard(second_payload)
-    qkv_parts, proj_piece = tie((qkv_parts, own_piece(proj_weight)))
-    qkv_parts = across_cores(qkv_parts)
-    second_stack, qkv_parts, proj_piece = tie((jnp.stack(second_slots), qkv_parts, proj_piece))
-    second_parts = across_chips(second_stack, 2)
-    proj_slots = along_shard(proj_piece)
-
     rows_of = [small] + [slot[piece_rows : piece_rows + small_rows] for slot in qkv_slots]
     ordered = []
     for index in range(shards):
@@ -747,6 +739,12 @@
     bias_fc = vectors[:, 8 * shard_rows :].reshape(1, -1)
     vectors = vectors[:, : 8 * shard_rows].reshape(shards, 8, shard_rows)
     vectors = vectors.transpose(1, 0, 2).reshape(8, width)
+    qkv_parts, proj_piece, vectors, bias_fc = tie(
+        (qkv_parts, own_piece(proj_weight), vectors, bias_fc)
+    )
+    qkv_parts = across_cores(qkv_parts)
+    second_stack, qkv_parts = tie((jnp.stack(second_slots), qkv_parts))
+    second_parts = across_chips(second_stack, 2)
 
     seg_row = segment[0]
     length = hidden_in.shape[0]
@@ -771,13 +769,14 @@
         sem_count,
     )
     attended_one, lse_one = attend_forward(qkv, seg_row, 0, 4)
-    attended_one, proj_slots, qkv = tie((attended_one, proj_slots, qkv))
+    attended_one, proj_piece, qkv, second_parts = tie((attended_one, proj_piece, qkv, second_parts))
+    proj_slots = along_shard(proj_piece)
+    attended_two, lse_two = attend_forward(qkv, seg_row, 4, 2)
+    attended_two, second_parts, proj_slots = tie((attended_two, second_parts, proj_slots))
+    second_parts = across_cores(second_parts)
     proj_parts = across_chips(jnp.stack(proj_slots), 4)
-    attended_two, lse_two = attend_forward(qkv, seg_row, 4, 2)
-    attended_two, second_parts = tie((attended_two, second_parts))
-    second_parts = across_cores(second_parts)
     attended = jnp.concatenate([attended_one, attended_two], axis=1)
-    w_out, w_fc, resid, norm_two, pre_act, gelu_low = row_call(
+    w_out, w_fc, resid, norm_two, slope, gelu_low = row_call(
         kernel_of(fc_kernel),
         "fc",
         steps,
@@ -790,7 +789,7 @@
             ((width, ff), BF16, False),
             ((length, width), F32, True),
             ((length, width), BF16, True),
-            ((length, ff), F32, True),
+            ((length, ff), BF16, True),
             ((length, ff), BF16, True),
         ],
         2,
@@ -857,7 +856,7 @@
         "back_gelu",
         steps,
         spots,
-        [cotangent, pre_act],
+        [cotangent, slope],
         [w_proj],
         [],
         [((length, ff), BF16, True), ((8, ff), F32, False), ((8, width), F32, False)],
@@ -901,20 +900,22 @@
     fc_onward, heads_one = tie((fc_onward, heads_one))
     fc_came = second_swap(fc_onward, 2)
     one_far, one_near = grad_heads(norm_one, heads_one, *call, first_of, (attended, grad_branch))
-    heads_one, one_far, one_near, proj_shards = tie((heads_one, one_far, one_near, proj_shards))
+    heads_one, one_far, one_near, proj_shards, fc_came = tie(
+        (heads_one, one_far, one_near, proj_shards, fc_came)
+    )
     one_old = swap(one_far, "rep", reps, 1)
     proj_piece = shard_total(proj_held, proj_shards)
-    proj_piece, heads_one = tie((proj_piece, heads_one))
+    fc_held = fc_held + fc_came.astype(F32)
+    proj_piece, heads_one, fc_held = tie((proj_piece, heads_one, fc_held))
+    fc_shards = shard_swaps(fc_held)
     part_one = back_one(w_qkv, heads_one)
-    part_one, one_old, grad_attended, fc_came = tie((part_one, one_old, grad_attended, fc_came))
+    part_one, one_old, grad_attended = tie((part_one, one_old, grad_attended))
     one_send = sent_part(one_near, one_old)
-    fc_held = fc_held + fc_came.astype(F32)
-    one_send, grad_attended, fc_held = tie((one_send, grad_attended, fc_held))
+    one_send, grad_attended = tie((one_send, grad_attended))
     one_came = swap(one_send, "rep", reps, first_of)
-    fc_shards = shard_swaps(fc_held)
     *heads_two, sums_two = attend_backward(qkv, seg_row, grad_attended, lse_two, 4, 2)
     heads_two, fc_shards = tie((heads_two, fc_shards))
-    two_far, two_near = grad_heads(norm_one, heads_two, *call, 2)
+    two_far, two_near = grad_heads(norm_one, heads_two, *call, first_of)
     heads_two, two_far, two_near, one_came = tie((heads_two, two_far, two_near, one_came))
     two_old = swap(two_far, "rep", reps, 1)
     one_held, one_onward = after_first(one_near, one_old, one_came)
@@ -923,39 +924,48 @@
     one_came = second_swap(one_onward, 2)
     two_send = sent_part(two_near, two_old)
     two_send, heads_two = tie((two_send, heads_two))
-    two_came = swap(two_send, "rep", reps, 2)
+    two_came = swap(two_send, "rep", reps, first_of)
     input_grad, ln1_sums = back_two(
         w_qkv, heads_two, 128 * 4, part_one, hidden_in, vectors, grad_resid
     )
     small_grads = pack(ln1_sums, sums_one, sums_two, resid_sums, proj_sums, fc_sums)
-    masks = [("rep", reps, 1 << i) for i in range(reps.bit_length() - 1)]
-    masks += [("shard", shards, 1 << i) for i in range(shards.bit_length() - 1)]
+    masks = [1 << i for i in range(reps.bit_length() - 1)]
 
     def vector_step(total, count=1):
-        for _ in range(count):
-            axis, size, mask = masks.pop(0)
-            total = total + swap(total, axis, size, mask)
+        for mask in masks[:count]:
+            total = total + swap(total, "rep", reps, mask)
+        del masks[:count]
         return total
 
+    small_grads = vector_step(small_grads)
     two_came, one_came, small_grads = tie((two_came, one_came, small_grads))
     two_held, two_onward = after_first(two_near, two_old, two_came)
     two_onward, small_grads = tie((two_onward, small_grads))
-    two_came = second_swap(two_onward, 4)
+    two_came = second_swap(two_onward, 2)
     one_held = one_held + one_came.astype(F32)
+    one_shards = shard_swaps(one_held)
     small_grads = vector_step(small_grads)
+    every_fc, every_proj = every_owner(fc_piece), every_owner(proj_piece)
     two_came, one_held, small_grads = tie((two_came, one_held, small_grads))
-    last_held = jnp.concatenate([one_held, two_held + two_came.astype(F32)], axis=-1)
-    last_shards = shard_swaps(last_held)
-    small_grads = vector_step(small_grads, 2)
-    last_shards, small_grads = tie((last_shards, small_grads))
-    last_parts = across_chips(shard_total(last_held, last_shards), 2)
+    two_held = two_held + two_came.astype(F32)
+    two_shards = shard_swaps(two_held)
     small_grads = vector_step(small_grads, len(masks))
-    last_parts, small_grads, every_fc, every_proj = tie(
-        (last_parts, small_grads, every_owner(fc_piece), every_owner(proj_piece))
-    )
-    last_parts = across_cores(last_parts)
+    two_shards, one_shards, small_grads, every_fc, every_proj = tie(
+        (two_shards, one_shards, small_grads, every_fc, every_proj)
+    )
+    last_piece = jnp.concatenate(
+        [shard_total(one_held, one_shards), shard_total(two_held, two_shards)], axis=-1
+    )
+    last_parts = across_chips(last_piece, 2)
+    small_shards = along_shard(small_grads)
     (d_fc_weight,) = settle(every_fc, (fc_weight.shape[1],), pieces)
     (d_proj_weight,) = settle(every_proj, (width,), pieces)
+    last_parts, small_shards, d_fc_weight, d_proj_weight = tie(
+        (last_parts, small_shards, d_fc_weight, d_proj_weight)
+    )
+    last_parts = across_cores(last_parts)
+    for value in small_shards:
+        small_grads = small_grads + value
     d_qkv_weight, d_out_weight = settle_last(
         last_parts, spots, pieces, heads_one[0].shape[1] // 2, width
     )

time: 376 us -> 357 us (0.949)
  waiting for transfers between devices: 55.5 us -> 40.9 us
    ppermute x63 -> x67, waiting for transfers between devices: 55.4 us -> 40.9 us  [swap(): return lax.ppermute(value, axis, [(i, i ^ mask) for i in range(size)])]
    unnamed x102 -> x100, local copies, waits for them, and re-layouts: 10.8 us -> 9.01 us
    ppermute x63 -> x67, starting transfers between devices: 65.6 us -> 66 us  [swap(): return lax.ppermute(value, axis, [(i, i ^ mask) for i in range(size)])]
  transfers between devices with their start and end apart: 65 -> 69, of which waited for: 16 -> 15; matrix products, arithmetic and copies ran while one was open for 6% -> 6% of each run, Pallas kernels for 52% -> 54%
where the time goes in v3:
time: 357 us; the launch traced here: 353 us
  Pallas kernels  194 us (54%)
  starting transfers between devices  66 us (18%)
  waiting for transfers between devices  40.9 us (11%)
  other arithmetic  18.7 us (5%)
  local copies, waits for them, and re-layouts  18.3 us (5%)
  between operations  15.3 us (4%)
    pallas_call x5, Pallas kernels, row_call(): pl.pallas_call(kernel, grid_spec=pltpu.PrefetchScalarGridSpec(num_scalar_...  72.1 us
    ppermute x67, starting transfers between devices, swap(): return lax.ppermute(value, axis, [(i, i ^ mask) for i in range(size)])  66 us
    ppermute x67, waiting for transfers between devices, swap(): return lax.ppermute(value, axis, [(i, i ^ mask) for i in range(size)])  40.9 us
    pallas_call x2, Pallas kernels, attend_backward(): pl.pallas_call(functools.partial(attend_back_kernel, rows), grid=(count,)...  37.6 us
    pallas_call x4, Pallas kernels, grad_call(): pl.pallas_call(kernel, grid_spec=pltpu.PrefetchScalarGridSpec(num_scalar_...  37.3 us
    pallas_call x2, Pallas kernels, attend_forward(): pl.pallas_call(functools.partial(attend_kernel, rows), grid=(count,), in_...  20.4 us
    unnamed x100, local copies, waits for them, and re-layouts  9.01 us
    pallas_call x1, Pallas kernels, back_two(): pl.pallas_call(functools.partial(back_two_kernel, start), grid=(4,), in_s...  8.5 us
  transfers between devices with their start and end apart: 69, of which 15 were waited for; matrix products, arithmetic and copies ran while one was open for 6% of the time, Pallas kernels for 54%

profile of v3, /device:TPU:0, one launch (start us, length us, event | category | flops | bytes accessed | tf_op | source)
XLA Modules:
  0.0 352.9 jit_solution(8405438867974173251)
XLA Ops:
  9.1 3.1 collective-permute-start
  12.2 2.6 collective-permute-start.1
  16.5 1.6 dynamic_slice.21
  18.1 8.1 %collective-permute-done.1 = bf16[64,1152]{1,0:T(8,128)(2,1)S(1)} collective-permute-done((bf16[64,1152]{1,0:T(8,128)(2,1)S(1)}, bf16[64,1152]{1,0:T(8,128)(2,1)S(1)}, u32[]{:S(2)}, u32[]{:S(2)}) %collective-permute-start.1) | collective-permute-done | bytes 147488 | tf_op jit(solution)/shard_map/ppermute | solution.py:38
  26.2 2.3 collective-permute-start.8
  28.4 1.6 collective-permute-start.6
  30.1 1.6 collective-permute-start.3
  33.9 7.1 %collective-permute-done.3.rest_1_ = bf16[3,48,1152]{2,1,0:T(8,128)(2,1)S(1)} collective-permute-done((bf16[3,48,1152]{2,1,0:T(8,128)(2,1)S(1)}, bf16[3,48,1152]{2,1,0:T(8,128)(2,1)S(1)}, u32[]{:S(2)}, u32[]{:S(2)}) %collective-permute-start.3) | collective-permute-done | bytes 331808 | tf_op jit(solution)/shard_map/ppermute | solution.py:38
  42.9 3.7 %collective-permute-done.4.rest_2_ = bf16[3,48,1152]{2,1,0:T(8,128)(2,1)S(1)} collective-permute-done((bf16[3,48,1152]{2,1,0:T(8,128)(2,1)S(1)}, bf16[3,48,1152]{2,1,0:T(8,128)(2,1)S(1)}, u32[]{:S(2)}, u32[]{:S(2)}) %collective-permute-start.4) | collective-permute-done | bytes 331808 | tf_op jit(solution)/shard_map/ppermute | solution.py:38
  47.6 1.7 collective-permute-done.7
  57.3 11.2 %qkv.1 = (bf16[768,2304]{1,0:T(8,128)(2,1)}, bf16[1024,768]{1,0:T(8,128)(2,1)}, bf16[1024,2304]{1,0:T(8,128)(2,1)}) custom-call(s32[3]{0:T(128)} %pad_add_fusion.1.spots, bf16[1024,768]{1,0:T(8,128)(2,1)} %x_ref.5, f32[8,768]{1,0:T(8,128)} %reshape.51.vec_ref, bf16[192,2304]{1,0:T(8,128)(2,1)} %own_ref.2, bf16[3,48,1152]{2,1,0:T(8,128)(2,1)} %copy-done.8, ...), custom_call_target="tpu_custom_call" | custom-call | flops 1000000 | bytes 100000 | tf_op jit(solution)/shard_map/qkv/pallas_call | solution.py:358
  68.5 12.9 %attend_forward.2 = (bf16[1024,512]{1,0:T(8,128)(2,1)}, f32[8,8,1024]{2,1,0:T(8,128)}) custom-call(s32[1024,1]{1,0:T(8,128)} %copy.32.seg_col, s32[1,1024]{1,0:T(1,128)} %seg_row.7, bf16[1024,2304]{1,0:T(8,128)(2,1)} %get-tuple-element.222.q_ref.k_ref.v_ref, bf16[1024,2304]{1,0:T(8,128)(2,1)} %get-tuple-element.222.q_ref.k_ref.v_ref, ...), custom_call_target="tpu_custom_call" | custom-call | flops 1000000 | bytes 100000 | tf_op jit(solution)/shard_map/attend_forward/pallas_call | solution.py:93
  81.6 2.0 collective-permute-start.17
  83.6 2.4 collective-permute-start.18
  86.0 7.5 %attend_forward.3 = (bf16[1024,256]{1,0:T(8,128)(2,1)}, f32[4,8,1024]{2,1,0:T(8,128)}) custom-call(s32[1024,1]{1,0:T(8,128)} %copy.32.seg_col, s32[1,1024]{1,0:T(1,128)} %seg_row.7, bf16[1024,2304]{1,0:T(8,128)(2,1)} %get-tuple-element.222.q_ref.k_ref.v_ref, bf16[1024,2304]{1,0:T(8,128)(2,1)} %get-tuple-element.222.q_ref.k_ref.v_ref, ...), custom_call_target="tpu_custom_call" | custom-call | flops 1000000 | bytes 100000 | tf_op jit(solution)/shard_map/attend_forward/pallas_call | solution.py:93
  101.3 21.2 %fc.1 = (bf16[768,768]{1,0:T(8,128)(2,1)}, bf16[768,3072]{1,0:T(8,128)(2,1)}, f32[1024,768]{1,0:T(8,128)}, bf16[1024,768]{1,0:T(8,128)(2,1)}, bf16[1024,3072]{1,0:T(8,128)(2,1)}, /*index=5*/bf16[1024,3072]{1,0:T(8,128)(2,1)}) custom-call(s32[3]{0:T(128)} %pad_add_fusion.1.spots, bf16[1024,768]{1,0:T(8,128)(2,1)} %copy-done, bf16[1024,768]{1,0:T(8,128)(2,1)} %x_ref.5, ...), custom_call_target="tpu_custom_call" | custom-call | flops 1000000 | bytes 100000 | tf_op jit(solution)/shard_map/fc/pallas_call | solution.py:358
  123.7 11.4 %weight_grad.4 = (bf16[4,4,192,384]{3,2,1,0:T(8,128)(2,1)}, bf16[4,4,192,384]{3,2,1,0:T(8,128)(2,1)}) custom-call(s32[3]{0:T(128)} %pad_add_fusion.1.spots, bf16[1024,3072]{1,0:T(8,128)(2,1)} %get-tuple-element.246.x_ref.gelu_ref, bf16[1024,768]{1,0:T(8,128)(2,1)} %g_ref.3, bf16[1024,768]{1,0:T(8,128)(2,1)} %g_ref.3), custom_call_target="tpu_custom_call" | custom-call | flops 1000000 | bytes 100000 | tf_op jit(solution)/shard_map/weight_grad/pallas_call | solution.py:215
  136.4 12.1 %proj.1 = (bf16[3072,768]{1,0:T(8,128)(2,1)}, bf16[1024,768]{1,0:T(8,128)(2,1)}) custom-call(s32[3]{0:T(128)} %pad_add_fusion.1.spots, bf16[1024,3072]{1,0:T(8,128)(2,1)} %get-tuple-element.246.x_ref.gelu_ref, f32[1024,768]{1,0:T(8,128)} %get-tuple-element.247.resid_ref, f32[8,768]{1,0:T(8,128)} %reshape.51.vec_ref, bf16[768,768]{1,0:T(8,128)(2,1)} %own_ref.3, ...), custom_call_target="tpu_custom_call" | custom-call | flops 1000000 | bytes 100000 | tf_op jit(solution)/shard_map/proj/pallas_call | solution.py:358
  151.0 11.7 %back_gelu.1 = (bf16[1024,3072]{1,0:T(8,128)(2,1)}, f32[8,3072]{1,0:T(8,128)}, f32[8,768]{1,0:T(8,128)}) custom-call(s32[3]{0:T(128)} %pad_add_fusion.1.spots, bf16[1024,768]{1,0:T(8,128)(2,1)} %g_ref.3, bf16[1024,3072]{1,0:T(8,128)(2,1)} %get-tuple-element.258.slope_ref, bf16[3072,768]{1,0:T(8,128)(2,1)} %get-tuple-element.264.w_ref), custom_call_target="tpu_custom_call" | custom-call | flops 1000000 | bytes 100000 | tf_op jit(solution)/shard_map/back_gelu/pallas_call | solution.py:358
  162.7 11.1 %weight_grad.5 = (bf16[4,4,48,1536]{3,2,1,0:T(8,128)(2,1)}, bf16[4,4,48,1536]{3,2,1,0:T(8,128)(2,1)}) custom-call(s32[3]{0:T(128)} %pad_add_fusion.1.spots, bf16[1024,768]{1,0:T(8,128)(2,1)} %get-tuple-element.266.x_ref, bf16[1024,3072]{1,0:T(8,128)(2,1)} %get-tuple-element.273.far_y.near_y.pre_ref, bf16[1024,3072]{1,0:T(8,128)(2,1)} %get-tuple-element.273.far_y.near_y.pre_ref), custom_call_target="tpu_custom_call" | custom-call | flops 1000000 | bytes 100000 | tf_op jit(solution)/shard_map/weight_grad/pallas_call | solution.py:215
  173.8 4.1 %collective-permute-done.31 = bf16[2,4,192,384]{3,2,1,0:T(8,128)(2,1)S(1)} collective-permute-done((bf16[2,4,192,384]{3,2,1,0:T(8,128)(2,1)S(1)}, bf16[2,4,192,384]{3,2,1,0:T(8,128)(2,1)S(1)}, u32[]{:S(2)}, u32[]{:S(2)}) %collective-permute-start.31) | collective-permute-done | bytes 1179680 | tf_op jit(solution)/shard_map/ppermute | solution.py:38
  177.9 1.7 convert_add_fusion.1
  181.8 15.9 %back_norm.1 = (f32[1024,768]{1,0:T(8,128)}, bf16[1024,768]{1,0:T(8,128)(2,1)}, bf16[1024,768]{1,0:T(8,128)(2,1)}, f32[8,768]{1,0:T(8,128)}) custom-call(s32[3]{0:T(128)} %pad_add_fusion.1.spots, bf16[1024,3072]{1,0:T(8,128)(2,1)} %get-tuple-element.273.far_y.near_y.pre_ref, f32[1024,768]{1,0:T(8,128)} %get-tuple-element.247.resid_ref, ...), custom_call_target="tpu_custom_call" | custom-call | flops 1000000 | bytes 100000 | tf_op jit(solution)/shard_map/back_norm/pallas_call | solution.py:358
  199.8 24.3 %attend_backward.2 = (bf16[1024,512]{1,0:T(8,128)(2,1)}, bf16[1024,512]{1,0:T(8,128)(2,1)}, bf16[1024,512]{1,0:T(8,128)(2,1)}, f32[8,512]{1,0:T(8,128)}) custom-call(s32[1024,1]{1,0:T(8,128)} %copy.32.seg_col, s32[1,1024]{1,0:T(1,128)} %seg_row.7, bf16[1024,2304]{1,0:T(8,128)(2,1)} %get-tuple-element.222.q_ref.k_ref.v_ref, ...), custom_call_target="tpu_custom_call" | custom-call | flops 1000000 | bytes 100000 | tf_op jit(solution)/shard_map/attend_backward/pallas_call | solution.py:160
  224.0 3.2 collective-permute-done.34
  227.2 1.7 convert_add_fusion
  231.4 2.2 collective-permute-start.35
  233.6 2.4 collective-permute-start.37
  236.0 9.7 %weight_grad.6 = (bf16[4,4,48,1152]{3,2,1,0:T(8,128)(2,1)}, bf16[4,4,48,1152]{3,2,1,0:T(8,128)(2,1)}) custom-call(s32[3]{0:T(128)} %pad_add_fusion.1.spots, bf16[1024,768]{1,0:T(8,128)(2,1)} %get-tuple-element.295.x_ref, bf16[1024,512]{1,0:T(8,128)(2,1)} %get-tuple-element.309.rest_0_.rest_3_.q_ref, ...), custom_call_target="tpu_custom_call" | custom-call | flops 1000000 | bytes 100000 | tf_op jit(solution)/shard_map/weight_grad/pallas_call | solution.py:215
  248.5 7.4 %back_one.1.part_ref = f32[1024,768]{1,0:T(8,128)} custom-call(bf16[768,2304]{1,0:T(8,128)(2,1)} %get-tuple-element.257.w_ref, bf16[1024,512]{1,0:T(8,128)(2,1)} %get-tuple-element.309.rest_0_.rest_3_.q_ref, bf16[1024,512]{1,0:T(8,128)(2,1)} %get-tuple-element.310.rest_1_.rest_4_.k_ref, bf16[1024,512]{1,0:T(8,128)(2,1)} %get-tuple-element.311.rest_2_.rest_5_.v_ref), custom_call_target="tpu_custom_call" | custom-call | flops 1000000 | bytes 100000 | tf_op jit(solution)/shard_map/back_one/pallas_call | solution.py:589
  255.9 2.3 add_convert_fusion.2
  259.6 2.6 collective-permute-start.40
  262.2 2.4 collective-permute-start.42
  264.7 13.4 %attend_backward.3 = (bf16[1024,256]{1,0:T(8,128)(2,1)}, bf16[1024,256]{1,0:T(8,128)(2,1)}, bf16[1024,256]{1,0:T(8,128)(2,1)}, f32[8,256]{1,0:T(8,128)}) custom-call(s32[1024,1]{1,0:T(8,128)} %copy.32.seg_col, s32[1,1024]{1,0:T(1,128)} %seg_row.7, bf16[1024,2304]{1,0:T(8,128)(2,1)} %get-tuple-element.222.q_ref.k_ref.v_ref, ...), custom_call_target="tpu_custom_call" | custom-call | flops 1000000 | bytes 100000 | tf_op jit(solution)/shard_map/attend_backward/pallas_call | solution.py:160
  278.1 5.2 %weight_grad.7 = (bf16[4,4,48,384]{3,2,1,0:T(8,128)(2,1)}, bf16[4,4,48,384]{3,2,1,0:T(8,128)(2,1)}) custom-call(s32[3]{0:T(128)} %pad_add_fusion.1.spots, bf16[1024,768]{1,0:T(8,128)(2,1)} %get-tuple-element.295.x_ref, bf16[1024,256]{1,0:T(8,128)(2,1)} %get-tuple-element.341.rest_0_.rest_3_.q_ref, ...), custom_call_target="tpu_custom_call" | custom-call | flops 1000000 | bytes 100000 | tf_op jit(solution)/shard_map/weight_grad/pallas_call | solution.py:215
  284.0 1.8 convert_add_fusion.2
  289.4 8.5 %back_two.1 = (bf16[1024,768]{1,0:T(8,128)(2,1)}, f32[8,768]{1,0:T(8,128)}) custom-call(bf16[768,2304]{1,0:T(8,128)(2,1)} %get-tuple-element.257.w_ref, bf16[1024,256]{1,0:T(8,128)(2,1)} %get-tuple-element.341.rest_0_.rest_3_.q_ref, bf16[1024,256]{1,0:T(8,128)(2,1)} %get-tuple-element.342.rest_1_.rest_4_.k_ref, ...), custom_call_target="tpu_custom_call" | custom-call | flops 1000000 | bytes 100000 | tf_op jit(solution)/shard_map/back_two/pallas_call | solution.py:606
  297.9 1.6 pack.1
  308.5 2.1 collective-permute-start.55
  313.7 2.1 collective-permute-done.56
  316.9 2.5 collective-permute-done.54
  319.5 2.9 collective-permute-done.51
  324.2 1.8 collective-permute-start.59
  327.1 2.4 collective-permute-start.61
  330.5 2.7 collective-permute-start.62
  333.2 2.8 settle.2
  336.0 2.8 settle.3
  342.9 2.9 settle_last.1
  (270 shorter events, 65.6 us)
Async XLA Ops:
  7.2 309.7 %all-gather.7.cloned.1.call-start = ((), (), s32[]{:S(2)}) async-start(), calls=%async_computation.1 | async-start | bytes 1327104 | tf_op jit(solution)/shard_map/all_gather | solution.py:829
  9.1 9.0 %collective-permute-start = (bf16[64,1152]{1,0:T(8,128)(2,1)S(1)}, bf16[64,1152]{1,0:T(8,128)(2,1)S(1)}, u32[]{:S(2)}, u32[]{:S(2)}) collective-permute-start(bf16[64,1152]{1,0:T(8,128)(2,1)S(1)} %fusion.18), channel_id=1, source_target_pairs={{0,1},{1,0},{2,3},{3,2},{4,5},{5,4},{6,7},{7,6},{8,9},{9,8},{10,11... | collective-permute-start | bytes 442376 | tf_op jit(solution)/shard_map/ppermute | solution.py:38
  12.2 14.0 %collective-permute-start.1 = (bf16[64,1152]{1,0:T(8,128)(2,1)S(1)}, bf16[64,1152]{1,0:T(8,128)(2,1)S(1)}, u32[]{:S(2)}, u32[]{:S(2)}) collective-permute-start(bf16[64,1152]{1,0:T(8,128)(2,1)S(1)} %fusion.18), channel_id=1, source_target_pairs={{0,2},{1,3},{2,0},{3,1},{4,6},{5,7},{6,4},{7,5},{8,10},{9,11},{10,... | collective-permute-start | bytes 442376 | tf_op jit(solution)/shard_map/ppermute | solution.py:38
  14.7 11.4 %collective-permute-start.2 = (bf16[64,1152]{1,0:T(8,128)(2,1)S(1)}, bf16[64,1152]{1,0:T(8,128)(2,1)S(1)}, u32[]{:S(2)}, u32[]{:S(2)}) collective-permute-start(bf16[64,1152]{1,0:T(8,128)(2,1)S(1)} %fusion.18), channel_id=1, source_target_pairs={{0,3},{1,2},{2,1},{3,0},{4,7},{5,6},{6,5},{7,4},{8,11},{9,10},{10,... | collective-permute-start | bytes 442376 | tf_op jit(solution)/shard_map/ppermute | solution.py:38
  26.2 21.0 %collective-permute-start.8 = (bf16[48,1920]{1,0:T(8,128)(2,1)S(1)}, bf16[48,1920]{1,0:T(8,128)(2,1)S(1)}, u32[]{:S(2)}, u32[]{:S(2)}) collective-permute-start(bf16[48,1920]{1,0:T(8,128)(2,1)S(1)} %pad_maximum_fusion.3), channel_id=1, source_target_pairs={{0,3},{1,2},{2,1},{3,0},{4,7},{5,6},{6,5},{7,4},{8,11},{9,10},{10,... | collective-permute-start | bytes 552968 | tf_op jit(solution)/shard_map/ppermute | solution.py:38
  28.4 18.8 %collective-permute-start.6 = (bf16[48,1920]{1,0:T(8,128)(2,1)S(1)}, bf16[48,1920]{1,0:T(8,128)(2,1)S(1)}, u32[]{:S(2)}, u32[]{:S(2)}) collective-permute-start(bf16[48,1920]{1,0:T(8,128)(2,1)S(1)} %pad_maximum_fusion.3), channel_id=1, source_target_pairs={{0,1},{1,0},{2,3},{3,2},{4,5},{5,4},{6,7},{7,6},{8,9},{9,8},{10,11... | collective-permute-start | bytes 552968 | tf_op jit(solution)/shard_map/ppermute | solution.py:38
  30.1 10.8 %collective-permute-start.3 = (bf16[3,48,1152]{2,1,0:T(8,128)(2,1)S(1)}, bf16[3,48,1152]{2,1,0:T(8,128)(2,1)S(1)}, u32[]{:S(2)}, u32[]{:S(2)}) collective-permute-start(bf16[3,48,1152]{2,1,0:T(8,128)(2,1)S(1)} %pad_maximum_fusion.2.rest_0_), channel_id=1, source_target_pairs={{0,8},{4,12},{8,0},{12,4},{16,24},{20,28},{24,16},{28,20},{1,9},{5... | collective-permute-start | bytes 995336 | tf_op jit(solution)/shard_map/ppermute | solution.py:38
  31.7 14.9 %collective-permute-start.4 = (bf16[3,48,1152]{2,1,0:T(8,128)(2,1)S(1)}, bf16[3,48,1152]{2,1,0:T(8,128)(2,1)S(1)}, u32[]{:S(2)}, u32[]{:S(2)}) collective-permute-start(bf16[3,48,1152]{2,1,0:T(8,128)(2,1)S(1)} %pad_maximum_fusion.2.rest_0_), channel_id=1, source_target_pairs={{0,16},{4,20},{8,24},{12,28},{16,0},{20,4},{24,8},{28,12},{1,17},{... | collective-permute-start | bytes 995336 | tf_op jit(solution)/shard_map/ppermute | solution.py:38
  33.2 13.3 %collective-permute-start.5 = (bf16[3,48,1152]{2,1,0:T(8,128)(2,1)S(1)}, bf16[3,48,1152]{2,1,0:T(8,128)(2,1)S(1)}, u32[]{:S(2)}, u32[]{:S(2)}) collective-permute-start(bf16[3,48,1152]{2,1,0:T(8,128)(2,1)S(1)} %pad_maximum_fusion.2.rest_0_), channel_id=1, source_target_pairs={{0,24},{4,28},{8,16},{12,20},{16,8},{20,12},{24,0},{28,4},{1,25},{... | collective-permute-start | bytes 995336 | tf_op jit(solution)/shard_map/ppermute | solution.py:38
  40.9 8.4 %collective-permute-start.7 = (bf16[48,1920]{1,0:T(8,128)(2,1)S(1)}, bf16[48,1920]{1,0:T(8,128)(2,1)}, u32[]{:S(2)}, u32[]{:S(2)}) collective-permute-start(bf16[48,1920]{1,0:T(8,128)(2,1)S(1)} %pad_maximum_fusion.3), channel_id=1, source_target_pairs={{0,2},{1,3},{2,0},{3,1},{4,6},{5,7},{6,4},{7,5},{8,10},{9,11},{10,... | collective-permute-start | bytes 552968 | tf_op jit(solution)/shard_map/ppermute | solution.py:38
  52.0 29.5 %collective-permute-start.13 = (bf16[3,48,1920]{2,1,0:T(8,128)(2,1)S(1)}, bf16[3,48,1920]{2,1,0:T(8,128)(2,1)S(1)}, u32[]{:S(2)}, u32[]{:S(2)}) collective-permute-start(bf16[3,48,1920]{2,1,0:T(8,128)(2,1)S(1)} %pad_maximum_fusion.rest_0_), channel_id=1, source_target_pairs={{0,8},{4,12},{8,0},{12,4},{16,24},{20,28},{24,16},{28,20},{1,9},{5... | collective-permute-start | bytes 1658888 | tf_op jit(solution)/shard_map/ppermute | solution.py:38
  53.4 28.0 %collective-permute-start.14 = (bf16[3,48,1920]{2,1,0:T(8,128)(2,1)S(1)}, bf16[3,48,1920]{2,1,0:T(8,128)(2,1)S(1)}, u32[]{:S(2)}, u32[]{:S(2)}) collective-permute-start(bf16[3,48,1920]{2,1,0:T(8,128)(2,1)S(1)} %pad_maximum_fusion.rest_0_), channel_id=1, source_target_pairs={{0,16},{4,20},{8,24},{12,28},{16,0},{20,4},{24,8},{28,12},{1,17},{... | collective-permute-start | bytes 1658888 | tf_op jit(solution)/shard_map/ppermute | solution.py:38
  55.0 26.5 %collective-permute-start.15 = (bf16[3,48,1920]{2,1,0:T(8,128)(2,1)S(1)}, bf16[3,48,1920]{2,1,0:T(8,128)(2,1)S(1)}, u32[]{:S(2)}, u32[]{:S(2)}) collective-permute-start(bf16[3,48,1920]{2,1,0:T(8,128)(2,1)S(1)} %pad_maximum_fusion.rest_0_), channel_id=1, source_target_pairs={{0,24},{4,28},{8,16},{12,20},{16,8},{20,12},{24,0},{28,4},{1,25},{... | collective-permute-start | bytes 1658888 | tf_op jit(solution)/shard_map/ppermute | solution.py:38
  81.6 11.9 %collective-permute-start.16 = (bf16[192,384]{1,0:T(8,128)(2,1)S(1)}, bf16[192,384]{1,0:T(8,128)(2,1)S(1)}, u32[]{:S(2)}, u32[]{:S(2)}) collective-permute-start(bf16[192,384]{1,0:T(8,128)(2,1)S(1)} %copy-done.38), channel_id=1, source_target_pairs={{0,1},{1,0},{2,3},{3,2},{4,5},{5,4},{6,7},{7,6},{8,9},{9,8},{10,11... | collective-permute-start | bytes 442376 | tf_op jit(solution)/shard_map/ppermute | solution.py:38
  81.6 12.8 %collective-permute-start.17 = (bf16[192,384]{1,0:T(8,128)(2,1)S(1)}, bf16[192,384]{1,0:T(8,128)(2,1)S(1)}, u32[]{:S(2)}, u32[]{:S(2)}) collective-permute-start(bf16[192,384]{1,0:T(8,128)(2,1)S(1)} %copy-done.38), channel_id=1, source_target_pairs={{0,2},{1,3},{2,0},{3,1},{4,6},{5,7},{6,4},{7,5},{8,10},{9,11},{10,... | collective-permute-start | bytes 442376 | tf_op jit(solution)/shard_map/ppermute | solution.py:38
  83.6 10.7 %collective-permute-start.18 = (bf16[192,384]{1,0:T(8,128)(2,1)S(1)}, bf16[192,384]{1,0:T(8,128)(2,1)S(1)}, u32[]{:S(2)}, u32[]{:S(2)}) collective-permute-start(bf16[192,384]{1,0:T(8,128)(2,1)S(1)} %copy-done.38), channel_id=1, source_target_pairs={{0,3},{1,2},{2,1},{3,0},{4,7},{5,6},{6,5},{7,4},{8,11},{9,10},{10,... | collective-permute-start | bytes 442376 | tf_op jit(solution)/shard_map/ppermute | solution.py:38
  95.5 27.0 %collective-permute-start.23 = (bf16[3,192,384]{2,1,0:T(8,128)(2,1)S(1)}, bf16[3,192,384]{2,1,0:T(8,128)(2,1)S(1)}, u32[]{:S(2)}, u32[]{:S(2)}) collective-permute-start(bf16[3,192,384]{2,1,0:T(8,128)(2,1)S(1)} %pad_maximum_fusion.1.rest_0_), channel_id=1, source_target_pairs={{0,8},{4,12},{8,0},{12,4},{16,24},{20,28},{24,16},{28,20},{1,9},{5... | collective-permute-start | bytes 1327112 | tf_op jit(solution)/shard_map/ppermute | solution.py:38
  96.6 26.0 %collective-permute-start.24 = (bf16[3,192,384]{2,1,0:T(8,128)(2,1)S(1)}, bf16[3,192,384]{2,1,0:T(8,128)(2,1)S(1)}, u32[]{:S(2)}, u32[]{:S(2)}) collective-permute-start(bf16[3,192,384]{2,1,0:T(8,128)(2,1)S(1)} %pad_maximum_fusion.1.rest_0_), channel_id=1, source_target_pairs={{0,16},{4,20},{8,24},{12,28},{16,0},{20,4},{24,8},{28,12},{1,17},{... | collective-permute-start | bytes 1327112 | tf_op jit(solution)/shard_map/ppermute | solution.py:38
  98.0 24.6 %collective-permute-start.25 = (bf16[3,192,384]{2,1,0:T(8,128)(2,1)S(1)}, bf16[3,192,384]{2,1,0:T(8,128)(2,1)S(1)}, u32[]{:S(2)}, u32[]{:S(2)}) collective-permute-start(bf16[3,192,384]{2,1,0:T(8,128)(2,1)S(1)} %pad_maximum_fusion.1.rest_0_), channel_id=1, source_target_pairs={{0,24},{4,28},{8,16},{12,20},{16,8},{20,12},{24,0},{28,4},{1,25},{... | collective-permute-start | bytes 1327112 | tf_op jit(solution)/shard_map/ppermute | solution.py:38
  122.6 12.5 %collective-permute-start.26 = (bf16[3,192,384]{2,1,0:T(8,128)(2,1)S(1)}, bf16[3,192,384]{2,1,0:T(8,128)(2,1)S(1)}, u32[]{:S(2)}, u32[]{:S(2)}) collective-permute-start(bf16[3,192,384]{2,1,0:T(8,128)(2,1)S(1)} %pad_maximum_fusion.1.rest_0_), channel_id=1, source_target_pairs={{0,4},{4,0},{8,12},{12,8},{16,20},{20,16},{24,28},{28,24},{1,5},{5... | collective-permute-start | bytes 1327112 | tf_op jit(solution)/shard_map/ppermute | solution.py:38
  122.7 12.5 %collective-permute-start.27 = (bf16[3,192,384]{2,1,0:T(8,128)(2,1)S(1)}, bf16[3,192,384]{2,1,0:T(8,128)(2,1)S(1)}, u32[]{:S(2)}, u32[]{:S(2)}) collective-permute-start(bf16[3,192,384]{2,1,0:T(8,128)(2,1)S(1)} %collective-permute-done.23.rest_1_), channel_id=1, source_target_pairs={{0,4},{4,0},{8,12},{12,8},{16,20},{20,16},{24,28},{28,24},{1,5},{5... | collective-permute-start | bytes 1327112 | tf_op jit(solution)/shard_map/ppermute | solution.py:38
  123.2 12.0 %collective-permute-start.28 = (bf16[3,192,384]{2,1,0:T(8,128)(2,1)S(1)}, bf16[3,192,384]{2,1,0:T(8,128)(2,1)S(1)}, u32[]{:S(2)}, u32[]{:S(2)}) collective-permute-start(bf16[3,192,384]{2,1,0:T(8,128)(2,1)S(1)} %collective-permute-done.24.rest_2_), channel_id=1, source_target_pairs={{0,4},{4,0},{8,12},{12,8},{16,20},{20,16},{24,28},{28,24},{1,5},{5... | collective-permute-start | bytes 1327112 | tf_op jit(solution)/shard_map/ppermute | solution.py:38
  123.3 11.9 %collective-permute-start.29 = (bf16[3,192,384]{2,1,0:T(8,128)(2,1)S(1)}, bf16[3,192,384]{2,1,0:T(8,128)(2,1)S(1)}, u32[]{:S(2)}, u32[]{:S(2)}) collective-permute-start(bf16[3,192,384]{2,1,0:T(8,128)(2,1)S(1)} %collective-permute-done.25.rest_3_), channel_id=1, source_target_pairs={{0,4},{4,0},{8,12},{12,8},{16,20},{20,16},{24,28},{28,24},{1,5},{5... | collective-permute-start | bytes 1327112 | tf_op jit(solution)/shard_map/ppermute | solution.py:38
  135.2 13.2 %collective-permute-start.30 = (bf16[4,4,192,384]{3,2,1,0:T(8,128)(2,1)}, bf16[4,4,192,384]{3,2,1,0:T(8,128)(2,1)S(1)}, u32[]{:S(2)}, u32[]{:S(2)}) collective-permute-start(bf16[4,4,192,384]{3,2,1,0:T(8,128)(2,1)} %get-tuple-element.261), channel_id=1, source_target_pairs={{0,4},{4,0},{8,12},{12,8},{16,20},{20,16},{24,28},{28,24},{1,5},{5... | collective-permute-start | bytes 7077896 | tf_op jit(solution)/shard_map/ppermute | solution.py:38
  150.0 28.0 %collective-permute-start.31 = (bf16[2,4,192,384]{3,2,1,0:T(8,128)(2,1)S(1)}, bf16[2,4,192,384]{3,2,1,0:T(8,128)(2,1)S(1)}, u32[]{:S(2)}, u32[]{:S(2)}) collective-permute-start(bf16[2,4,192,384]{3,2,1,0:T(8,128)(2,1)S(1)} %add_convert_fusion.1), channel_id=1, source_target_pairs={{0,8},{4,12},{8,0},{12,4},{16,24},{20,28},{24,16},{28,20},{1,9},{5... | collective-permute-start | bytes 3538952 | tf_op jit(solution)/shard_map/ppermute | solution.py:38
  177.9 19.8 %collective-permute-start.32 = (bf16[4,4,48,1536]{3,2,1,0:T(8,128)(2,1)}, bf16[4,4,48,1536]{3,2,1,0:T(8,128)(2,1)S(1)}, u32[]{:S(2)}, u32[]{:S(2)}) collective-permute-start(bf16[4,4,48,1536]{3,2,1,0:T(8,128)(2,1)} %get-tuple-element.277), channel_id=1, source_target_pairs={{0,4},{4,0},{8,12},{12,8},{16,20},{20,16},{24,28},{28,24},{1,5},{5... | collective-permute-start | bytes 7077896 | tf_op jit(solution)/shard_map/ppermute | solution.py:38
  180.5 18.7 %collective-permute-start.33 = (bf16[4,192,384]{2,1,0:T(8,128)(2,1)}, bf16[4,192,384]{2,1,0:T(8,128)(2,1)}, u32[]{:S(2)}, u32[]{:S(2)}) collective-permute-start(bf16[4,192,384]{2,1,0:T(8,128)(2,1)} %fusion.3), channel_id=1, source_target_pairs={{0,16},{4,20},{8,24},{12,28},{16,0},{20,4},{24,8},{28,12},{1,17},{... | collective-permute-start | bytes 1769480 | tf_op jit(solution)/shard_map/ppermute | solution.py:38
  199.1 28.1 %collective-permute-start.34 = (bf16[2,4,48,1536]{3,2,1,0:T(8,128)(2,1)S(1)}, bf16[2,4,48,1536]{3,2,1,0:T(8,128)(2,1)S(1)}, u32[]{:S(2)}, u32[]{:S(2)}) collective-permute-start(bf16[2,4,48,1536]{3,2,1,0:T(8,128)(2,1)S(1)} %add_convert_fusion), channel_id=1, source_target_pairs={{0,16},{4,20},{8,24},{12,28},{16,0},{20,4},{24,8},{28,12},{1,17},{... | collective-permute-start | bytes 3538952 | tf_op jit(solution)/shard_map/ppermute | solution.py:38
  229.0 17.5 %collective-permute-start.38 = (bf16[4,48,1536]{2,1,0:T(8,128)(2,1)S(1)}, bf16[4,48,1536]{2,1,0:T(8,128)(2,1)}, u32[]{:S(2)}, u32[]{:S(2)}) collective-permute-start(bf16[4,48,1536]{2,1,0:T(8,128)(2,1)S(1)} %fusion.4), channel_id=1, source_target_pairs={{0,8},{4,12},{8,0},{12,4},{16,24},{20,28},{24,16},{28,20},{1,9},{5... | collective-permute-start | bytes 1769480 | tf_op jit(solution)/shard_map/ppermute | solution.py:38
  231.4 14.3 %collective-permute-start.35 = (bf16[192,384]{1,0:T(8,128)(2,1)S(1)}, bf16[192,384]{1,0:T(8,128)(2,1)S(1)}, u32[]{:S(2)}, u32[]{:S(2)}) collective-permute-start(bf16[192,384]{1,0:T(8,128)(2,1)S(1)} %get-tuple-element.396), channel_id=1, source_target_pairs={{0,1},{1,0},{2,3},{3,2},{4,5},{5,4},{6,7},{7,6},{8,9},{9,8},{10,11... | collective-permute-start | bytes 442376 | tf_op jit(solution)/shard_map/ppermute | solution.py:38
  233.6 12.9 %collective-permute-start.36 = (bf16[192,384]{1,0:T(8,128)(2,1)S(1)}, bf16[192,384]{1,0:T(8,128)(2,1)S(1)}, u32[]{:S(2)}, u32[]{:S(2)}) collective-permute-start(bf16[192,384]{1,0:T(8,128)(2,1)S(1)} %get-tuple-element.395), channel_id=1, source_target_pairs={{0,2},{1,3},{2,0},{3,1},{4,6},{5,7},{6,4},{7,5},{8,10},{9,11},{10,... | collective-permute-start | bytes 442376 | tf_op jit(solution)/shard_map/ppermute | solution.py:38
  233.6 12.9 %collective-permute-start.37 = (bf16[192,384]{1,0:T(8,128)(2,1)S(1)}, bf16[192,384]{1,0:T(8,128)(2,1)S(1)}, u32[]{:S(2)}, u32[]{:S(2)}) collective-permute-start(bf16[192,384]{1,0:T(8,128)(2,1)S(1)} %get-tuple-element.394), channel_id=1, source_target_pairs={{0,3},{1,2},{2,1},{3,0},{4,7},{5,6},{6,5},{7,4},{8,11},{9,10},{10,... | collective-permute-start | bytes 442376 | tf_op jit(solution)/shard_map/ppermute | solution.py:38
  246.5 9.4 %collective-permute-start.39 = (bf16[4,4,48,1152]{3,2,1,0:T(8,128)(2,1)}, bf16[4,4,48,1152]{3,2,1,0:T(8,128)(2,1)}, u32[]{:S(2)}, u32[]{:S(2)}) collective-permute-start(bf16[4,4,48,1152]{3,2,1,0:T(8,128)(2,1)} %get-tuple-element.312), channel_id=1, source_target_pairs={{0,4},{4,0},{8,12},{12,8},{16,20},{20,16},{24,28},{28,24},{1,5},{5... | collective-permute-start | bytes 5308424 | tf_op jit(solution)/shard_map/ppermute | solution.py:38
  258.2 25.8 %collective-permute-start.43 = (bf16[2,4,48,1152]{3,2,1,0:T(8,128)(2,1)}, bf16[2,4,48,1152]{3,2,1,0:T(8,128)(2,1)}, u32[]{:S(2)}, u32[]{:S(2)}) collective-permute-start(bf16[2,4,48,1152]{3,2,1,0:T(8,128)(2,1)} %add_convert_fusion.2), channel_id=1, source_target_pairs={{0,16},{4,20},{8,24},{12,28},{16,0},{20,4},{24,8},{28,12},{1,17},{... | collective-permute-start | bytes 2654216 | tf_op jit(solution)/shard_map/ppermute | solution.py:38
  259.6 18.4 %collective-permute-start.40 = (bf16[48,1536]{1,0:T(8,128)(2,1)}, bf16[48,1536]{1,0:T(8,128)(2,1)S(1)}, u32[]{:S(2)}, u32[]{:S(2)}) collective-permute-start(bf16[48,1536]{1,0:T(8,128)(2,1)} %get-tuple-element.393), channel_id=1, source_target_pairs={{0,1},{1,0},{2,3},{3,2},{4,5},{5,4},{6,7},{7,6},{8,9},{9,8},{10,11... | collective-permute-start | bytes 442376 | tf_op jit(solution)/shard_map/ppermute | solution.py:38
  262.2 15.8 %collective-permute-start.41 = (bf16[48,1536]{1,0:T(8,128)(2,1)}, bf16[48,1536]{1,0:T(8,128)(2,1)S(1)}, u32[]{:S(2)}, u32[]{:S(2)}) collective-permute-start(bf16[48,1536]{1,0:T(8,128)(2,1)} %get-tuple-element.392), channel_id=1, source_target_pairs={{0,2},{1,3},{2,0},{3,1},{4,6},{5,7},{6,4},{7,5},{8,10},{9,11},{10,... | collective-permute-start | bytes 442376 | tf_op jit(solution)/shard_map/ppermute | solution.py:38
  262.2 15.8 %collective-permute-start.42 = (bf16[48,1536]{1,0:T(8,128)(2,1)S(1)}, bf16[48,1536]{1,0:T(8,128)(2,1)S(1)}, u32[]{:S(2)}, u32[]{:S(2)}) collective-permute-start(bf16[48,1536]{1,0:T(8,128)(2,1)S(1)} %get-tuple-element.391), channel_id=1, source_target_pairs={{0,3},{1,2},{2,1},{3,0},{4,7},{5,6},{6,5},{7,4},{8,11},{9,10},{10,... | collective-permute-start | bytes 442376 | tf_op jit(solution)/shard_map/ppermute | solution.py:38
  264.6 57.7 %all-gather.5.cloned.1.call-start = ((), (), s32[]{:S(2)}) async-start(), calls=%async_computation | async-start | bytes 1327104 | tf_op jit(solution)/shard_map/all_gather | solution.py:829
  286.2 15.5 %collective-permute-start.46 = (bf16[4,48,1152]{2,1,0:T(8,128)(2,1)S(1)}, bf16[4,48,1152]{2,1,0:T(8,128)(2,1)}, u32[]{:S(2)}, u32[]{:S(2)}) collective-permute-start(bf16[4,48,1152]{2,1,0:T(8,128)(2,1)S(1)} %fusion.5), channel_id=1, source_target_pairs={{0,8},{4,12},{8,0},{12,4},{16,24},{20,28},{24,16},{28,20},{1,9},{5... | collective-permute-start | bytes 1327112 | tf_op jit(solution)/shard_map/ppermute | solution.py:38
  288.0 13.7 %collective-permute-start.45 = (bf16[2,4,48,384]{3,2,1,0:T(8,128)(2,1)}, bf16[2,4,48,384]{3,2,1,0:T(8,128)(2,1)}, u32[]{:S(2)}, u32[]{:S(2)}) collective-permute-start(bf16[2,4,48,384]{3,2,1,0:T(8,128)(2,1)} %add_convert_fusion.3), channel_id=1, source_target_pairs={{0,16},{4,20},{8,24},{12,28},{16,0},{20,4},{24,8},{28,12},{1,17},{... | collective-permute-start | bytes 884744 | tf_op jit(solution)/shard_map/ppermute | solution.py:38
  307.3 12.2 %collective-permute-start.54 = (bf16[48,1152]{1,0:T(8,128)(2,1)S(1)}, bf16[48,1152]{1,0:T(8,128)(2,1)S(1)}, u32[]{:S(2)}, u32[]{:S(2)}) collective-permute-start(bf16[48,1152]{1,0:T(8,128)(2,1)S(1)} %get-tuple-element.402), channel_id=1, source_target_pairs={{0,2},{1,3},{2,0},{3,1},{4,6},{5,7},{6,4},{7,5},{8,10},{9,11},{10,... | collective-permute-start | bytes 331784 | tf_op jit(solution)/shard_map/ppermute | solution.py:38
  308.5 11.0 %collective-permute-start.55 = (bf16[48,1152]{1,0:T(8,128)(2,1)S(1)}, bf16[48,1152]{1,0:T(8,128)(2,1)S(1)}, u32[]{:S(2)}, u32[]{:S(2)}) collective-permute-start(bf16[48,1152]{1,0:T(8,128)(2,1)S(1)} %get-tuple-element.401), channel_id=1, source_target_pairs={{0,3},{1,2},{2,1},{3,0},{4,7},{5,6},{6,5},{7,4},{8,11},{9,10},{10,... | collective-permute-start | bytes 331784 | tf_op jit(solution)/shard_map/ppermute | solution.py:38
  313.6 8.8 %collective-permute-start.51 = (bf16[48,384]{1,0:T(8,128)(2,1)S(1)}, bf16[48,384]{1,0:T(8,128)(2,1)S(1)}, u32[]{:S(2)}, u32[]{:S(2)}) collective-permute-start(bf16[48,384]{1,0:T(8,128)(2,1)S(1)} %get-tuple-element.405), channel_id=1, source_target_pairs={{0,2},{1,3},{2,0},{3,1},{4,6},{5,7},{6,4},{7,5},{8,10},{9,11},{10,... | collective-permute-start | bytes 110600 | tf_op jit(solution)/shard_map/ppermute | solution.py:38
  322.5 16.4 %collective-permute-start.57 = (bf16[48,1536]{1,0:T(8,128)(2,1)S(1)}, bf16[48,1536]{1,0:T(8,128)(2,1)S(1)}, u32[]{:S(2)}, u32[]{:S(2)}) collective-permute-start(bf16[48,1536]{1,0:T(8,128)(2,1)S(1)} %pad_maximum_fusion.4.rest_0_), channel_id=1, source_target_pairs={{0,8},{4,12},{8,0},{12,4},{16,24},{20,28},{24,16},{28,20},{1,9},{5... | collective-permute-start | bytes 442376 | tf_op jit(solution)/shard_map/ppermute | solution.py:38
  323.6 15.3 %collective-permute-start.58 = (bf16[48,1536]{1,0:T(8,128)(2,1)S(1)}, bf16[48,1536]{1,0:T(8,128)(2,1)S(1)}, u32[]{:S(2)}, u32[]{:S(2)}) collective-permute-start(bf16[48,1536]{1,0:T(8,128)(2,1)S(1)} %pad_maximum_fusion.4.rest_0_), channel_id=1, source_target_pairs={{0,16},{4,20},{8,24},{12,28},{16,0},{20,4},{24,8},{28,12},{1,17},{... | collective-permute-start | bytes 442376 | tf_op jit(solution)/shard_map/ppermute | solution.py:38
  324.2 14.7 %collective-permute-start.59 = (bf16[48,1536]{1,0:T(8,128)(2,1)S(1)}, bf16[48,1536]{1,0:T(8,128)(2,1)S(1)}, u32[]{:S(2)}, u32[]{:S(2)}) collective-permute-start(bf16[48,1536]{1,0:T(8,128)(2,1)S(1)} %pad_maximum_fusion.4.rest_0_), channel_id=1, source_target_pairs={{0,24},{4,28},{8,16},{12,20},{16,8},{20,12},{24,0},{28,4},{1,25},{... | collective-permute-start | bytes 442376 | tf_op jit(solution)/shard_map/ppermute | solution.py:38
  327.1 11.7 %collective-permute-start.61 = (f32[16,768]{1,0:T(8,128)S(1)}, f32[16,768]{1,0:T(8,128)S(1)}, u32[]{:S(2)}, u32[]{:S(2)}) collective-permute-start(f32[16,768]{1,0:T(8,128)S(1)} %add.207), channel_id=1, source_target_pairs={{0,2},{1,3},{2,0},{3,1},{4,6},{5,7},{6,4},{7,5},{8,10},{9,11},{10,... | collective-permute-start | bytes 147464 | tf_op jit(solution)/shard_map/ppermute | solution.py:38
  330.5 8.4 %collective-permute-start.62 = (f32[16,768]{1,0:T(8,128)S(1)}, f32[16,768]{1,0:T(8,128)S(1)}, u32[]{:S(2)}, u32[]{:S(2)}) collective-permute-start(f32[16,768]{1,0:T(8,128)S(1)} %add.207), channel_id=1, source_target_pairs={{0,3},{1,2},{2,1},{3,0},{4,7},{5,6},{6,5},{7,4},{8,11},{9,10},{10,... | collective-permute-start | bytes 147464 | tf_op jit(solution)/shard_map/ppermute | solution.py:38
  (68 other events, 482.6 us)
Sparse Core Ops, SparseCore 0:
  264.7 24.2 all-gather.6
  299.6 22.2 all-gather.4

commit v4 on v3

--- a/solution.py
+++ b/solution.py
@@ -14,7 +14,7 @@
 NEG = -1e30
 BF16 = jnp.bfloat16
 F32 = jnp.float32
-VMEM_LIMIT = 56 << 20
+VMEM_LIMIT = 24 << 20
 SMALL_COST = pl.CostEstimate(flops=10**6, bytes_accessed=10**5, transcendentals=0)
 
 
@@ -946,26 +946,27 @@
     one_shards = shard_swaps(one_held)
     small_grads = vector_step(small_grads)
     every_fc, every_proj = every_owner(fc_piece), every_owner(proj_piece)
-    two_came, one_held, small_grads = tie((two_came, one_held, small_grads))
+    two_came, one_held, small_grads, every_proj = tie(
+        (two_came, one_held, small_grads, every_proj)
+    )
+    (d_proj_weight,) = settle(every_proj, (width,), pieces)
     two_held = two_held + two_came.astype(F32)
     two_shards = shard_swaps(two_held)
     small_grads = vector_step(small_grads, len(masks))
-    two_shards, one_shards, small_grads, every_fc, every_proj = tie(
-        (two_shards, one_shards, small_grads, every_fc, every_proj)
+    two_shards, one_shards, small_grads, every_fc, d_proj_weight = tie(
+        (two_shards, one_shards, small_grads, every_fc, d_proj_weight)
     )
     last_piece = jnp.concatenate(
         [shard_total(one_held, one_shards), shard_total(two_held, two_shards)], axis=-1
     )
     last_parts = across_chips(last_piece, 2)
-    small_shards = along_shard(small_grads)
+    masks = [1 << i for i in range(shards.bit_length() - 1)]
+    for mask in masks[:-1]:
+        small_grads = small_grads + swap(small_grads, "shard", shards, mask)
     (d_fc_weight,) = settle(every_fc, (fc_weight.shape[1],), pieces)
-    (d_proj_weight,) = settle(every_proj, (width,), pieces)
-    last_parts, small_shards, d_fc_weight, d_proj_weight = tie(
-        (last_parts, small_shards, d_fc_weight, d_proj_weight)
-    )
+    last_parts, small_grads, d_fc_weight = tie((last_parts, small_grads, d_fc_weight))
     last_parts = across_cores(last_parts)
-    for value in small_shards:
-        small_grads = small_grads + value
+    small_grads = small_grads + swap(small_grads, "shard", shards, masks[-1])
     d_qkv_weight, d_out_weight = settle_last(
         last_parts, spots, pieces, heads_one[0].shape[1] // 2, width
     )

time: 357 us -> 353 us (0.989)
  Pallas kernels: 194 us -> 145 us
  local copies, waits for them, and re-layouts: 18.3 us -> 59.4 us
  waiting for transfers between devices: 40.9 us -> 47.4 us
    unnamed x100 -> x180, local copies, waits for them, and re-layouts: 9.01 us -> 50.8 us
    pallas_call x5, Pallas kernels: 72.1 us -> 52.4 us  [row_call(): pl.pallas_call(kernel, grid_spec=pltpu.PrefetchScalarGridSpec(num_scalar_...]
    pallas_call x4, Pallas kernels: 37.3 us -> 28.3 us  [grad_call(): pl.pallas_call(kernel, grid_spec=pltpu.PrefetchScalarGridSpec(num_scalar_...]
    ppermute x67 -> x66, waiting for transfers between devices: 40.9 us -> 47.1 us  [swap(): return lax.ppermute(value, axis, [(i, i ^ mask) for i in range(size)])]
    pallas_call x1, Pallas kernels: 8.5 us -> 4.35 us  [back_two(): pl.pallas_call(functools.partial(back_two_kernel, start), grid=(4,), in_s...]
    pallas_call x1, Pallas kernels: 7.38 us -> 3.27 us  [back_one(): pl.pallas_call(back_one_kernel, grid=(4,), in_specs=[pl.BlockSpec(w.shape...]
    ppermute x67 -> x66, starting transfers between devices: 66 us -> 62.9 us  [swap(): return lax.ppermute(value, axis, [(i, i ^ mask) for i in range(size)])]
  transfers between devices with their start and end apart: 69 -> 68, of which waited for: 15 -> 19; matrix products, arithmetic and copies ran while one was open for 6% -> 6% of each run, Pallas kernels for 54% -> 41%
where the time goes in v4:
time: 353 us; the launch traced here: 350 us
  Pallas kernels  145 us (41%)
  starting transfers between devices  63 us (18%)
  local copies, waits for them, and re-layouts  59.4 us (17%)
  waiting for transfers between devices  47.4 us (13%)
  other arithmetic  19.1 us (5%)
  between operations  15.6 us (4%)
    ppermute x66, starting transfers between devices, swap(): return lax.ppermute(value, axis, [(i, i ^ mask) for i in range(size)])  62.9 us
    pallas_call x5, Pallas kernels, row_call(): pl.pallas_call(kernel, grid_spec=pltpu.PrefetchScalarGridSpec(num_scalar_...  52.4 us
    unnamed x180, local copies, waits for them, and re-layouts  50.8 us
    ppermute x66, waiting for transfers between devices, swap(): return lax.ppermute(value, axis, [(i, i ^ mask) for i in range(size)])  47.1 us
    pallas_call x2, Pallas kernels, attend_backward(): pl.pallas_call(functools.partial(attend_back_kernel, rows), grid=(count,)...  34.6 us
    pallas_call x4, Pallas kernels, grad_call(): pl.pallas_call(kernel, grid_spec=pltpu.PrefetchScalarGridSpec(num_scalar_...  28.3 us
    pallas_call x2, Pallas kernels, attend_forward(): pl.pallas_call(functools.partial(attend_kernel, rows), grid=(count,), in_...  17.1 us
  transfers between devices with their start and end apart: 68, of which 19 were waited for; matrix products, arithmetic and copies ran while one was open for 6% of the time, Pallas kernels for 41%

profile of v4, /device:TPU:0, one launch (start us, length us, event | category | flops | bytes accessed | tf_op | source)
XLA Modules:
  0.0 349.7 jit_solution(7520469590082783008)
XLA Ops:
  9.1 3.1 collective-permute-start
  12.2 2.6 collective-permute-start.1
  18.1 8.0 %collective-permute-done.1 = bf16[64,1152]{1,0:T(8,128)(2,1)S(1)} collective-permute-done((bf16[64,1152]{1,0:T(8,128)(2,1)S(1)}, bf16[64,1152]{1,0:T(8,128)(2,1)S(1)}, u32[]{:S(2)}, u32[]{:S(2)}) %collective-permute-start.1) | collective-permute-done | bytes 147488 | tf_op jit(solution)/shard_map/ppermute | solution.py:38
  26.2 2.3 collective-permute-start.8
  35.3 5.6 %collective-permute-done.3.rest_1_ = bf16[3,48,1152]{2,1,0:T(8,128)(2,1)S(1)} collective-permute-done((bf16[3,48,1152]{2,1,0:T(8,128)(2,1)S(1)}, bf16[3,48,1152]{2,1,0:T(8,128)(2,1)S(1)}, u32[]{:S(2)}, u32[]{:S(2)}) %collective-permute-start.3) | collective-permute-done | bytes 331808 | tf_op jit(solution)/shard_map/ppermute | solution.py:38
  41.7 4.8 %collective-permute-done.4.rest_2_ = bf16[3,48,1152]{2,1,0:T(8,128)(2,1)S(1)} collective-permute-done((bf16[3,48,1152]{2,1,0:T(8,128)(2,1)S(1)}, bf16[3,48,1152]{2,1,0:T(8,128)(2,1)S(1)}, u32[]{:S(2)}, u32[]{:S(2)}) %collective-permute-start.4) | collective-permute-done | bytes 331808 | tf_op jit(solution)/shard_map/ppermute | solution.py:38
  63.9 8.3 %qkv.1 = (bf16[768,2304]{1,0:T(8,128)(2,1)S(1)}, bf16[1024,768]{1,0:T(8,128)(2,1)S(1)}, bf16[1024,2304]{1,0:T(8,128)(2,1)S(1)}) custom-call(s32[3]{0:T(128)S(1)} %pad_add_fusion.1.spots, bf16[1024,768]{1,0:T(8,128)(2,1)S(1)} %copy-done.7, f32[8,768]{1,0:T(8,128)S(1)} %reshape.51.vec_ref, bf16[192,2304]{1,0:T(8,128)(2,1)S(1)} %copy-done.50, ...), custom_call_target="tpu_custom_call" | custom-call | flops 1000000 | bytes 100000 | tf_op jit(solution)/shard_map/qkv/pallas_call | solution.py:358
  72.2 1.9 copy-done.5
  74.1 11.4 %attend_forward.2 = (bf16[1024,512]{1,0:T(8,128)(2,1)S(1)}, f32[8,8,1024]{2,1,0:T(8,128)S(1)}) custom-call(s32[1024,1]{1,0:T(8,128)S(1)} %copy.32.seg_col, s32[1,1024]{1,0:T(1,128)S(1)} %copy-done.67, bf16[1024,2304]{1,0:T(8,128)(2,1)S(1)} %get-tuple-element.220.q_ref.k_ref.v_ref, bf16[1024,2304]{1,0:T(8,128)(2,1)S(1)} %get-tuple-element.220.q_ref.k_ref.v_ref, ...), custom_call_target="tpu_custom_call" | custom-call | flops 1000000 | bytes 100000 | tf_op jit(solution)/shard_map/attend_forward/pallas_call | solution.py:93
  85.6 2.0 collective-permute-start.17
  87.6 2.4 collective-permute-start.18
  89.9 5.7 %attend_forward.3 = (bf16[1024,256]{1,0:T(8,128)(2,1)S(1)}, f32[4,8,1024]{2,1,0:T(8,128)S(1)}) custom-call(s32[1024,1]{1,0:T(8,128)S(1)} %copy.32.seg_col, s32[1,1024]{1,0:T(1,128)S(1)} %copy-done.67, bf16[1024,2304]{1,0:T(8,128)(2,1)S(1)} %get-tuple-element.220.q_ref.k_ref.v_ref, bf16[1024,2304]{1,0:T(8,128)(2,1)S(1)} %get-tuple-element.220.q_ref.k_ref.v_ref, ...), custom_call_target="tpu_custom_call" | custom-call | flops 1000000 | bytes 100000 | tf_op jit(solution)/shard_map/attend_forward/pallas_call | solution.py:93
  103.5 18.3 %fc.1 = (bf16[768,768]{1,0:T(8,128)(2,1)S(1)}, bf16[768,3072]{1,0:T(8,128)(2,1)S(1)}, f32[1024,768]{1,0:T(8,128)S(1)}, bf16[1024,768]{1,0:T(8,128)(2,1)S(1)}, bf...) custom-call(s32[3]{0:T(128)S(1)} %pad_add_fusion.1.spots, ...), custom_call_target="tpu_custom_call" | custom-call | flops 1000000 | bytes 100000 | tf_op jit(solution)/shard_map/fc/pallas_call | solution.py:358
  121.8 2.7 copy-done.28
  124.5 2.1 copy-done.38
  127.7 2.8 copy-done.2
  130.5 9.5 %weight_grad.4 = (bf16[4,4,192,384]{3,2,1,0:T(8,128)(2,1)S(1)}, bf16[4,4,192,384]{3,2,1,0:T(8,128)(2,1)S(1)}) custom-call(s32[3]{0:T(128)S(1)} %pad_add_fusion.1.spots, bf16[1024,3072]{1,0:T(8,128)(2,1)S(1)} %copy-done.2, bf16[1024,768]{1,0:T(8,128)(2,1)S(1)} %copy-done.4, bf16[1024,768]{1,0:T(8,128)(2,1)S(1)} %copy-done.4), custom_call_target="tpu_custom_call" | custom-call | flops 1000000 | bytes 100000 | tf_op jit(solution)/shard_map/weight_grad/pallas_call | solution.py:215
  140.2 8.0 %proj.1 = (bf16[3072,768]{1,0:T(8,128)(2,1)S(1)}, bf16[1024,768]{1,0:T(8,128)(2,1)}) custom-call(s32[3]{0:T(128)S(1)} %pad_add_fusion.1.spots, bf16[1024,3072]{1,0:T(8,128)(2,1)S(1)} %copy-done.3, f32[1024,768]{1,0:T(8,128)S(1)} %get-tuple-element.245.resid_ref, f32[8,768]{1,0:T(8,128)S(1)} %reshape.51.vec_ref, bf16[768,768]{1,0:T(8,128)(2,1)S(1)} %copy-done.46, ...), custom_call_target="tpu_custom_call" | custom-call | flops 1000000 | bytes 100000 | tf_op jit(solution)/shard_map/proj/pallas_call | solution.py:358
  148.2 2.1 copy-done.36
  151.4 2.8 copy-done.29
  154.2 2.3 copy-done.37
  156.5 6.9 %back_gelu.1 = (bf16[1024,3072]{1,0:T(8,128)(2,1)S(1)}, f32[8,3072]{1,0:T(8,128)S(1)}, f32[8,768]{1,0:T(8,128)S(1)}) custom-call(s32[3]{0:T(128)S(1)} %pad_add_fusion.1.spots, bf16[1024,768]{1,0:T(8,128)(2,1)S(1)} %copy-done.4, bf16[1024,3072]{1,0:T(8,128)(2,1)S(1)} %copy-done.29, bf16[3072,768]{1,0:T(8,128)(2,1)S(1)} %copy-done.37), custom_call_target="tpu_custom_call" | custom-call | flops 1000000 | bytes 100000 | tf_op jit(solution)/shard_map/back_gelu/pallas_call | solution.py:358
  164.0 9.6 %weight_grad.5 = (bf16[4,4,48,1536]{3,2,1,0:T(8,128)(2,1)S(1)}, bf16[4,4,48,1536]{3,2,1,0:T(8,128)(2,1)S(1)}) custom-call(s32[3]{0:T(128)S(1)} %pad_add_fusion.1.spots, bf16[1024,768]{1,0:T(8,128)(2,1)S(1)} %get-tuple-element.264.x_ref, bf16[1024,3072]{1,0:T(8,128)(2,1)S(1)} %get-tuple-element.271.far_y.near_y.pre_ref, ...), custom_call_target="tpu_custom_call" | custom-call | flops 1000000 | bytes 100000 | tf_op jit(solution)/shard_map/weight_grad/pallas_call | solution.py:215
  173.6 5.4 %collective-permute-done.31 = bf16[2,4,192,384]{3,2,1,0:T(8,128)(2,1)S(1)} collective-permute-done((bf16[2,4,192,384]{3,2,1,0:T(8,128)(2,1)S(1)}, bf16[2,4,192,384]{3,2,1,0:T(8,128)(2,1)S(1)}, u32[]{:S(2)}, u32[]{:S(2)}) %collective-permute-start.31) | collective-permute-done | bytes 1179680 | tf_op jit(solution)/shard_map/ppermute | solution.py:38
  180.9 2.3 copy-done.39
  183.3 11.0 %back_norm.1 = (f32[1024,768]{1,0:T(8,128)S(1)}, bf16[1024,768]{1,0:T(8,128)(2,1)S(1)}, bf16[1024,768]{1,0:T(8,128)(2,1)S(1)}, f32[8,768]{1,0:T(8,128)S(1)}) custom-call(s32[3]{0:T(128)S(1)} %pad_add_fusion.1.spots, bf16[1024,3072]{1,0:T(8,128)(2,1)S(1)} %get-tuple-element.271.far_y.near_y.pre_ref, f32[1024,768]{1,0:T(8,128)S(1)} %copy-done.14, ...), custom_call_target="tpu_custom_call" | custom-call | flops 1000000 | bytes 100000 | tf_op jit(solution)/shard_map/back_norm/pallas_call | solution.py:358
  197.3 23.0 %attend_backward.2 = (bf16[1024,512]{1,0:T(8,128)(2,1)S(1)}, bf16[1024,512]{1,0:T(8,128)(2,1)S(1)}, bf16[1024,512]{1,0:T(8,128)(2,1)S(1)}, f32[8,512]{1,0:T(8,128)S(1)}) custom-call(s32[1024,1]{1,0:T(8,128)S(1)} %copy.32.seg_col, s32[1,1024]{1,0:T(1,128)S(1)} %copy-done.67, bf16[1024,2304]{1,0:T(8,128)(2,1)S(1)} %get-tuple-element.220.q_ref.k_ref.v_ref, ...), custom_call_target="tpu_custom_call" | custom-call | flops 1000000 | bytes 100000 | tf_op jit(solution)/shard_map/attend_backward/pallas_call | solution.py:160
  220.3 4.7 %collective-permute-done.34 = bf16[2,4,48,1536]{3,2,1,0:T(8,128)(2,1)S(1)} collective-permute-done((bf16[2,4,48,1536]{3,2,1,0:T(8,128)(2,1)S(1)}, bf16[2,4,48,1536]{3,2,1,0:T(8,128)(2,1)S(1)}, u32[]{:S(2)}, u32[]{:S(2)}) %collective-permute-start.34) | collective-permute-done | bytes 1179680 | tf_op jit(solution)/shard_map/ppermute | solution.py:38
  226.8 2.2 collective-permute-start.35
  229.0 2.4 collective-permute-start.37
  231.5 6.6 %weight_grad.6 = (bf16[4,4,48,1152]{3,2,1,0:T(8,128)(2,1)}, bf16[4,4,48,1152]{3,2,1,0:T(8,128)(2,1)S(1)}) custom-call(s32[3]{0:T(128)S(1)} %pad_add_fusion.1.spots, bf16[1024,768]{1,0:T(8,128)(2,1)S(1)} %copy-done.24, bf16[1024,512]{1,0:T(8,128)(2,1)S(1)} %get-tuple-element.307.rest_0_.rest_3_.q_ref, ...), custom_call_target="tpu_custom_call" | custom-call | flops 1000000 | bytes 100000 | tf_op jit(solution)/shard_map/weight_grad/pallas_call | solution.py:215
  239.3 3.2 collective-permute-done.36
  249.8 3.3 back_one.1.part_ref
  253.1 3.0 add_convert_fusion.2
  257.7 2.6 collective-permute-start.40
  260.3 2.4 collective-permute-start.42
  262.7 2.3 copy-done.1
  268.4 11.6 %attend_backward.3 = (bf16[1024,256]{1,0:T(8,128)(2,1)S(1)}, bf16[1024,256]{1,0:T(8,128)(2,1)S(1)}, bf16[1024,256]{1,0:T(8,128)(2,1)S(1)}, f32[8,256]{1,0:T(8,128)S(1)}) custom-call(s32[1024,1]{1,0:T(8,128)S(1)} %copy-done.10, s32[1,1024]{1,0:T(1,128)S(1)} %copy-done.67, bf16[1024,2304]{1,0:T(8,128)(2,1)S(1)} %copy-done.1, bf16[1024,2304]{1,0:T(8,128)(2,1)S(1)} %copy-done.1, ...), custom_call_target="tpu_custom_call" | custom-call | flops 1000000 | bytes 100000 | tf_op jit(solution)/shard_map/attend_backward/pallas_call | solution.py:160
  280.2 2.6 weight_grad.7
  284.4 1.9 fusion.13
  286.4 2.1 convert_add_fusion.2
  294.0 1.9 copy-done.41
  295.9 4.4 %back_two.1 = (bf16[1024,768]{1,0:T(8,128)(2,1)}, f32[8,768]{1,0:T(8,128)S(1)}) custom-call(bf16[768,2304]{1,0:T(8,128)(2,1)S(1)} %copy-done.6, bf16[1024,256]{1,0:T(8,128)(2,1)S(1)} %copy-done.31, bf16[1024,256]{1,0:T(8,128)(2,1)S(1)} %copy-done.33, bf16[1024,256]{1,0:T(8,128)(2,1)S(1)} %copy-done.35, f32[1024,768]{1,0:T(8,128)S(1)} %copy-done.12, ...), custom_call_target="tpu_custom_call" | custom-call | flops 1000000 | bytes 100000 | tf_op jit(solution)/shard_map/back_two/pallas_call | solution.py:606
  309.4 2.4 collective-permute-start.55
  321.2 2.0 collective-permute-done.51
  331.1 2.8 collective-permute-done.58.rest_2_
  333.9 2.4 collective-permute-start.61
  340.3 2.2 settle_last.1
  (349 shorter events, 98.4 us)
Async XLA Ops:
  7.2 304.7 %all-gather.5.cloned.1.call-start = ((), (), s32[]{:S(2)}) async-start(), calls=%async_computation | async-start | bytes 1327104 | tf_op jit(solution)/shard_map/all_gather | solution.py:829
  9.1 9.0 %collective-permute-start = (bf16[64,1152]{1,0:T(8,128)(2,1)S(1)}, bf16[64,1152]{1,0:T(8,128)(2,1)S(1)}, u32[]{:S(2)}, u32[]{:S(2)}) collective-permute-start(bf16[64,1152]{1,0:T(8,128)(2,1)S(1)} %fusion.18), channel_id=1, source_target_pairs={{0,1},{1,0},{2,3},{3,2},{4,5},{5,4},{6,7},{7,6},{8,9},{9,8},{10,11... | collective-permute-start | bytes 442376 | tf_op jit(solution)/shard_map/ppermute | solution.py:38
  12.2 14.0 %collective-permute-start.1 = (bf16[64,1152]{1,0:T(8,128)(2,1)S(1)}, bf16[64,1152]{1,0:T(8,128)(2,1)S(1)}, u32[]{:S(2)}, u32[]{:S(2)}) collective-permute-start(bf16[64,1152]{1,0:T(8,128)(2,1)S(1)} %fusion.18), channel_id=1, source_target_pairs={{0,2},{1,3},{2,0},{3,1},{4,6},{5,7},{6,4},{7,5},{8,10},{9,11},{10,... | collective-permute-start | bytes 442376 | tf_op jit(solution)/shard_map/ppermute | solution.py:38
  14.7 11.4 %collective-permute-start.2 = (bf16[64,1152]{1,0:T(8,128)(2,1)S(1)}, bf16[64,1152]{1,0:T(8,128)(2,1)S(1)}, u32[]{:S(2)}, u32[]{:S(2)}) collective-permute-start(bf16[64,1152]{1,0:T(8,128)(2,1)S(1)} %fusion.18), channel_id=1, source_target_pairs={{0,3},{1,2},{2,1},{3,0},{4,7},{5,6},{6,5},{7,4},{8,11},{9,10},{10,... | collective-permute-start | bytes 442376 | tf_op jit(solution)/shard_map/ppermute | solution.py:38
  26.2 20.9 %collective-permute-start.8 = (bf16[48,1920]{1,0:T(8,128)(2,1)S(1)}, bf16[48,1920]{1,0:T(8,128)(2,1)S(1)}, u32[]{:S(2)}, u32[]{:S(2)}) collective-permute-start(bf16[48,1920]{1,0:T(8,128)(2,1)S(1)} %pad_maximum_fusion.3), channel_id=1, source_target_pairs={{0,3},{1,2},{2,1},{3,0},{4,7},{5,6},{6,5},{7,4},{8,11},{9,10},{10,... | collective-permute-start | bytes 552968 | tf_op jit(solution)/shard_map/ppermute | solution.py:38
  28.4 18.7 %collective-permute-start.6 = (bf16[48,1920]{1,0:T(8,128)(2,1)S(1)}, bf16[48,1920]{1,0:T(8,128)(2,1)S(1)}, u32[]{:S(2)}, u32[]{:S(2)}) collective-permute-start(bf16[48,1920]{1,0:T(8,128)(2,1)S(1)} %pad_maximum_fusion.3), channel_id=1, source_target_pairs={{0,1},{1,0},{2,3},{3,2},{4,5},{5,4},{6,7},{7,6},{8,9},{9,8},{10,11... | collective-permute-start | bytes 552968 | tf_op jit(solution)/shard_map/ppermute | solution.py:38
  30.1 10.8 %collective-permute-start.3 = (bf16[3,48,1152]{2,1,0:T(8,128)(2,1)S(1)}, bf16[3,48,1152]{2,1,0:T(8,128)(2,1)S(1)}, u32[]{:S(2)}, u32[]{:S(2)}) collective-permute-start(bf16[3,48,1152]{2,1,0:T(8,128)(2,1)S(1)} %pad_maximum_fusion.2.rest_0_), channel_id=1, source_target_pairs={{0,8},{4,12},{8,0},{12,4},{16,24},{20,28},{24,16},{28,20},{1,9},{5... | collective-permute-start | bytes 995336 | tf_op jit(solution)/shard_map/ppermute | solution.py:38
  31.7 14.9 %collective-permute-start.4 = (bf16[3,48,1152]{2,1,0:T(8,128)(2,1)S(1)}, bf16[3,48,1152]{2,1,0:T(8,128)(2,1)S(1)}, u32[]{:S(2)}, u32[]{:S(2)}) collective-permute-start(bf16[3,48,1152]{2,1,0:T(8,128)(2,1)S(1)} %pad_maximum_fusion.2.rest_0_), channel_id=1, source_target_pairs={{0,16},{4,20},{8,24},{12,28},{16,0},{20,4},{24,8},{28,12},{1,17},{... | collective-permute-start | bytes 995336 | tf_op jit(solution)/shard_map/ppermute | solution.py:38
  33.2 13.3 %collective-permute-start.5 = (bf16[3,48,1152]{2,1,0:T(8,128)(2,1)S(1)}, bf16[3,48,1152]{2,1,0:T(8,128)(2,1)}, u32[]{:S(2)}, u32[]{:S(2)}) collective-permute-start(bf16[3,48,1152]{2,1,0:T(8,128)(2,1)S(1)} %pad_maximum_fusion.2.rest_0_), channel_id=1, source_target_pairs={{0,24},{4,28},{8,16},{12,20},{16,8},{20,12},{24,0},{28,4},{1,25},{... | collective-permute-start | bytes 995336 | tf_op jit(solution)/shard_map/ppermute | solution.py:38
  40.9 8.3 %collective-permute-start.7 = (bf16[48,1920]{1,0:T(8,128)(2,1)S(1)}, bf16[48,1920]{1,0:T(8,128)(2,1)S(1)}, u32[]{:S(2)}, u32[]{:S(2)}) collective-permute-start(bf16[48,1920]{1,0:T(8,128)(2,1)S(1)} %pad_maximum_fusion.3), channel_id=1, source_target_pairs={{0,2},{1,3},{2,0},{3,1},{4,6},{5,7},{6,4},{7,5},{8,10},{9,11},{10,... | collective-permute-start | bytes 552968 | tf_op jit(solution)/shard_map/ppermute | solution.py:38
  53.9 31.5 %collective-permute-start.13 = (bf16[3,48,1920]{2,1,0:T(8,128)(2,1)S(1)}, bf16[3,48,1920]{2,1,0:T(8,128)(2,1)}, u32[]{:S(2)}, u32[]{:S(2)}) collective-permute-start(bf16[3,48,1920]{2,1,0:T(8,128)(2,1)S(1)} %pad_maximum_fusion.rest_0_), channel_id=1, source_target_pairs={{0,8},{4,12},{8,0},{12,4},{16,24},{20,28},{24,16},{28,20},{1,9},{5... | collective-permute-start | bytes 1658888 | tf_op jit(solution)/shard_map/ppermute | solution.py:38
  55.4 30.0 %collective-permute-start.14 = (bf16[3,48,1920]{2,1,0:T(8,128)(2,1)S(1)}, bf16[3,48,1920]{2,1,0:T(8,128)(2,1)}, u32[]{:S(2)}, u32[]{:S(2)}) collective-permute-start(bf16[3,48,1920]{2,1,0:T(8,128)(2,1)S(1)} %pad_maximum_fusion.rest_0_), channel_id=1, source_target_pairs={{0,16},{4,20},{8,24},{12,28},{16,0},{20,4},{24,8},{28,12},{1,17},{... | collective-permute-start | bytes 1658888 | tf_op jit(solution)/shard_map/ppermute | solution.py:38
  56.9 28.5 %collective-permute-start.15 = (bf16[3,48,1920]{2,1,0:T(8,128)(2,1)S(1)}, bf16[3,48,1920]{2,1,0:T(8,128)(2,1)}, u32[]{:S(2)}, u32[]{:S(2)}) collective-permute-start(bf16[3,48,1920]{2,1,0:T(8,128)(2,1)S(1)} %pad_maximum_fusion.rest_0_), channel_id=1, source_target_pairs={{0,24},{4,28},{8,16},{12,20},{16,8},{20,12},{24,0},{28,4},{1,25},{... | collective-permute-start | bytes 1658888 | tf_op jit(solution)/shard_map/ppermute | solution.py:38
  85.5 10.8 %collective-permute-start.16 = (bf16[192,384]{1,0:T(8,128)(2,1)S(1)}, bf16[192,384]{1,0:T(8,128)(2,1)S(1)}, u32[]{:S(2)}, u32[]{:S(2)}) collective-permute-start(bf16[192,384]{1,0:T(8,128)(2,1)S(1)} %copy-done.85), channel_id=1, source_target_pairs={{0,1},{1,0},{2,3},{3,2},{4,5},{5,4},{6,7},{7,6},{8,9},{9,8},{10,11... | collective-permute-start | bytes 442376 | tf_op jit(solution)/shard_map/ppermute | solution.py:38
  85.6 12.3 %collective-permute-start.17 = (bf16[192,384]{1,0:T(8,128)(2,1)S(1)}, bf16[192,384]{1,0:T(8,128)(2,1)S(1)}, u32[]{:S(2)}, u32[]{:S(2)}) collective-permute-start(bf16[192,384]{1,0:T(8,128)(2,1)S(1)} %copy-done.85), channel_id=1, source_target_pairs={{0,2},{1,3},{2,0},{3,1},{4,6},{5,7},{6,4},{7,5},{8,10},{9,11},{10,... | collective-permute-start | bytes 442376 | tf_op jit(solution)/shard_map/ppermute | solution.py:38
  87.6 10.2 %collective-permute-start.18 = (bf16[192,384]{1,0:T(8,128)(2,1)S(1)}, bf16[192,384]{1,0:T(8,128)(2,1)S(1)}, u32[]{:S(2)}, u32[]{:S(2)}) collective-permute-start(bf16[192,384]{1,0:T(8,128)(2,1)S(1)} %copy-done.85), channel_id=1, source_target_pairs={{0,3},{1,2},{2,1},{3,0},{4,7},{5,6},{6,5},{7,4},{8,11},{9,10},{10,... | collective-permute-start | bytes 442376 | tf_op jit(solution)/shard_map/ppermute | solution.py:38
  98.9 27.7 %collective-permute-start.23 = (bf16[3,192,384]{2,1,0:T(8,128)(2,1)S(1)}, bf16[3,192,384]{2,1,0:T(8,128)(2,1)S(1)}, u32[]{:S(2)}, u32[]{:S(2)}) collective-permute-start(bf16[3,192,384]{2,1,0:T(8,128)(2,1)S(1)} %pad_maximum_fusion.1.rest_0_), channel_id=1, source_target_pairs={{0,8},{4,12},{8,0},{12,4},{16,24},{20,28},{24,16},{28,20},{1,9},{5... | collective-permute-start | bytes 1327112 | tf_op jit(solution)/shard_map/ppermute | solution.py:38
  100.5 26.1 %collective-permute-start.24 = (bf16[3,192,384]{2,1,0:T(8,128)(2,1)S(1)}, bf16[3,192,384]{2,1,0:T(8,128)(2,1)S(1)}, u32[]{:S(2)}, u32[]{:S(2)}) collective-permute-start(bf16[3,192,384]{2,1,0:T(8,128)(2,1)S(1)} %pad_maximum_fusion.1.rest_0_), channel_id=1, source_target_pairs={{0,16},{4,20},{8,24},{12,28},{16,0},{20,4},{24,8},{28,12},{1,17},{... | collective-permute-start | bytes 1327112 | tf_op jit(solution)/shard_map/ppermute | solution.py:38
  102.0 24.6 %collective-permute-start.25 = (bf16[3,192,384]{2,1,0:T(8,128)(2,1)S(1)}, bf16[3,192,384]{2,1,0:T(8,128)(2,1)S(1)}, u32[]{:S(2)}, u32[]{:S(2)}) collective-permute-start(bf16[3,192,384]{2,1,0:T(8,128)(2,1)S(1)} %pad_maximum_fusion.1.rest_0_), channel_id=1, source_target_pairs={{0,24},{4,28},{8,16},{12,20},{16,8},{20,12},{24,0},{28,4},{1,25},{... | collective-permute-start | bytes 1327112 | tf_op jit(solution)/shard_map/ppermute | solution.py:38
  126.6 13.4 %collective-permute-start.26 = (bf16[3,192,384]{2,1,0:T(8,128)(2,1)S(1)}, bf16[3,192,384]{2,1,0:T(8,128)(2,1)S(1)}, u32[]{:S(2)}, u32[]{:S(2)}) collective-permute-start(bf16[3,192,384]{2,1,0:T(8,128)(2,1)S(1)} %pad_maximum_fusion.1.rest_0_), channel_id=1, source_target_pairs={{0,4},{4,0},{8,12},{12,8},{16,20},{20,16},{24,28},{28,24},{1,5},{5... | collective-permute-start | bytes 1327112 | tf_op jit(solution)/shard_map/ppermute | solution.py:38
  126.7 13.3 %collective-permute-start.27 = (bf16[3,192,384]{2,1,0:T(8,128)(2,1)S(1)}, bf16[3,192,384]{2,1,0:T(8,128)(2,1)S(1)}, u32[]{:S(2)}, u32[]{:S(2)}) collective-permute-start(bf16[3,192,384]{2,1,0:T(8,128)(2,1)S(1)} %collective-permute-done.23.rest_1_), channel_id=1, source_target_pairs={{0,4},{4,0},{8,12},{12,8},{16,20},{20,16},{24,28},{28,24},{1,5},{5... | collective-permute-start | bytes 1327112 | tf_op jit(solution)/shard_map/ppermute | solution.py:38
  127.2 12.8 %collective-permute-start.28 = (bf16[3,192,384]{2,1,0:T(8,128)(2,1)S(1)}, bf16[3,192,384]{2,1,0:T(8,128)(2,1)S(1)}, u32[]{:S(2)}, u32[]{:S(2)}) collective-permute-start(bf16[3,192,384]{2,1,0:T(8,128)(2,1)S(1)} %collective-permute-done.24.rest_2_), channel_id=1, source_target_pairs={{0,4},{4,0},{8,12},{12,8},{16,20},{20,16},{24,28},{28,24},{1,5},{5... | collective-permute-start | bytes 1327112 | tf_op jit(solution)/shard_map/ppermute | solution.py:38
  127.3 12.8 %collective-permute-start.29 = (bf16[3,192,384]{2,1,0:T(8,128)(2,1)S(1)}, bf16[3,192,384]{2,1,0:T(8,128)(2,1)S(1)}, u32[]{:S(2)}, u32[]{:S(2)}) collective-permute-start(bf16[3,192,384]{2,1,0:T(8,128)(2,1)S(1)} %collective-permute-done.25.rest_3_), channel_id=1, source_target_pairs={{0,4},{4,0},{8,12},{12,8},{16,20},{20,16},{24,28},{28,24},{1,5},{5... | collective-permute-start | bytes 1327112 | tf_op jit(solution)/shard_map/ppermute | solution.py:38
  140.1 10.3 %collective-permute-start.30 = (bf16[4,4,192,384]{3,2,1,0:T(8,128)(2,1)S(1)}, bf16[4,4,192,384]{3,2,1,0:T(8,128)(2,1)S(1)}, u32[]{:S(2)}, u32[]{:S(2)}) collective-permute-start(bf16[4,4,192,384]{3,2,1,0:T(8,128)(2,1)S(1)} %get-tuple-element.259), channel_id=1, source_target_pairs={{0,4},{4,0},{8,12},{12,8},{16,20},{20,16},{24,28},{28,24},{1,5},{5... | collective-permute-start | bytes 7077896 | tf_op jit(solution)/shard_map/ppermute | solution.py:38
  150.6 28.4 %collective-permute-start.31 = (bf16[2,4,192,384]{3,2,1,0:T(8,128)(2,1)S(1)}, bf16[2,4,192,384]{3,2,1,0:T(8,128)(2,1)S(1)}, u32[]{:S(2)}, u32[]{:S(2)}) collective-permute-start(bf16[2,4,192,384]{3,2,1,0:T(8,128)(2,1)S(1)} %add_convert_fusion.1), channel_id=1, source_target_pairs={{0,8},{4,12},{8,0},{12,4},{16,24},{20,28},{24,16},{28,20},{1,9},{5... | collective-permute-start | bytes 3538952 | tf_op jit(solution)/shard_map/ppermute | solution.py:38
  179.0 16.9 %collective-permute-start.32 = (bf16[4,4,48,1536]{3,2,1,0:T(8,128)(2,1)S(1)}, bf16[4,4,48,1536]{3,2,1,0:T(8,128)(2,1)S(1)}, u32[]{:S(2)}, u32[]{:S(2)}) collective-permute-start(bf16[4,4,48,1536]{3,2,1,0:T(8,128)(2,1)S(1)} %get-tuple-element.275), channel_id=1, source_target_pairs={{0,4},{4,0},{8,12},{12,8},{16,20},{20,16},{24,28},{28,24},{1,5},{5... | collective-permute-start | bytes 7077896 | tf_op jit(solution)/shard_map/ppermute | solution.py:38
  179.5 17.0 %collective-permute-start.33 = (bf16[4,192,384]{2,1,0:T(8,128)(2,1)S(1)}, bf16[4,192,384]{2,1,0:T(8,128)(2,1)S(1)}, u32[]{:S(2)}, u32[]{:S(2)}) collective-permute-start(bf16[4,192,384]{2,1,0:T(8,128)(2,1)S(1)} %fusion.3), channel_id=1, source_target_pairs={{0,16},{4,20},{8,24},{12,28},{16,0},{20,4},{24,8},{28,12},{1,17},{... | collective-permute-start | bytes 1769480 | tf_op jit(solution)/shard_map/ppermute | solution.py:38
  196.5 28.4 %collective-permute-start.34 = (bf16[2,4,48,1536]{3,2,1,0:T(8,128)(2,1)S(1)}, bf16[2,4,48,1536]{3,2,1,0:T(8,128)(2,1)S(1)}, u32[]{:S(2)}, u32[]{:S(2)}) collective-permute-start(bf16[2,4,48,1536]{3,2,1,0:T(8,128)(2,1)S(1)} %add_convert_fusion), channel_id=1, source_target_pairs={{0,16},{4,20},{8,24},{12,28},{16,0},{20,4},{24,8},{28,12},{1,17},{... | collective-permute-start | bytes 3538952 | tf_op jit(solution)/shard_map/ppermute | solution.py:38
  225.5 17.1 %collective-permute-start.38 = (bf16[4,48,1536]{2,1,0:T(8,128)(2,1)S(1)}, bf16[4,48,1536]{2,1,0:T(8,128)(2,1)S(1)}, u32[]{:S(2)}, u32[]{:S(2)}) collective-permute-start(bf16[4,48,1536]{2,1,0:T(8,128)(2,1)S(1)} %fusion.4), channel_id=1, source_target_pairs={{0,8},{4,12},{8,0},{12,4},{16,24},{20,28},{24,16},{28,20},{1,9},{5... | collective-permute-start | bytes 1769480 | tf_op jit(solution)/shard_map/ppermute | solution.py:38
  226.8 12.5 %collective-permute-start.35 = (bf16[192,384]{1,0:T(8,128)(2,1)S(1)}, bf16[192,384]{1,0:T(8,128)(2,1)S(1)}, u32[]{:S(2)}, u32[]{:S(2)}) collective-permute-start(bf16[192,384]{1,0:T(8,128)(2,1)S(1)} %get-tuple-element.392), channel_id=1, source_target_pairs={{0,1},{1,0},{2,3},{3,2},{4,5},{5,4},{6,7},{7,6},{8,9},{9,8},{10,11... | collective-permute-start | bytes 442376 | tf_op jit(solution)/shard_map/ppermute | solution.py:38
  229.0 13.5 %collective-permute-start.36 = (bf16[192,384]{1,0:T(8,128)(2,1)S(1)}, bf16[192,384]{1,0:T(8,128)(2,1)S(1)}, u32[]{:S(2)}, u32[]{:S(2)}) collective-permute-start(bf16[192,384]{1,0:T(8,128)(2,1)S(1)} %get-tuple-element.391), channel_id=1, source_target_pairs={{0,2},{1,3},{2,0},{3,1},{4,6},{5,7},{6,4},{7,5},{8,10},{9,11},{10,... | collective-permute-start | bytes 442376 | tf_op jit(solution)/shard_map/ppermute | solution.py:38
  229.0 13.5 %collective-permute-start.37 = (bf16[192,384]{1,0:T(8,128)(2,1)S(1)}, bf16[192,384]{1,0:T(8,128)(2,1)S(1)}, u32[]{:S(2)}, u32[]{:S(2)}) collective-permute-start(bf16[192,384]{1,0:T(8,128)(2,1)S(1)} %get-tuple-element.390), channel_id=1, source_target_pairs={{0,3},{1,2},{2,1},{3,0},{4,7},{5,6},{6,5},{7,4},{8,11},{9,10},{10,... | collective-permute-start | bytes 442376 | tf_op jit(solution)/shard_map/ppermute | solution.py:38
  243.4 9.7 %collective-permute-start.39 = (bf16[4,4,48,1152]{3,2,1,0:T(8,128)(2,1)}, bf16[4,4,48,1152]{3,2,1,0:T(8,128)(2,1)}, u32[]{:S(2)}, u32[]{:S(2)}) collective-permute-start(bf16[4,4,48,1152]{3,2,1,0:T(8,128)(2,1)} %get-tuple-element.310), channel_id=1, source_target_pairs={{0,4},{4,0},{8,12},{12,8},{16,20},{20,16},{24,28},{28,24},{1,5},{5... | collective-permute-start | bytes 5308424 | tf_op jit(solution)/shard_map/ppermute | solution.py:38
  256.1 30.3 %collective-permute-start.43 = (bf16[2,4,48,1152]{3,2,1,0:T(8,128)(2,1)}, bf16[2,4,48,1152]{3,2,1,0:T(8,128)(2,1)}, u32[]{:S(2)}, u32[]{:S(2)}) collective-permute-start(bf16[2,4,48,1152]{3,2,1,0:T(8,128)(2,1)} %add_convert_fusion.2), channel_id=1, source_target_pairs={{0,16},{4,20},{8,24},{12,28},{16,0},{20,4},{24,8},{28,12},{1,17},{... | collective-permute-start | bytes 2654216 | tf_op jit(solution)/shard_map/ppermute | solution.py:38
  257.7 22.4 %collective-permute-start.40 = (bf16[48,1536]{1,0:T(8,128)(2,1)}, bf16[48,1536]{1,0:T(8,128)(2,1)}, u32[]{:S(2)}, u32[]{:S(2)}) collective-permute-start(bf16[48,1536]{1,0:T(8,128)(2,1)} %get-tuple-element.389), channel_id=1, source_target_pairs={{0,1},{1,0},{2,3},{3,2},{4,5},{5,4},{6,7},{7,6},{8,9},{9,8},{10,11... | collective-permute-start | bytes 442376 | tf_op jit(solution)/shard_map/ppermute | solution.py:38
  260.3 19.8 %collective-permute-start.41 = (bf16[48,1536]{1,0:T(8,128)(2,1)}, bf16[48,1536]{1,0:T(8,128)(2,1)}, u32[]{:S(2)}, u32[]{:S(2)}) collective-permute-start(bf16[48,1536]{1,0:T(8,128)(2,1)} %get-tuple-element.388), channel_id=1, source_target_pairs={{0,2},{1,3},{2,0},{3,1},{4,6},{5,7},{6,4},{7,5},{8,10},{9,11},{10,... | collective-permute-start | bytes 442376 | tf_op jit(solution)/shard_map/ppermute | solution.py:38
  260.3 19.9 %collective-permute-start.42 = (bf16[48,1536]{1,0:T(8,128)(2,1)}, bf16[48,1536]{1,0:T(8,128)(2,1)}, u32[]{:S(2)}, u32[]{:S(2)}) collective-permute-start(bf16[48,1536]{1,0:T(8,128)(2,1)} %get-tuple-element.387), channel_id=1, source_target_pairs={{0,3},{1,2},{2,1},{3,0},{4,7},{5,6},{6,5},{7,4},{8,11},{9,10},{10,... | collective-permute-start | bytes 442376 | tf_op jit(solution)/shard_map/ppermute | solution.py:38
  262.7 60.7 %all-gather.7.cloned.1.call-start = ((), (), s32[]{:S(2)}) async-start(), calls=%async_computation.1 | async-start | bytes 1327104 | tf_op jit(solution)/shard_map/all_gather | solution.py:829
  289.4 12.9 %collective-permute-start.46 = (bf16[4,48,1152]{2,1,0:T(8,128)(2,1)}, bf16[4,48,1152]{2,1,0:T(8,128)(2,1)}, u32[]{:S(2)}, u32[]{:S(2)}) collective-permute-start(bf16[4,48,1152]{2,1,0:T(8,128)(2,1)} %fusion.5), channel_id=1, source_target_pairs={{0,8},{4,12},{8,0},{12,4},{16,24},{20,28},{24,16},{28,20},{1,9},{5... | collective-permute-start | bytes 1327112 | tf_op jit(solution)/shard_map/ppermute | solution.py:38
  292.5 9.4 %collective-permute-start.45 = (bf16[2,4,48,384]{3,2,1,0:T(8,128)(2,1)}, bf16[2,4,48,384]{3,2,1,0:T(8,128)(2,1)}, u32[]{:S(2)}, u32[]{:S(2)}) collective-permute-start(bf16[2,4,48,384]{3,2,1,0:T(8,128)(2,1)} %add_convert_fusion.3), channel_id=1, source_target_pairs={{0,16},{4,20},{8,24},{12,28},{16,0},{20,4},{24,8},{28,12},{1,17},{... | collective-permute-start | bytes 884744 | tf_op jit(solution)/shard_map/ppermute | solution.py:38
  304.2 7.6 %collective-permute-start.49 = (f32[16,768]{1,0:T(8,128)S(1)}, f32[16,768]{1,0:T(8,128)S(1)}, u32[]{:S(2)}, u32[]{:S(2)}) collective-permute-start(f32[16,768]{1,0:T(8,128)S(1)} %add.199), channel_id=1, source_target_pairs={{0,8},{4,12},{8,0},{12,4},{16,24},{20,28},{24,16},{28,20},{1,9},{5... | collective-permute-start | bytes 147464 | tf_op jit(solution)/shard_map/ppermute | solution.py:38
  307.4 7.7 %collective-permute-start.53 = (bf16[48,1152]{1,0:T(8,128)(2,1)S(1)}, bf16[48,1152]{1,0:T(8,128)(2,1)S(1)}, u32[]{:S(2)}, u32[]{:S(2)}) collective-permute-start(bf16[48,1152]{1,0:T(8,128)(2,1)S(1)} %get-tuple-element.399), channel_id=1, source_target_pairs={{0,1},{1,0},{2,3},{3,2},{4,5},{5,4},{6,7},{7,6},{8,9},{9,8},{10,11... | collective-permute-start | bytes 331784 | tf_op jit(solution)/shard_map/ppermute | solution.py:38
  308.5 12.6 %collective-permute-start.54 = (bf16[48,1152]{1,0:T(8,128)(2,1)S(1)}, bf16[48,1152]{1,0:T(8,128)(2,1)S(1)}, u32[]{:S(2)}, u32[]{:S(2)}) collective-permute-start(bf16[48,1152]{1,0:T(8,128)(2,1)S(1)} %get-tuple-element.398), channel_id=1, source_target_pairs={{0,2},{1,3},{2,0},{3,1},{4,6},{5,7},{6,4},{7,5},{8,10},{9,11},{10,... | collective-permute-start | bytes 331784 | tf_op jit(solution)/shard_map/ppermute | solution.py:38
  309.4 11.7 %collective-permute-start.55 = (bf16[48,1152]{1,0:T(8,128)(2,1)S(1)}, bf16[48,1152]{1,0:T(8,128)(2,1)S(1)}, u32[]{:S(2)}, u32[]{:S(2)}) collective-permute-start(bf16[48,1152]{1,0:T(8,128)(2,1)S(1)} %get-tuple-element.397), channel_id=1, source_target_pairs={{0,3},{1,2},{2,1},{3,0},{4,7},{5,6},{6,5},{7,4},{8,11},{9,10},{10,... | collective-permute-start | bytes 331784 | tf_op jit(solution)/shard_map/ppermute | solution.py:38
  315.1 8.0 %collective-permute-start.51 = (bf16[48,384]{1,0:T(8,128)(2,1)S(1)}, bf16[48,384]{1,0:T(8,128)(2,1)S(1)}, u32[]{:S(2)}, u32[]{:S(2)}) collective-permute-start(bf16[48,384]{1,0:T(8,128)(2,1)S(1)} %get-tuple-element.401), channel_id=1, source_target_pairs={{0,2},{1,3},{2,0},{3,1},{4,6},{5,7},{6,4},{7,5},{8,10},{9,11},{10,... | collective-permute-start | bytes 110600 | tf_op jit(solution)/shard_map/ppermute | solution.py:38
  323.4 7.7 %collective-permute-start.57 = (bf16[48,1536]{1,0:T(8,128)(2,1)S(1)}, bf16[48,1536]{1,0:T(8,128)(2,1)S(1)}, u32[]{:S(2)}, u32[]{:S(2)}) collective-permute-start(bf16[48,1536]{1,0:T(8,128)(2,1)S(1)} %pad_maximum_fusion.4.rest_0_), channel_id=1, source_target_pairs={{0,8},{4,12},{8,0},{12,4},{16,24},{20,28},{24,16},{28,20},{1,9},{5... | collective-permute-start | bytes 442376 | tf_op jit(solution)/shard_map/ppermute | solution.py:38
  325.0 8.9 %collective-permute-start.58 = (bf16[48,1536]{1,0:T(8,128)(2,1)S(1)}, bf16[48,1536]{1,0:T(8,128)(2,1)S(1)}, u32[]{:S(2)}, u32[]{:S(2)}) collective-permute-start(bf16[48,1536]{1,0:T(8,128)(2,1)S(1)} %pad_maximum_fusion.4.rest_0_), channel_id=1, source_target_pairs={{0,16},{4,20},{8,24},{12,28},{16,0},{20,4},{24,8},{28,12},{1,17},{... | collective-permute-start | bytes 442376 | tf_op jit(solution)/shard_map/ppermute | solution.py:38
  325.5 8.4 %collective-permute-start.59 = (bf16[48,1536]{1,0:T(8,128)(2,1)S(1)}, bf16[48,1536]{1,0:T(8,128)(2,1)S(1)}, u32[]{:S(2)}, u32[]{:S(2)}) collective-permute-start(bf16[48,1536]{1,0:T(8,128)(2,1)S(1)} %pad_maximum_fusion.4.rest_0_), channel_id=1, source_target_pairs={{0,24},{4,28},{8,16},{12,20},{16,8},{20,12},{24,0},{28,4},{1,25},{... | collective-permute-start | bytes 442376 | tf_op jit(solution)/shard_map/ppermute | solution.py:38
  (107 other events, 944.9 us)
Sparse Core Ops, SparseCore 0:
  262.8 23.7 all-gather.4
  300.7 22.5 all-gather.6

commit v5 on v4

--- a/solution.py
+++ b/solution.py
@@ -15,6 +15,7 @@
 BF16 = jnp.bfloat16
 F32 = jnp.float32
 VMEM_LIMIT = 24 << 20
+WIDE_LIMIT = 56 << 20
 SMALL_COST = pl.CostEstimate(flops=10**6, bytes_accessed=10**5, transcendentals=0)
 
 
@@ -30,8 +31,8 @@
     return lax.dot_general(a, b, (((0,), (0,)), ((), ())), preferred_element_type=F32)
 
 
-def params():
-    return pltpu.CompilerParams(vmem_limit_bytes=VMEM_LIMIT)
+def params(limit=VMEM_LIMIT):
+    return pltpu.CompilerParams(vmem_limit_bytes=limit)
 
 
 def swap(value, axis, size, mask):
@@ -369,7 +370,7 @@
             scratch_shapes=[pltpu.SemaphoreType.DMA((sem_count,))] * sem_sets,
         ),
         out_shape=[jax.ShapeDtypeStruct(shape, dtype) for shape, dtype, _ in outs],
-        compiler_params=params(),
+        compiler_params=params(WIDE_LIMIT if name == "qkv" else VMEM_LIMIT),
         cost_estimate=SMALL_COST,
         name=name,
     )(spots, *rows_in, *whole_in, *parts_in)

time: 353 us -> 355 us (level)
  local copies, waits for them, and re-layouts: 59.4 us -> 51.8 us
  Pallas kernels: 145 us -> 149 us
  other arithmetic: 19.1 us -> 22.9 us
    unnamed x180 -> x166, local copies, waits for them, and re-layouts: 50.8 us -> 41.4 us
    pallas_call x5, Pallas kernels: 52.4 us -> 56.3 us  [row_call(): pl.pallas_call(kernel, grid_spec=pltpu.PrefetchScalarGridSpec(num_scalar_...]
  transfers between devices with their start and end apart: 68 -> 68, of which waited for: 19 -> 18; matrix products, arithmetic and copies ran while one was open for 6% -> 7% of each run, Pallas kernels for 41% -> 42%
where the time goes in v5:
time: 355 us; the launch traced here: 352 us
  Pallas kernels  149 us (42%)
  starting transfers between devices  65 us (18%)
  local copies, waits for them, and re-layouts  51.8 us (15%)
  waiting for transfers between devices  47.4 us (13%)
  other arithmetic  22.9 us (6%)
  between operations  15.7 us (4%)
    ppermute x66, starting transfers between devices, swap(): return lax.ppermute(value, axis, [(i, i ^ mask) for i in range(size)])  64.9 us
    pallas_call x5, Pallas kernels, row_call(): pl.pallas_call(kernel, grid_spec=pltpu.PrefetchScalarGridSpec(num_scalar_...  56.3 us
    ppermute x66, waiting for transfers between devices, swap(): return lax.ppermute(value, axis, [(i, i ^ mask) for i in range(size)])  47 us
    unnamed x166, local copies, waits for them, and re-layouts  41.4 us
    pallas_call x2, Pallas kernels, attend_backward(): pl.pallas_call(functools.partial(attend_back_kernel, rows), grid=(count,)...  34.6 us
    pallas_call x4, Pallas kernels, grad_call(): pl.pallas_call(kernel, grid_spec=pltpu.PrefetchScalarGridSpec(num_scalar_...  28.4 us
    pallas_call x2, Pallas kernels, attend_forward(): pl.pallas_call(functools.partial(attend_kernel, rows), grid=(count,), in_...  17.1 us
    convert_element_type x4, other arithmetic, sent_part(): return summed(near[half_pieces:], old[half_pieces:]).astype(BF16)  7.18 us
  transfers between devices with their start and end apart: 68, of which 18 were waited for; matrix products, arithmetic and copies ran while one was open for 7% of the time, Pallas kernels for 42%

profile of v5, /device:TPU:0, one launch (start us, length us, event | category | flops | bytes accessed | tf_op | source)
XLA Modules:
  0.0 352.1 jit_solution(12405640120905526868)
XLA Ops:
  9.1 3.1 collective-permute-start
  12.2 2.6 collective-permute-start.1
  18.1 8.1 %collective-permute-done.1 = bf16[64,1152]{1,0:T(8,128)(2,1)S(1)} collective-permute-done((bf16[64,1152]{1,0:T(8,128)(2,1)S(1)}, bf16[64,1152]{1,0:T(8,128)(2,1)S(1)}, u32[]{:S(2)}, u32[]{:S(2)}) %collective-permute-start.1) | collective-permute-done | bytes 147488 | tf_op jit(solution)/shard_map/ppermute | solution.py:39
  26.2 2.3 collective-permute-start.8
  33.9 7.1 %collective-permute-done.3.rest_1_ = bf16[3,48,1152]{2,1,0:T(8,128)(2,1)S(1)} collective-permute-done((bf16[3,48,1152]{2,1,0:T(8,128)(2,1)S(1)}, bf16[3,48,1152]{2,1,0:T(8,128)(2,1)S(1)}, u32[]{:S(2)}, u32[]{:S(2)}) %collective-permute-start.3) | collective-permute-done | bytes 331808 | tf_op jit(solution)/shard_map/ppermute | solution.py:39
  42.3 4.2 %collective-permute-done.4.rest_2_ = bf16[3,48,1152]{2,1,0:T(8,128)(2,1)S(1)} collective-permute-done((bf16[3,48,1152]{2,1,0:T(8,128)(2,1)S(1)}, bf16[3,48,1152]{2,1,0:T(8,128)(2,1)S(1)}, u32[]{:S(2)}, u32[]{:S(2)}) %collective-permute-start.4) | collective-permute-done | bytes 331808 | tf_op jit(solution)/shard_map/ppermute | solution.py:39
  57.2 11.1 %qkv.1 = (bf16[768,2304]{1,0:T(8,128)(2,1)}, bf16[1024,768]{1,0:T(8,128)(2,1)}, bf16[1024,2304]{1,0:T(8,128)(2,1)}) custom-call(s32[3]{0:T(128)} %pad_add_fusion.1.spots, bf16[1024,768]{1,0:T(8,128)(2,1)} %x_ref.5, f32[8,768]{1,0:T(8,128)} %reshape.51.vec_ref, bf16[192,2304]{1,0:T(8,128)(2,1)} %own_ref.2, bf16[3,48,1152]{2,1,0:T(8,128)(2,1)} %copy-done.64, ...), custom_call_target="tpu_custom_call" | custom-call | flops 1000000 | bytes 100000 | tf_op jit(solution)/shard_map/qkv/pallas_call | solution.py:359
  68.3 2.3 copy-done
  70.6 11.4 %attend_forward.2 = (bf16[1024,512]{1,0:T(8,128)(2,1)S(1)}, f32[8,8,1024]{2,1,0:T(8,128)S(1)}) custom-call(s32[1024,1]{1,0:T(8,128)S(1)} %copy.32.seg_col, s32[1,1024]{1,0:T(1,128)S(1)} %copy-done.50, bf16[1024,2304]{1,0:T(8,128)(2,1)S(1)} %copy-done, bf16[1024,2304]{1,0:T(8,128)(2,1)S(1)} %copy-done, bf16[1024,2304]{1,0:T(8,128)(2,1)S(1)} %copy-done), custom_call_target="tpu_custom_call" | custom-call | flops 1000000 | bytes 100000 | tf_op jit(solution)/shard_map/attend_forward/pallas_call | solution.py:94
  82.2 2.0 collective-permute-start.17
  84.2 2.3 collective-permute-start.18
  86.5 5.7 %attend_forward.3 = (bf16[1024,256]{1,0:T(8,128)(2,1)S(1)}, f32[4,8,1024]{2,1,0:T(8,128)S(1)}) custom-call(s32[1024,1]{1,0:T(8,128)S(1)} %copy.32.seg_col, s32[1,1024]{1,0:T(1,128)S(1)} %copy-done.50, bf16[1024,2304]{1,0:T(8,128)(2,1)S(1)} %copy-done, bf16[1024,2304]{1,0:T(8,128)(2,1)S(1)} %copy-done, bf16[1024,2304]{1,0:T(8,128)(2,1)S(1)} %copy-done), custom_call_target="tpu_custom_call" | custom-call | flops 1000000 | bytes 100000 | tf_op jit(solution)/shard_map/attend_forward/pallas_call | solution.py:94
  92.3 2.2 collective-permute-done.17
  99.4 18.8 %fc.1 = (bf16[768,768]{1,0:T(8,128)(2,1)S(1)}, bf16[768,3072]{1,0:T(8,128)(2,1)S(1)}, f32[1024,768]{1,0:T(8,128)S(1)}, bf16[1024,768]{1,0:T(8,128)(2,1)S(1)}, bf...) custom-call(s32[3]{0:T(128)S(1)} %copy-done.53, ...), custom_call_target="tpu_custom_call" | custom-call | flops 1000000 | bytes 100000 | tf_op jit(solution)/shard_map/fc/pallas_call | solution.py:359
  118.2 2.7 copy-done.24
  122.0 4.3 %copy-done.2 = bf16[1024,3072]{1,0:T(8,128)(2,1)S(1)} copy-done((bf16[1024,3072]{1,0:T(8,128)(2,1)S(1)}, bf16[1024,3072]{1,0:T(8,128)(2,1)}, u32[]{:S(2)}) %copy-start.2) | copy-done | bytes 6291480
  126.3 9.5 %weight_grad.4 = (bf16[4,4,192,384]{3,2,1,0:T(8,128)(2,1)S(1)}, bf16[4,4,192,384]{3,2,1,0:T(8,128)(2,1)S(1)}) custom-call(s32[3]{0:T(128)S(1)} %copy-done.53, bf16[1024,3072]{1,0:T(8,128)(2,1)S(1)} %copy-done.2, bf16[1024,768]{1,0:T(8,128)(2,1)S(1)} %copy-done.4, bf16[1024,768]{1,0:T(8,128)(2,1)S(1)} %copy-done.4), custom_call_target="tpu_custom_call" | custom-call | flops 1000000 | bytes 100000 | tf_op jit(solution)/shard_map/weight_grad/pallas_call | solution.py:216
  135.9 8.1 %proj.1 = (bf16[3072,768]{1,0:T(8,128)(2,1)S(1)}, bf16[1024,768]{1,0:T(8,128)(2,1)}) custom-call(s32[3]{0:T(128)S(1)} %copy-done.53, bf16[1024,3072]{1,0:T(8,128)(2,1)S(1)} %copy-done.3, f32[1024,768]{1,0:T(8,128)S(1)} %get-tuple-element.245.resid_ref, f32[8,768]{1,0:T(8,128)S(1)} %copy-done.44, bf16[768,768]{1,0:T(8,128)(2,1)S(1)} %copy-done.40, ...), custom_call_target="tpu_custom_call" | custom-call | flops 1000000 | bytes 100000 | tf_op jit(solution)/shard_map/proj/pallas_call | solution.py:359
  144.1 2.2 copy-done.32
  147.7 2.8 copy-done.25
  150.5 2.3 copy-done.33
  152.8 7.0 %back_gelu.1 = (bf16[1024,3072]{1,0:T(8,128)(2,1)S(1)}, f32[8,3072]{1,0:T(8,128)S(1)}, f32[8,768]{1,0:T(8,128)S(1)}) custom-call(s32[3]{0:T(128)S(1)} %copy-done.53, bf16[1024,768]{1,0:T(8,128)(2,1)S(1)} %copy-done.4, bf16[1024,3072]{1,0:T(8,128)(2,1)S(1)} %copy-done.25, bf16[3072,768]{1,0:T(8,128)(2,1)S(1)} %copy-done.33), custom_call_target="tpu_custom_call" | custom-call | flops 1000000 | bytes 100000 | tf_op jit(solution)/shard_map/back_gelu/pallas_call | solution.py:359
  160.5 9.7 %weight_grad.5 = (bf16[4,4,48,1536]{3,2,1,0:T(8,128)(2,1)S(1)}, bf16[4,4,48,1536]{3,2,1,0:T(8,128)(2,1)S(1)}) custom-call(s32[3]{0:T(128)S(1)} %copy-done.53, bf16[1024,768]{1,0:T(8,128)(2,1)S(1)} %get-tuple-element.264.x_ref, bf16[1024,3072]{1,0:T(8,128)(2,1)S(1)} %get-tuple-element.271.far_y.near_y.pre_ref, ...), custom_call_target="tpu_custom_call" | custom-call | flops 1000000 | bytes 100000 | tf_op jit(solution)/shard_map/weight_grad/pallas_call | solution.py:216
  170.2 4.9 %collective-permute-done.31 = bf16[2,4,192,384]{3,2,1,0:T(8,128)(2,1)S(1)} collective-permute-done((bf16[2,4,192,384]{3,2,1,0:T(8,128)(2,1)S(1)}, bf16[2,4,192,384]{3,2,1,0:T(8,128)(2,1)S(1)}, u32[]{:S(2)}, u32[]{:S(2)}) %collective-permute-start.31) | collective-permute-done | bytes 1179680 | tf_op jit(solution)/shard_map/ppermute | solution.py:39
  176.9 2.5 copy-done.35
  179.4 11.2 %back_norm.1 = (f32[1024,768]{1,0:T(8,128)S(1)}, bf16[1024,768]{1,0:T(8,128)(2,1)S(1)}, bf16[1024,768]{1,0:T(8,128)(2,1)S(1)}, f32[8,768]{1,0:T(8,128)S(1)}) custom-call(s32[3]{0:T(128)S(1)} %copy-done.53, bf16[1024,3072]{1,0:T(8,128)(2,1)S(1)} %get-tuple-element.271.far_y.near_y.pre_ref, f32[1024,768]{1,0:T(8,128)S(1)} %copy-done.13, ...), custom_call_target="tpu_custom_call" | custom-call | flops 1000000 | bytes 100000 | tf_op jit(solution)/shard_map/back_norm/pallas_call | solution.py:359
  192.4 2.2 add_convert_fusion
  196.2 23.0 %attend_backward.2 = (bf16[1024,512]{1,0:T(8,128)(2,1)S(1)}, bf16[1024,512]{1,0:T(8,128)(2,1)S(1)}, bf16[1024,512]{1,0:T(8,128)(2,1)S(1)}, f32[8,512]{1,0:T(8,128)S(1)}) custom-call(s32[1024,1]{1,0:T(8,128)S(1)} %copy.32.seg_col, s32[1,1024]{1,0:T(1,128)S(1)} %copy-done.50, bf16[1024,2304]{1,0:T(8,128)(2,1)S(1)} %bitcast.135, ...), custom_call_target="tpu_custom_call" | custom-call | flops 1000000 | bytes 100000 | tf_op jit(solution)/shard_map/attend_backward/pallas_call | solution.py:161
  219.2 3.8 %collective-permute-done.34 = bf16[2,4,48,1536]{3,2,1,0:T(8,128)(2,1)S(1)} collective-permute-done((bf16[2,4,48,1536]{3,2,1,0:T(8,128)(2,1)S(1)}, bf16[2,4,48,1536]{3,2,1,0:T(8,128)(2,1)S(1)}, u32[]{:S(2)}, u32[]{:S(2)}) %collective-permute-start.34) | collective-permute-done | bytes 1179680 | tf_op jit(solution)/shard_map/ppermute | solution.py:39
  223.0 3.1 convert_add_fusion
  228.8 2.2 collective-permute-start.35
  231.0 2.4 collective-permute-start.37
  233.4 6.7 %weight_grad.6 = (bf16[4,4,48,1152]{3,2,1,0:T(8,128)(2,1)}, bf16[4,4,48,1152]{3,2,1,0:T(8,128)(2,1)S(1)}) custom-call(s32[3]{0:T(128)S(1)} %copy-done.53, bf16[1024,768]{1,0:T(8,128)(2,1)S(1)} %copy-done.20, bf16[1024,512]{1,0:T(8,128)(2,1)S(1)} %get-tuple-element.307.rest_0_.rest_3_.q_ref, bf16[1024,512]{1,0:T(8,128)(2,1)S(1)} %get-tuple-element.308.rest_1_.rest_4_.k_ref, ...), custom_call_target="tpu_custom_call" | custom-call | flops 1000000 | bytes 100000 | tf_op jit(solution)/shard_map/weight_grad/pallas_call | solution.py:216
  241.3 3.0 collective-permute-done.36
  251.5 3.3 back_one.1.part_ref
  254.8 3.0 add_convert_fusion.2
  259.9 2.6 collective-permute-start.40
  262.5 2.4 collective-permute-start.42
  265.0 2.3 copy-done.1
  270.7 11.6 %attend_backward.3 = (bf16[1024,256]{1,0:T(8,128)(2,1)S(1)}, bf16[1024,256]{1,0:T(8,128)(2,1)S(1)}, bf16[1024,256]{1,0:T(8,128)(2,1)S(1)}, f32[8,256]{1,0:T(8,128)S(1)}) custom-call(s32[1024,1]{1,0:T(8,128)S(1)} %copy-done.9, s32[1,1024]{1,0:T(1,128)S(1)} %copy-done.50, bf16[1024,2304]{1,0:T(8,128)(2,1)S(1)} %copy-done.1, bf16[1024,2304]{1,0:T(8,128)(2,1)S(1)} %copy-done.1, ...), custom_call_target="tpu_custom_call" | custom-call | flops 1000000 | bytes 100000 | tf_op jit(solution)/shard_map/attend_backward/pallas_call | solution.py:161
  282.4 2.6 weight_grad.7
  288.7 2.1 convert_add_fusion.2
  297.9 4.4 %back_two.1 = (bf16[1024,768]{1,0:T(8,128)(2,1)}, f32[8,768]{1,0:T(8,128)S(1)}) custom-call(bf16[768,2304]{1,0:T(8,128)(2,1)S(1)} %copy-done.5, bf16[1024,256]{1,0:T(8,128)(2,1)S(1)} %copy-done.27, bf16[1024,256]{1,0:T(8,128)(2,1)S(1)} %copy-done.29, bf16[1024,256]{1,0:T(8,128)(2,1)S(1)} %copy-done.31, f32[1024,768]{1,0:T(8,128)S(1)} %copy-done.11, ...), custom_call_target="tpu_custom_call" | custom-call | flops 1000000 | bytes 100000 | tf_op jit(solution)/shard_map/back_two/pallas_call | solution.py:607
  311.7 2.4 collective-permute-start.55
  323.3 2.1 collective-permute-done.51
  333.5 2.8 collective-permute-done.58.rest_2_
  336.3 2.4 collective-permute-start.61
  342.7 2.2 settle_last.1
  (336 shorter events, 93.5 us)
Async XLA Ops:
  7.2 307.0 %all-gather.5.cloned.1.call-start = ((), (), s32[]{:S(2)}) async-start(), calls=%async_computation | async-start | bytes 1327104 | tf_op jit(solution)/shard_map/all_gather | solution.py:830
  9.1 9.0 %collective-permute-start = (bf16[64,1152]{1,0:T(8,128)(2,1)S(1)}, bf16[64,1152]{1,0:T(8,128)(2,1)S(1)}, u32[]{:S(2)}, u32[]{:S(2)}) collective-permute-start(bf16[64,1152]{1,0:T(8,128)(2,1)S(1)} %fusion.18), channel_id=1, source_target_pairs={{0,1},{1,0},{2,3},{3,2},{4,5},{5,4},{6,7},{7,6},{8,9},{9,8},{10,11... | collective-permute-start | bytes 442376 | tf_op jit(solution)/shard_map/ppermute | solution.py:39
  12.2 14.0 %collective-permute-start.1 = (bf16[64,1152]{1,0:T(8,128)(2,1)S(1)}, bf16[64,1152]{1,0:T(8,128)(2,1)S(1)}, u32[]{:S(2)}, u32[]{:S(2)}) collective-permute-start(bf16[64,1152]{1,0:T(8,128)(2,1)S(1)} %fusion.18), channel_id=1, source_target_pairs={{0,2},{1,3},{2,0},{3,1},{4,6},{5,7},{6,4},{7,5},{8,10},{9,11},{10,... | collective-permute-start | bytes 442376 | tf_op jit(solution)/shard_map/ppermute | solution.py:39
  14.7 11.4 %collective-permute-start.2 = (bf16[64,1152]{1,0:T(8,128)(2,1)S(1)}, bf16[64,1152]{1,0:T(8,128)(2,1)S(1)}, u32[]{:S(2)}, u32[]{:S(2)}) collective-permute-start(bf16[64,1152]{1,0:T(8,128)(2,1)S(1)} %fusion.18), channel_id=1, source_target_pairs={{0,3},{1,2},{2,1},{3,0},{4,7},{5,6},{6,5},{7,4},{8,11},{9,10},{10,... | collective-permute-start | bytes 442376 | tf_op jit(solution)/shard_map/ppermute | solution.py:39
  26.2 21.0 %collective-permute-start.8 = (bf16[48,1920]{1,0:T(8,128)(2,1)S(1)}, bf16[48,1920]{1,0:T(8,128)(2,1)S(1)}, u32[]{:S(2)}, u32[]{:S(2)}) collective-permute-start(bf16[48,1920]{1,0:T(8,128)(2,1)S(1)} %pad_maximum_fusion.3), channel_id=1, source_target_pairs={{0,3},{1,2},{2,1},{3,0},{4,7},{5,6},{6,5},{7,4},{8,11},{9,10},{10,... | collective-permute-start | bytes 552968 | tf_op jit(solution)/shard_map/ppermute | solution.py:39
  28.4 18.8 %collective-permute-start.6 = (bf16[48,1920]{1,0:T(8,128)(2,1)S(1)}, bf16[48,1920]{1,0:T(8,128)(2,1)S(1)}, u32[]{:S(2)}, u32[]{:S(2)}) collective-permute-start(bf16[48,1920]{1,0:T(8,128)(2,1)S(1)} %pad_maximum_fusion.3), channel_id=1, source_target_pairs={{0,1},{1,0},{2,3},{3,2},{4,5},{5,4},{6,7},{7,6},{8,9},{9,8},{10,11... | collective-permute-start | bytes 552968 | tf_op jit(solution)/shard_map/ppermute | solution.py:39
  30.1 10.8 %collective-permute-start.3 = (bf16[3,48,1152]{2,1,0:T(8,128)(2,1)S(1)}, bf16[3,48,1152]{2,1,0:T(8,128)(2,1)S(1)}, u32[]{:S(2)}, u32[]{:S(2)}) collective-permute-start(bf16[3,48,1152]{2,1,0:T(8,128)(2,1)S(1)} %pad_maximum_fusion.2.rest_0_), channel_id=1, source_target_pairs={{0,8},{4,12},{8,0},{12,4},{16,24},{20,28},{24,16},{28,20},{1,9},{5... | collective-permute-start | bytes 995336 | tf_op jit(solution)/shard_map/ppermute | solution.py:39
  31.7 14.9 %collective-permute-start.4 = (bf16[3,48,1152]{2,1,0:T(8,128)(2,1)S(1)}, bf16[3,48,1152]{2,1,0:T(8,128)(2,1)S(1)}, u32[]{:S(2)}, u32[]{:S(2)}) collective-permute-start(bf16[3,48,1152]{2,1,0:T(8,128)(2,1)S(1)} %pad_maximum_fusion.2.rest_0_), channel_id=1, source_target_pairs={{0,16},{4,20},{8,24},{12,28},{16,0},{20,4},{24,8},{28,12},{1,17},{... | collective-permute-start | bytes 995336 | tf_op jit(solution)/shard_map/ppermute | solution.py:39
  33.2 13.3 %collective-permute-start.5 = (bf16[3,48,1152]{2,1,0:T(8,128)(2,1)S(1)}, bf16[3,48,1152]{2,1,0:T(8,128)(2,1)S(1)}, u32[]{:S(2)}, u32[]{:S(2)}) collective-permute-start(bf16[3,48,1152]{2,1,0:T(8,128)(2,1)S(1)} %pad_maximum_fusion.2.rest_0_), channel_id=1, source_target_pairs={{0,24},{4,28},{8,16},{12,20},{16,8},{20,12},{24,0},{28,4},{1,25},{... | collective-permute-start | bytes 995336 | tf_op jit(solution)/shard_map/ppermute | solution.py:39
  40.9 8.3 %collective-permute-start.7 = (bf16[48,1920]{1,0:T(8,128)(2,1)S(1)}, bf16[48,1920]{1,0:T(8,128)(2,1)S(1)}, u32[]{:S(2)}, u32[]{:S(2)}) collective-permute-start(bf16[48,1920]{1,0:T(8,128)(2,1)S(1)} %pad_maximum_fusion.3), channel_id=1, source_target_pairs={{0,2},{1,3},{2,0},{3,1},{4,6},{5,7},{6,4},{7,5},{8,10},{9,11},{10,... | collective-permute-start | bytes 552968 | tf_op jit(solution)/shard_map/ppermute | solution.py:39
  52.6 29.5 %collective-permute-start.13 = (bf16[3,48,1920]{2,1,0:T(8,128)(2,1)S(1)}, bf16[3,48,1920]{2,1,0:T(8,128)(2,1)S(1)}, u32[]{:S(2)}, u32[]{:S(2)}) collective-permute-start(bf16[3,48,1920]{2,1,0:T(8,128)(2,1)S(1)} %pad_maximum_fusion.rest_0_), channel_id=1, source_target_pairs={{0,8},{4,12},{8,0},{12,4},{16,24},{20,28},{24,16},{28,20},{1,9},{5... | collective-permute-start | bytes 1658888 | tf_op jit(solution)/shard_map/ppermute | solution.py:39
  54.1 28.0 %collective-permute-start.14 = (bf16[3,48,1920]{2,1,0:T(8,128)(2,1)S(1)}, bf16[3,48,1920]{2,1,0:T(8,128)(2,1)S(1)}, u32[]{:S(2)}, u32[]{:S(2)}) collective-permute-start(bf16[3,48,1920]{2,1,0:T(8,128)(2,1)S(1)} %pad_maximum_fusion.rest_0_), channel_id=1, source_target_pairs={{0,16},{4,20},{8,24},{12,28},{16,0},{20,4},{24,8},{28,12},{1,17},{... | collective-permute-start | bytes 1658888 | tf_op jit(solution)/shard_map/ppermute | solution.py:39
  55.6 26.5 %collective-permute-start.15 = (bf16[3,48,1920]{2,1,0:T(8,128)(2,1)S(1)}, bf16[3,48,1920]{2,1,0:T(8,128)(2,1)S(1)}, u32[]{:S(2)}, u32[]{:S(2)}) collective-permute-start(bf16[3,48,1920]{2,1,0:T(8,128)(2,1)S(1)} %pad_maximum_fusion.rest_0_), channel_id=1, source_target_pairs={{0,24},{4,28},{8,16},{12,20},{16,8},{20,12},{24,0},{28,4},{1,25},{... | collective-permute-start | bytes 1658888 | tf_op jit(solution)/shard_map/ppermute | solution.py:39
  82.1 10.2 %collective-permute-start.16 = (bf16[192,384]{1,0:T(8,128)(2,1)S(1)}, bf16[192,384]{1,0:T(8,128)(2,1)S(1)}, u32[]{:S(2)}, u32[]{:S(2)}) collective-permute-start(bf16[192,384]{1,0:T(8,128)(2,1)S(1)} %copy-done.77), channel_id=1, source_target_pairs={{0,1},{1,0},{2,3},{3,2},{4,5},{5,4},{6,7},{7,6},{8,9},{9,8},{10,11... | collective-permute-start | bytes 442376 | tf_op jit(solution)/shard_map/ppermute | solution.py:39
  82.2 12.3 %collective-permute-start.17 = (bf16[192,384]{1,0:T(8,128)(2,1)S(1)}, bf16[192,384]{1,0:T(8,128)(2,1)S(1)}, u32[]{:S(2)}, u32[]{:S(2)}) collective-permute-start(bf16[192,384]{1,0:T(8,128)(2,1)S(1)} %copy-done.77), channel_id=1, source_target_pairs={{0,2},{1,3},{2,0},{3,1},{4,6},{5,7},{6,4},{7,5},{8,10},{9,11},{10,... | collective-permute-start | bytes 442376 | tf_op jit(solution)/shard_map/ppermute | solution.py:39
  84.2 10.3 %collective-permute-start.18 = (bf16[192,384]{1,0:T(8,128)(2,1)S(1)}, bf16[192,384]{1,0:T(8,128)(2,1)S(1)}, u32[]{:S(2)}, u32[]{:S(2)}) collective-permute-start(bf16[192,384]{1,0:T(8,128)(2,1)S(1)} %copy-done.77), channel_id=1, source_target_pairs={{0,3},{1,2},{2,1},{3,0},{4,7},{5,6},{6,5},{7,4},{8,11},{9,10},{10,... | collective-permute-start | bytes 442376 | tf_op jit(solution)/shard_map/ppermute | solution.py:39
  95.6 25.2 %collective-permute-start.23 = (bf16[3,192,384]{2,1,0:T(8,128)(2,1)S(1)}, bf16[3,192,384]{2,1,0:T(8,128)(2,1)S(1)}, u32[]{:S(2)}, u32[]{:S(2)}) collective-permute-start(bf16[3,192,384]{2,1,0:T(8,128)(2,1)S(1)} %pad_maximum_fusion.1.rest_0_), channel_id=1, source_target_pairs={{0,8},{4,12},{8,0},{12,4},{16,24},{20,28},{24,16},{28,20},{1,9},{5... | collective-permute-start | bytes 1327112 | tf_op jit(solution)/shard_map/ppermute | solution.py:39
  96.7 24.1 %collective-permute-start.24 = (bf16[3,192,384]{2,1,0:T(8,128)(2,1)S(1)}, bf16[3,192,384]{2,1,0:T(8,128)(2,1)S(1)}, u32[]{:S(2)}, u32[]{:S(2)}) collective-permute-start(bf16[3,192,384]{2,1,0:T(8,128)(2,1)S(1)} %pad_maximum_fusion.1.rest_0_), channel_id=1, source_target_pairs={{0,16},{4,20},{8,24},{12,28},{16,0},{20,4},{24,8},{28,12},{1,17},{... | collective-permute-start | bytes 1327112 | tf_op jit(solution)/shard_map/ppermute | solution.py:39
  98.1 22.8 %collective-permute-start.25 = (bf16[3,192,384]{2,1,0:T(8,128)(2,1)S(1)}, bf16[3,192,384]{2,1,0:T(8,128)(2,1)S(1)}, u32[]{:S(2)}, u32[]{:S(2)}) collective-permute-start(bf16[3,192,384]{2,1,0:T(8,128)(2,1)S(1)} %pad_maximum_fusion.1.rest_0_), channel_id=1, source_target_pairs={{0,24},{4,28},{8,16},{12,20},{16,8},{20,12},{24,0},{28,4},{1,25},{... | collective-permute-start | bytes 1327112 | tf_op jit(solution)/shard_map/ppermute | solution.py:39
  120.9 14.9 %collective-permute-start.26 = (bf16[3,192,384]{2,1,0:T(8,128)(2,1)S(1)}, bf16[3,192,384]{2,1,0:T(8,128)(2,1)S(1)}, u32[]{:S(2)}, u32[]{:S(2)}) collective-permute-start(bf16[3,192,384]{2,1,0:T(8,128)(2,1)S(1)} %pad_maximum_fusion.1.rest_0_), channel_id=1, source_target_pairs={{0,4},{4,0},{8,12},{12,8},{16,20},{20,16},{24,28},{28,24},{1,5},{5... | collective-permute-start | bytes 1327112 | tf_op jit(solution)/shard_map/ppermute | solution.py:39
  120.9 14.9 %collective-permute-start.27 = (bf16[3,192,384]{2,1,0:T(8,128)(2,1)S(1)}, bf16[3,192,384]{2,1,0:T(8,128)(2,1)S(1)}, u32[]{:S(2)}, u32[]{:S(2)}) collective-permute-start(bf16[3,192,384]{2,1,0:T(8,128)(2,1)S(1)} %collective-permute-done.23.rest_1_), channel_id=1, source_target_pairs={{0,4},{4,0},{8,12},{12,8},{16,20},{20,16},{24,28},{28,24},{1,5},{5... | collective-permute-start | bytes 1327112 | tf_op jit(solution)/shard_map/ppermute | solution.py:39
  121.4 14.4 %collective-permute-start.28 = (bf16[3,192,384]{2,1,0:T(8,128)(2,1)S(1)}, bf16[3,192,384]{2,1,0:T(8,128)(2,1)S(1)}, u32[]{:S(2)}, u32[]{:S(2)}) collective-permute-start(bf16[3,192,384]{2,1,0:T(8,128)(2,1)S(1)} %collective-permute-done.24.rest_2_), channel_id=1, source_target_pairs={{0,4},{4,0},{8,12},{12,8},{16,20},{20,16},{24,28},{28,24},{1,5},{5... | collective-permute-start | bytes 1327112 | tf_op jit(solution)/shard_map/ppermute | solution.py:39
  121.5 14.3 %collective-permute-start.29 = (bf16[3,192,384]{2,1,0:T(8,128)(2,1)S(1)}, bf16[3,192,384]{2,1,0:T(8,128)(2,1)S(1)}, u32[]{:S(2)}, u32[]{:S(2)}) collective-permute-start(bf16[3,192,384]{2,1,0:T(8,128)(2,1)S(1)} %collective-permute-done.25.rest_3_), channel_id=1, source_target_pairs={{0,4},{4,0},{8,12},{12,8},{16,20},{20,16},{24,28},{28,24},{1,5},{5... | collective-permute-start | bytes 1327112 | tf_op jit(solution)/shard_map/ppermute | solution.py:39
  135.8 10.5 %collective-permute-start.30 = (bf16[4,4,192,384]{3,2,1,0:T(8,128)(2,1)S(1)}, bf16[4,4,192,384]{3,2,1,0:T(8,128)(2,1)S(1)}, u32[]{:S(2)}, u32[]{:S(2)}) collective-permute-start(bf16[4,4,192,384]{3,2,1,0:T(8,128)(2,1)S(1)} %get-tuple-element.259), channel_id=1, source_target_pairs={{0,4},{4,0},{8,12},{12,8},{16,20},{20,16},{24,28},{28,24},{1,5},{5... | collective-permute-start | bytes 7077896 | tf_op jit(solution)/shard_map/ppermute | solution.py:39
  146.6 28.4 %collective-permute-start.31 = (bf16[2,4,192,384]{3,2,1,0:T(8,128)(2,1)S(1)}, bf16[2,4,192,384]{3,2,1,0:T(8,128)(2,1)S(1)}, u32[]{:S(2)}, u32[]{:S(2)}) collective-permute-start(bf16[2,4,192,384]{3,2,1,0:T(8,128)(2,1)S(1)} %add_convert_fusion.1), channel_id=1, source_target_pairs={{0,8},{4,12},{8,0},{12,4},{16,24},{20,28},{24,16},{28,20},{1,9},{5... | collective-permute-start | bytes 3538952 | tf_op jit(solution)/shard_map/ppermute | solution.py:39
  175.0 17.4 %collective-permute-start.32 = (bf16[4,4,48,1536]{3,2,1,0:T(8,128)(2,1)S(1)}, bf16[4,4,48,1536]{3,2,1,0:T(8,128)(2,1)}, u32[]{:S(2)}, u32[]{:S(2)}) collective-permute-start(bf16[4,4,48,1536]{3,2,1,0:T(8,128)(2,1)S(1)} %get-tuple-element.275), channel_id=1, source_target_pairs={{0,4},{4,0},{8,12},{12,8},{16,20},{20,16},{24,28},{28,24},{1,5},{5... | collective-permute-start | bytes 7077896 | tf_op jit(solution)/shard_map/ppermute | solution.py:39
  175.5 19.1 %collective-permute-start.33 = (bf16[4,192,384]{2,1,0:T(8,128)(2,1)S(1)}, bf16[4,192,384]{2,1,0:T(8,128)(2,1)S(1)}, u32[]{:S(2)}, u32[]{:S(2)}) collective-permute-start(bf16[4,192,384]{2,1,0:T(8,128)(2,1)S(1)} %fusion.3), channel_id=1, source_target_pairs={{0,16},{4,20},{8,24},{12,28},{16,0},{20,4},{24,8},{28,12},{1,17},{... | collective-permute-start | bytes 1769480 | tf_op jit(solution)/shard_map/ppermute | solution.py:39
  194.6 28.4 %collective-permute-start.34 = (bf16[2,4,48,1536]{3,2,1,0:T(8,128)(2,1)S(1)}, bf16[2,4,48,1536]{3,2,1,0:T(8,128)(2,1)S(1)}, u32[]{:S(2)}, u32[]{:S(2)}) collective-permute-start(bf16[2,4,48,1536]{3,2,1,0:T(8,128)(2,1)S(1)} %add_convert_fusion), channel_id=1, source_target_pairs={{0,16},{4,20},{8,24},{12,28},{16,0},{20,4},{24,8},{28,12},{1,17},{... | collective-permute-start | bytes 3538952 | tf_op jit(solution)/shard_map/ppermute | solution.py:39
  227.5 16.8 %collective-permute-start.38 = (bf16[4,48,1536]{2,1,0:T(8,128)(2,1)S(1)}, bf16[4,48,1536]{2,1,0:T(8,128)(2,1)S(1)}, u32[]{:S(2)}, u32[]{:S(2)}) collective-permute-start(bf16[4,48,1536]{2,1,0:T(8,128)(2,1)S(1)} %fusion.4), channel_id=1, source_target_pairs={{0,8},{4,12},{8,0},{12,4},{16,24},{20,28},{24,16},{28,20},{1,9},{5... | collective-permute-start | bytes 1769480 | tf_op jit(solution)/shard_map/ppermute | solution.py:39
  228.8 12.6 %collective-permute-start.35 = (bf16[192,384]{1,0:T(8,128)(2,1)S(1)}, bf16[192,384]{1,0:T(8,128)(2,1)S(1)}, u32[]{:S(2)}, u32[]{:S(2)}) collective-permute-start(bf16[192,384]{1,0:T(8,128)(2,1)S(1)} %get-tuple-element.392), channel_id=1, source_target_pairs={{0,1},{1,0},{2,3},{3,2},{4,5},{5,4},{6,7},{7,6},{8,9},{9,8},{10,11... | collective-permute-start | bytes 442376 | tf_op jit(solution)/shard_map/ppermute | solution.py:39
  231.0 13.3 %collective-permute-start.36 = (bf16[192,384]{1,0:T(8,128)(2,1)S(1)}, bf16[192,384]{1,0:T(8,128)(2,1)S(1)}, u32[]{:S(2)}, u32[]{:S(2)}) collective-permute-start(bf16[192,384]{1,0:T(8,128)(2,1)S(1)} %get-tuple-element.391), channel_id=1, source_target_pairs={{0,2},{1,3},{2,0},{3,1},{4,6},{5,7},{6,4},{7,5},{8,10},{9,11},{10,... | collective-permute-start | bytes 442376 | tf_op jit(solution)/shard_map/ppermute | solution.py:39
  231.0 13.3 %collective-permute-start.37 = (bf16[192,384]{1,0:T(8,128)(2,1)S(1)}, bf16[192,384]{1,0:T(8,128)(2,1)S(1)}, u32[]{:S(2)}, u32[]{:S(2)}) collective-permute-start(bf16[192,384]{1,0:T(8,128)(2,1)S(1)} %get-tuple-element.390), channel_id=1, source_target_pairs={{0,3},{1,2},{2,1},{3,0},{4,7},{5,6},{6,5},{7,4},{8,11},{9,10},{10,... | collective-permute-start | bytes 442376 | tf_op jit(solution)/shard_map/ppermute | solution.py:39
  245.1 9.7 %collective-permute-start.39 = (bf16[4,4,48,1152]{3,2,1,0:T(8,128)(2,1)}, bf16[4,4,48,1152]{3,2,1,0:T(8,128)(2,1)}, u32[]{:S(2)}, u32[]{:S(2)}) collective-permute-start(bf16[4,4,48,1152]{3,2,1,0:T(8,128)(2,1)} %get-tuple-element.310), channel_id=1, source_target_pairs={{0,4},{4,0},{8,12},{12,8},{16,20},{20,16},{24,28},{28,24},{1,5},{5... | collective-permute-start | bytes 5308424 | tf_op jit(solution)/shard_map/ppermute | solution.py:39
  257.8 30.8 %collective-permute-start.43 = (bf16[2,4,48,1152]{3,2,1,0:T(8,128)(2,1)}, bf16[2,4,48,1152]{3,2,1,0:T(8,128)(2,1)}, u32[]{:S(2)}, u32[]{:S(2)}) collective-permute-start(bf16[2,4,48,1152]{3,2,1,0:T(8,128)(2,1)} %add_convert_fusion.2), channel_id=1, source_target_pairs={{0,16},{4,20},{8,24},{12,28},{16,0},{20,4},{24,8},{28,12},{1,17},{... | collective-permute-start | bytes 2654216 | tf_op jit(solution)/shard_map/ppermute | solution.py:39
  259.9 22.4 %collective-permute-start.40 = (bf16[48,1536]{1,0:T(8,128)(2,1)}, bf16[48,1536]{1,0:T(8,128)(2,1)}, u32[]{:S(2)}, u32[]{:S(2)}) collective-permute-start(bf16[48,1536]{1,0:T(8,128)(2,1)} %get-tuple-element.389), channel_id=1, source_target_pairs={{0,1},{1,0},{2,3},{3,2},{4,5},{5,4},{6,7},{7,6},{8,9},{9,8},{10,11... | collective-permute-start | bytes 442376 | tf_op jit(solution)/shard_map/ppermute | solution.py:39
  262.5 19.9 %collective-permute-start.41 = (bf16[48,1536]{1,0:T(8,128)(2,1)}, bf16[48,1536]{1,0:T(8,128)(2,1)}, u32[]{:S(2)}, u32[]{:S(2)}) collective-permute-start(bf16[48,1536]{1,0:T(8,128)(2,1)} %get-tuple-element.388), channel_id=1, source_target_pairs={{0,2},{1,3},{2,0},{3,1},{4,6},{5,7},{6,4},{7,5},{8,10},{9,11},{10,... | collective-permute-start | bytes 442376 | tf_op jit(solution)/shard_map/ppermute | solution.py:39
  262.5 19.9 %collective-permute-start.42 = (bf16[48,1536]{1,0:T(8,128)(2,1)}, bf16[48,1536]{1,0:T(8,128)(2,1)}, u32[]{:S(2)}, u32[]{:S(2)}) collective-permute-start(bf16[48,1536]{1,0:T(8,128)(2,1)} %get-tuple-element.387), channel_id=1, source_target_pairs={{0,3},{1,2},{2,1},{3,0},{4,7},{5,6},{6,5},{7,4},{8,11},{9,10},{10,... | collective-permute-start | bytes 442376 | tf_op jit(solution)/shard_map/ppermute | solution.py:39
  264.9 60.8 %all-gather.7.cloned.1.call-start = ((), (), s32[]{:S(2)}) async-start(), calls=%async_computation.1 | async-start | bytes 1327104 | tf_op jit(solution)/shard_map/all_gather | solution.py:830
  291.7 12.9 %collective-permute-start.46 = (bf16[4,48,1152]{2,1,0:T(8,128)(2,1)}, bf16[4,48,1152]{2,1,0:T(8,128)(2,1)}, u32[]{:S(2)}, u32[]{:S(2)}) collective-permute-start(bf16[4,48,1152]{2,1,0:T(8,128)(2,1)} %fusion.5), channel_id=1, source_target_pairs={{0,8},{4,12},{8,0},{12,4},{16,24},{20,28},{24,16},{28,20},{1,9},{5... | collective-permute-start | bytes 1327112 | tf_op jit(solution)/shard_map/ppermute | solution.py:39
  294.4 9.4 %collective-permute-start.45 = (bf16[2,4,48,384]{3,2,1,0:T(8,128)(2,1)}, bf16[2,4,48,384]{3,2,1,0:T(8,128)(2,1)}, u32[]{:S(2)}, u32[]{:S(2)}) collective-permute-start(bf16[2,4,48,384]{3,2,1,0:T(8,128)(2,1)} %add_convert_fusion.3), channel_id=1, source_target_pairs={{0,16},{4,20},{8,24},{12,28},{16,0},{20,4},{24,8},{28,12},{1,17},{... | collective-permute-start | bytes 884744 | tf_op jit(solution)/shard_map/ppermute | solution.py:39
  306.5 7.7 %collective-permute-start.49 = (f32[16,768]{1,0:T(8,128)S(1)}, f32[16,768]{1,0:T(8,128)S(1)}, u32[]{:S(2)}, u32[]{:S(2)}) collective-permute-start(f32[16,768]{1,0:T(8,128)S(1)} %add.199), channel_id=1, source_target_pairs={{0,8},{4,12},{8,0},{12,4},{16,24},{20,28},{24,16},{28,20},{1,9},{5... | collective-permute-start | bytes 147464 | tf_op jit(solution)/shard_map/ppermute | solution.py:39
  307.4 7.5 %collective-permute-start.48 = (bf16[4,48,384]{2,1,0:T(8,128)(2,1)}, bf16[4,48,384]{2,1,0:T(8,128)(2,1)S(1)}, u32[]{:S(2)}, u32[]{:S(2)}) collective-permute-start(bf16[4,48,384]{2,1,0:T(8,128)(2,1)} %fusion.19), channel_id=1, source_target_pairs={{0,8},{4,12},{8,0},{12,4},{16,24},{20,28},{24,16},{28,20},{1,9},{5... | collective-permute-start | bytes 442376 | tf_op jit(solution)/shard_map/ppermute | solution.py:39
  310.8 12.5 %collective-permute-start.54 = (bf16[48,1152]{1,0:T(8,128)(2,1)S(1)}, bf16[48,1152]{1,0:T(8,128)(2,1)S(1)}, u32[]{:S(2)}, u32[]{:S(2)}) collective-permute-start(bf16[48,1152]{1,0:T(8,128)(2,1)S(1)} %get-tuple-element.398), channel_id=1, source_target_pairs={{0,2},{1,3},{2,0},{3,1},{4,6},{5,7},{6,4},{7,5},{8,10},{9,11},{10,... | collective-permute-start | bytes 331784 | tf_op jit(solution)/shard_map/ppermute | solution.py:39
  311.7 11.6 %collective-permute-start.55 = (bf16[48,1152]{1,0:T(8,128)(2,1)S(1)}, bf16[48,1152]{1,0:T(8,128)(2,1)S(1)}, u32[]{:S(2)}, u32[]{:S(2)}) collective-permute-start(bf16[48,1152]{1,0:T(8,128)(2,1)S(1)} %get-tuple-element.397), channel_id=1, source_target_pairs={{0,3},{1,2},{2,1},{3,0},{4,7},{5,6},{6,5},{7,4},{8,11},{9,10},{10,... | collective-permute-start | bytes 331784 | tf_op jit(solution)/shard_map/ppermute | solution.py:39
  317.1 8.3 %collective-permute-start.51 = (bf16[48,384]{1,0:T(8,128)(2,1)S(1)}, bf16[48,384]{1,0:T(8,128)(2,1)S(1)}, u32[]{:S(2)}, u32[]{:S(2)}) collective-permute-start(bf16[48,384]{1,0:T(8,128)(2,1)S(1)} %get-tuple-element.401), channel_id=1, source_target_pairs={{0,2},{1,3},{2,0},{3,1},{4,6},{5,7},{6,4},{7,5},{8,10},{9,11},{10,... | collective-permute-start | bytes 110600 | tf_op jit(solution)/shard_map/ppermute | solution.py:39
  325.9 7.7 %collective-permute-start.57 = (bf16[48,1536]{1,0:T(8,128)(2,1)S(1)}, bf16[48,1536]{1,0:T(8,128)(2,1)S(1)}, u32[]{:S(2)}, u32[]{:S(2)}) collective-permute-start(bf16[48,1536]{1,0:T(8,128)(2,1)S(1)} %pad_maximum_fusion.4.rest_0_), channel_id=1, source_target_pairs={{0,8},{4,12},{8,0},{12,4},{16,24},{20,28},{24,16},{28,20},{1,9},{5... | collective-permute-start | bytes 442376 | tf_op jit(solution)/shard_map/ppermute | solution.py:39
  327.4 8.9 %collective-permute-start.58 = (bf16[48,1536]{1,0:T(8,128)(2,1)S(1)}, bf16[48,1536]{1,0:T(8,128)(2,1)S(1)}, u32[]{:S(2)}, u32[]{:S(2)}) collective-permute-start(bf16[48,1536]{1,0:T(8,128)(2,1)S(1)} %pad_maximum_fusion.4.rest_0_), channel_id=1, source_target_pairs={{0,16},{4,20},{8,24},{12,28},{16,0},{20,4},{24,8},{28,12},{1,17},{... | collective-permute-start | bytes 442376 | tf_op jit(solution)/shard_map/ppermute | solution.py:39
  328.0 8.4 %collective-permute-start.59 = (bf16[48,1536]{1,0:T(8,128)(2,1)S(1)}, bf16[48,1536]{1,0:T(8,128)(2,1)S(1)}, u32[]{:S(2)}, u32[]{:S(2)}) collective-permute-start(bf16[48,1536]{1,0:T(8,128)(2,1)S(1)} %pad_maximum_fusion.4.rest_0_), channel_id=1, source_target_pairs={{0,24},{4,28},{8,16},{12,20},{16,8},{20,12},{24,0},{28,4},{1,25},{... | collective-permute-start | bytes 442376 | tf_op jit(solution)/shard_map/ppermute | solution.py:39
  (100 other events, 684.9 us)
Sparse Core Ops, SparseCore 0:
  265.0 23.4 all-gather.4
  302.6 23.1 all-gather.6
